TPU v7x, 512 devices: a whole 4x8x8 slice. The times are simulated.
512 devices in a mesh: seq: 64 (over x, y, core), kv: 8 (over z).
Axes of the slice: x: 4, y: 8, z: 8, core: 2. Of those that a mesh axis runs over, the one named last changes fastest.
Arguments:
- new_hidden: bfloat16 [2, 2048, 12288], P(None, 'seq', 'kv'), may hold values from -6 to 6
- kv_weight: bfloat16 [12288, 2048], P(('kv', 'seq')), may hold values from -0.0546875 to 0.0546875
- kv_cache: bfloat16 [2, 16384, 8, 256], P(None, 'seq', 'kv'), may hold values from -4 to 4
- step_kv: bfloat16 [2, 4, 8, 256], P(None, None, 'kv'), may hold values from -12 to 12
- queries: bfloat16 [2, 4, 96, 128], P(None, None, 'kv'), may hold values from -8 to 8
- hist_len: int32 [2], replicated, may hold values from 4096 to 14336
- new_len: int32 [2], replicated, may hold values from 1 to 2048
Outputs:
- attended: bfloat16 [2, 4, 96, 128], P(None, None, 'kv')
- new_cache: bfloat16 [2, 16384, 8, 256], P(None, 'seq', 'kv')
All inputs are finite; a program needn't handle non-finite values.
Results may differ from a plain program's by a relative error of at most 0.013.
Values may be sent and summed in bfloat16 or wider, within the bound.
No kernel may reach another device: no remote copies, remote signals or barrier semaphores. Data moves between devices by JAX's collectives and lax.ppermute only.
A program may use at most 64 MiB of HBM per device.

v0:
```python
import jax
import jax.numpy as jnp
from jax import lax
from jax.sharding import PartitionSpec as P

rope_base = 1000000.0


def rotate(key_half, positions):
    half_size = key_half.shape[-1] // 2
    frequency = rope_base ** (-2.0 * jnp.arange(half_size, dtype=jnp.float32) / key_half.shape[-1])
    angles = positions.astype(jnp.float32)[..., None] * frequency
    cosine = jnp.cos(angles)
    sine = jnp.sin(angles)
    lower = key_half[..., :half_size]
    upper = key_half[..., half_size:]
    return jnp.concatenate([lower * cosine - upper * sine, upper * cosine + lower * sine], axis=-1)


def pick_rows(rows, index):
    return rows[index]


def on_device(new_hidden, kv_weight, kv_cache, step_kv, queries, hist_len, new_len):
    shards = lax.axis_size("seq")
    groups = lax.axis_size("kv")
    seq_index = lax.axis_index("seq")
    conversations, turn_dev, width_local = new_hidden.shape
    row_total = conversations * turn_dev
    block_rows = kv_weight.shape[0]
    local_heads = kv_cache.shape[2]
    head_size = queries.shape[3]
    feature = 2 * head_size
    step_count = queries.shape[1]
    per_group = queries.shape[2] // local_heads
    tokens = new_hidden.reshape(row_total, width_local)
    gathered = lax.all_gather(tokens, "kv", axis=1, tiled=True)
    own_columns = lax.all_to_all(kv_weight, "kv", split_axis=1, concat_axis=0, tiled=True)
    viewed = gathered.reshape(row_total, groups, shards, block_rows)
    stride = groups * block_rows
    arrived_rows = lax.all_gather(own_columns, "seq", axis=0, tiled=True)
    piece_count = arrived_rows.shape[0] // stride
    columns = viewed
    columns = columns.transpose(0, 2, 1, 3).reshape(row_total, piece_count * stride)
    projected = jnp.dot(columns, arrived_rows, preferred_element_type=jnp.float32)
    projected = projected.reshape(conversations, turn_dev, local_heads, feature)
    offsets = seq_index * turn_dev + jnp.arange(turn_dev, dtype=jnp.int32)
    positions = hist_len[:, None] + offsets[None, :]
    rotated = rotate(projected[..., :head_size], positions[:, :, None])
    turn_kv = jnp.concatenate([rotated, projected[..., head_size:]], axis=-1).astype(jnp.bfloat16)
    slot_count = -(-turn_dev // shards)
    slot_index = jnp.arange(slot_count, dtype=jnp.int32)[None, None, :]
    target = jnp.arange(shards, dtype=jnp.int32)[:, None, None]
    sent_start = (hist_len + seq_index * turn_dev)[None, :, None]
    within = (target - sent_start) % shards + slot_index * shards
    usable = (within < turn_dev) & (seq_index * turn_dev + within < new_len[None, :, None])
    conv_index = jnp.arange(conversations, dtype=jnp.int32)[None, :, None]
    picked = turn_kv[conv_index, jnp.minimum(within, turn_dev - 1)]
    outgoing = jnp.where(usable[..., None, None], picked, jnp.zeros_like(picked))
    outgoing = outgoing.reshape(shards, conversations, slot_count, local_heads * feature)
    incoming = lax.all_to_all(outgoing, "seq", split_axis=0, concat_axis=0, tiled=True)
    source = jnp.arange(shards, dtype=jnp.int32)[:, None, None]
    source_start = hist_len[None, :, None] + source * turn_dev
    arrived_at = (seq_index - source_start) % shards + slot_index * shards
    arrived = (arrived_at < turn_dev) & (source * turn_dev + arrived_at < new_len[None, :, None])
    turn_rows = incoming.transpose(1, 0, 2, 3)
    turn_live = arrived.transpose(1, 0, 2).reshape(conversations, shards * slot_count)
    slot_position = jnp.arange(kv_cache.shape[1], dtype=jnp.int32) * shards + seq_index
    cache_offset = slot_position[None, :] - hist_len[:, None]
    written = (cache_offset >= 0) & (cache_offset < new_len[:, None])
    safe_offset = jnp.clip(cache_offset, 0, shards * turn_dev - 1)
    from_row = safe_offset // turn_dev * slot_count + safe_offset % turn_dev // shards
    fetched = jax.vmap(pick_rows)(turn_rows, from_row)
    new_cache = jnp.where(written[..., None, None], fetched, kv_cache)
    query_heads = queries.reshape(conversations, step_count, local_heads, per_group, head_size)
    score_scale = head_size ** (-0.5)

    def score(key_rows):
        return (
            jnp.einsum(
                "ctgqd,ckgd->ctgqk",
                query_heads,
                key_rows[..., :head_size],
                preferred_element_type=jnp.float32,
            )
            * score_scale
        )

    def blend(weights, key_rows):
        return jnp.einsum(
            "ctgqk,ckgd->ctgqd",
            weights,
            key_rows[..., head_size:],
            preferred_element_type=jnp.float32,
        )

    cache_live = slot_position[None, :] < hist_len[:, None]
    step_number = jnp.arange(step_count, dtype=jnp.int32)
    step_here = ((hist_len + new_len)[:, None] + step_number[None, :]) % shards == seq_index
    causal = step_number[:, None] >= step_number[None, :]
    step_live = step_here[:, None, :] & causal[None, :, :]
    cache_score = jnp.where(cache_live[:, None, None, None, :], score(kv_cache), -jnp.inf)
    turn_score = jnp.where(turn_live[:, None, None, None, :], score(turn_rows), -jnp.inf)
    step_score = jnp.where(step_live[:, :, None, None, :], score(step_kv), -jnp.inf)
    local_max = jnp.maximum(
        jnp.maximum(cache_score.max(-1), turn_score.max(-1)), step_score.max(-1)
    )
    cache_weight = jnp.exp(cache_score - local_max[..., None])
    turn_weight = jnp.exp(turn_score - local_max[..., None])
    step_weight = jnp.exp(step_score - local_max[..., None])
    weight_sum = cache_weight.sum(-1) + turn_weight.sum(-1) + step_weight.sum(-1)
    weighted = (
        blend(cache_weight, kv_cache) + blend(turn_weight, turn_rows) + blend(step_weight, step_kv)
    )
    global_max = lax.pmax(local_max, "seq")
    factor = jnp.exp(local_max - global_max)
    weight_sum, weighted = lax.psum((weight_sum * factor, weighted * factor[..., None]), "seq")
    attended = (weighted / weight_sum[..., None]).astype(jnp.bfloat16)
    attended = attended.reshape(conversations, step_count, local_heads * per_group, head_size)
    return (attended, new_cache)


def solution(mesh):
    return jax.shard_map(
        on_device,
        mesh=mesh,
        in_specs=(
            P(None, "seq", "kv"),
            P(("kv", "seq"), None),
            P(None, "seq", "kv", None),
            P(None, None, "kv", None),
            P(None, None, "kv", None),
            P(),
            P(),
        ),
        out_specs=(P(None, None, "kv", None), P(None, "seq", "kv", None)),
        check_vma=False,
    )
```

profile of v0, /device:TPU:1, one launch (start us, length us, event | category | flops | bytes accessed | tf_op | source)
XLA Modules:
  0.0 547.5 jit_solution(7426880468451653271)
XLA Ops:
  7.2 0.7 all-gather.3.cloned.1.call-update
  8.0 0.9 copy.126
  8.9 18.4 %all_to_all.24 = bf16[24,8,256]{2,0,1:T(8,128)(2,1)} all-to-all(bf16[24,8,256]{2,0,1:T(8,128)(2,1)S(1)} %bitcast.170), channel_id=1, replica_groups=mesh['seq'=64,'kv'=8] {'kv'}, dimensions={1} | all-to-all | bytes 196608 | tf_op jit(solution)/shard_map/all_to_all | solution.py:38
  27.3 0.7 broadcast_add_fusion
  28.3 0.7 compare_and_fusion.1
  29.2 0.8 fusion.44
  30.1 0.7 add_convert_fusion
  30.8 0.7 compare_and_fusion
  31.6 0.9 fusion.55
  32.5 1.2 fusion.56
  33.6 21.6 %all-gather.3.cloned.1.call-done = bf16[64,12288]{1,0:T(8,128)(2,1)} async-done(((bf16[64,1536]{1,0:T(8,128)(2,1)}), bf16[64,12288]{1,0:T(8,128)(2,1)}) %all-gather.3.cloned.1.call-update) | async-done | bytes 1572880 | tf_op jit(solution)/shard_map/all_gather | solution.py:37
  55.2 3.1 copy.85
  58.3 12.7 %copy.106 = bf16[64,64,8,24]{3,2,1,0:T(8,128)(2,1)} copy(bf16[64,64,8,24]{0,3,1,2:T(8,128)(2,1)S(1)} %bitcast.165) | data formatting | bytes 3145728 | tf_op jit(solution)/shard_map/dot_general | solution.py:45
  71.1 13.3 %reshape.885 = bf16[2,32,12288]{2,1,0:T(8,128)(2,1)S(1)} reshape(bf16[64,64,8,24]{3,2,1,0:T(8,128)(2,1)} %copy.106) | data formatting | bytes 3145728 | tf_op jit(solution)/shard_map/dot_general | solution.py:45
  84.4 62.9 %all-gather.5.cloned.1.call-done = bf16[12288,256]{1,0:T(8,128)(2,1)} async-done(((bf16[192,256]{1,0:T(8,128)(2,1)}), bf16[12288,256]{1,0:T(8,128)(2,1)}) %all-gather.5.cloned.1.call-update) | async-done | bytes 6291472 | tf_op jit(solution)/shard_map/all_gather | solution.py:41
  147.3 3.9 fusion.5
  151.5 1.1 gather_fusion
  152.7 0.8 fusion.19
  153.5 5.6 %all-to-all-start.1 = ((bf16[64,2,1,256]{3,1,2,0:T(2,128)(2,1)}), bf16[64,2,1,256]{3,1,2,0:T(2,128)(2,1)S(1)}, u32[]{:S(2)}, u32[]{:S(2)}) async-start(bf16[64,2,1,256]{3,1,2,0:T(2,128)(2,1)} %fusion.19), calls=%async_computation.1 | async-start | bytes 131072 | tf_op jit(solution)/shard_map/all_to_all | solution.py:61
  159.2 9.7 %all-to-all-done.1 = bf16[64,2,1,256]{3,1,2,0:T(2,128)(2,1)S(1)} async-done(((bf16[64,2,1,256]{3,1,2,0:T(2,128)(2,1)}), bf16[64,2,1,256]{3,1,2,0:T(2,128)(2,1)S(1)}, u32[]{:S(2)}, u32[]{:S(2)}) %all-to-all-start.1) | async-done | bytes 65568 | tf_op jit(solution)/shard_map/all_to_all | solution.py:61
  169.7 123.8 %pmax.7 = f32[2,4,1,12]{3,1,0,2:T(4,128)S(1)} all-reduce(f32[2,4,1,12]{3,1,0,2:T(4,128)S(1)} %bitcast.175), channel_id=1, replica_groups=mesh['seq'=64,'kv'=8] {'seq'}, use_global_device_ids=true, to_apply=%region_3.4 | all-reduce | flops 96 | bytes 768 | tf_op jit(solution)/shard_map/pmax | solution.py:115
  294.0 242.0 %all-reduce = (f32[2,4,1,12,128]{4,3,1,0,2:T(8,128)S(1)}, f32[2,4,12]{2,1,0:T(4,128)S(1)}) all-reduce(f32[2,4,1,12,128]{4,3,1,0,2:T(8,128)S(1)} %fusion.12, f32[2,4,12]{2,1,0:T(4,128)S(1)} %get-tuple-element.20), channel_id=1, replica_groups=mesh['seq'=64,'kv'=8] {'seq'}, use_global_device_ids=true, to_apply=%region_4.5 | all-reduce | flops 12384 | bytes 99072 | tf_op jit(solution)/shard_map/psum | solution.py:117
  536.7 3.2 gather_fusion.1
  539.9 0.8 broadcast_select_fusion
  (46 shorter events, 3.1 us)
Async XLA Ops:
  7.2 24.4 %copy-start = (bf16[2,4,12,128]{3,1,2,0:T(4,128)(2,1)S(1)}, bf16[2,4,12,128]{3,1,2,0:T(4,128)(2,1)}, u32[]{:S(2)}) copy-start(bf16[2,4,12,128]{3,1,2,0:T(4,128)(2,1)} %param.11) | copy-start | bytes 73732
  7.2 48.0 %all-gather.3.cloned.1.call-start = ((), (), s32[]{:S(2)}) async-start(), calls=%async_computation.2 | async-start | bytes 1769472 | tf_op jit(solution)/shard_map/all_gather | solution.py:37
  7.9 139.4 %all-gather.5.cloned.1.call-start = ((), (), s32[]{:S(2)}) async-start(), calls=%async_computation.3 | async-start | bytes 6389760 | tf_op jit(solution)/shard_map/all_gather | solution.py:41
  84.4 74.7 %copy-start.2 = (s32[2]{0:T(128)S(1)}, s32[2]{0:T(128)}, u32[]{:S(2)}) copy-start(s32[2]{0:T(128)} %param.12) | copy-start | bytes 28
  84.4 74.7 %copy-start.3 = (s32[2]{0:T(128)S(1)}, s32[2]{0:T(128)}, u32[]{:S(2)}) copy-start(s32[2]{0:T(128)} %param.13) | copy-start | bytes 28
  84.4 84.9 %copy-start.1 = (bf16[2,256,1,256]{3,1,2,0:T(8,128)(2,1)S(1)}, bf16[2,256,1,256]{3,1,2,0:T(8,128)(2,1)}, u32[]{:S(2)}) copy-start(bf16[2,256,1,256]{3,1,2,0:T(8,128)(2,1)} %param.9) | copy-start | bytes 786436
  84.4 209.4 %copy-start.4 = (bf16[2,4,1,256]{3,1,2,0:T(4,128)(2,1)S(1)}, bf16[2,4,1,256]{3,1,2,0:T(4,128)(2,1)}, u32[]{:S(2)}) copy-start(bf16[2,4,1,256]{3,1,2,0:T(4,128)(2,1)} %param.10) | copy-start | bytes 12292
  153.5 15.4 %all-to-all-start.1 = ((bf16[64,2,1,256]{3,1,2,0:T(2,128)(2,1)}), bf16[64,2,1,256]{3,1,2,0:T(2,128)(2,1)S(1)}, u32[]{:S(2)}, u32[]{:S(2)}) async-start(bf16[64,2,1,256]{3,1,2,0:T(2,128)(2,1)} %fusion.19), calls=%async_computation.1 | async-start | bytes 131072 | tf_op jit(solution)/shard_map/all_to_all | solution.py:61
Sparse Core Ops, SparseCore 0:
  10.1 45.0 all-gather.2
  58.5 88.7 all-gather.4
where the time goes:
time: 551 us; the launch traced here: 548 us
  blocking collectives  384 us (70%)
  waiting for transfers between devices  94.9 us (17%)
  local copies, waits for them, and re-layouts  35.4 us (6%)
  between operations  14.3 us (3%)
  matrix products  6.81 us (1%)
  other arithmetic  6.35 us (1%)
  starting transfers between devices  5.65 us (1%)
    psum x1, blocking collectives, on_device(): lax.psum((weight_sum * factor, weighted * factor[..., None]), 'seq')  242 us
    pmax x1, blocking collectives, on_device(): global_max = lax.pmax(local_max, 'seq')  124 us
    all_gather x1, waiting for transfers between devices, on_device(): arrived_rows = lax.all_gather(own_columns, 'seq', axis=0, tiled=True)  62.9 us
    dot_general x2, local copies, waits for them, and re-layouts, on_device(): jnp.dot(columns, arrived_rows, preferred_element_type=jnp.float32)  26 us
    all_gather x1, waiting for transfers between devices, on_device(): gathered = lax.all_gather(tokens, 'kv', axis=1, tiled=True)  21.6 us
    all_to_all x1, blocking collectives, on_device(): lax.all_to_all(kv_weight, 'kv', split_axis=1, concat_axis=0, tiled=True)  18.4 us
  transfers between devices with their start and end apart: 3, of which 3 were waited for; matrix products, arithmetic and copies ran while one was open for 7% of the time, Pallas kernels for 0%

commit v1 on v0

v1 whole, which is shorter than its diff:
```python
import jax
import jax.numpy as jnp
from jax import lax
from jax.experimental import pallas as pl
from jax.experimental.pallas import tpu as pltpu
from jax.sharding import Mesh
from jax.sharding import PartitionSpec as P

rope_base = 1000000.0
NX, NY, NC, NZ = 4, 8, 2, 8
SEQ = NX * NY * NC
GROUP = NX * NC
ALL = ("x", "y", "core", "kv")
CONV, TURN_DEV, WIDTH, HEAD, FEATURE = 2, 32, 1536, 128, 256
ROWS, SLICE = 512, 64
LOCAL = 256
STEPS, QPK = 4, 12
QROWS = STEPS * QPK
ALL_Q = CONV * QROWS
PACK = ALL_Q + 16
PIECE = 32
VMEM_LIMIT = 48 * 1024 * 1024
SMEM = pl.BlockSpec(memory_space=pltpu.SMEM)
VMEM = pl.BlockSpec(memory_space=pltpu.VMEM)


def params(flops, nbytes, limit=VMEM_LIMIT):
    return dict(
        compiler_params=pltpu.CompilerParams(vmem_limit_bytes=limit),
        cost_estimate=pl.CostEstimate(flops=flops, bytes_accessed=nbytes, transcendentals=0),
    )


def exchange(value, names):
    return lax.all_to_all(value, names, split_axis=0, concat_axis=0, tiled=True)


def lane_group(rows):
    return lax.broadcasted_iota(jnp.int32, (rows, HEAD), 1) // PIECE


def split_weight_kernel(source, out, weight):
    pltpu.sync_copy(source, weight)
    depth = weight.shape[0]
    group = lane_group(depth)
    for c in range(GROUP):
        tiles = []
        for half in range(2):
            tile = jnp.zeros((depth, HEAD), jnp.float32)
            for head in range(4 * half, 4 * half + 4):
                start = head * FEATURE + c // 4 * HEAD
                columns = weight[:, start : start + HEAD].astype(jnp.float32)
                tile = jnp.where(group == (c + head) % 4, columns, tile)
            tiles.append(tile)
        columns = jnp.concatenate(tiles, axis=1).astype(jnp.bfloat16)
        for y in range(NY):
            out[c // NC * (NY * NC) + y * NC + c % NC] = columns


def split_weight(weight):
    depth = weight.shape[0]
    return pl.pallas_call(
        split_weight_kernel,
        in_specs=[pl.BlockSpec(memory_space=pltpu.HBM)],
        scratch_shapes=[pltpu.VMEM(weight.shape, weight.dtype)],
        out_shape=jax.ShapeDtypeStruct((SEQ, depth, FEATURE), jnp.bfloat16),
        **params(1 << 20, 1 << 20, 64 * 1024 * 1024 - 128 * 1024),
    )(weight)


def project_kernel(numbers, near, near_other, far, far_other, weight, order, out):
    rows = jnp.concatenate([near[...], near_other[...], far[...], far_other[...]], axis=0)
    partial = jnp.dot(rows, weight[...], preferred_element_type=jnp.float32).astype(jnp.bfloat16)
    ordered = jnp.dot(order[...], partial, preferred_element_type=jnp.float32)
    own = numbers[6]
    group = lane_group(16)
    for owner in range(GROUP):
        for half in range(2):
            turned = []
            for part in range(4):
                start = owner * SLICE + part * 16
                tile = ordered[start : start + 16, half * HEAD : half * HEAD + HEAD]
                turned.append(pltpu.roll(tile, part * PIECE, 1) if part else tile)
            for head in range(4 * half, 4 * half + 4):
                message = turned[0]
                for part in range(1, 4):
                    message = jnp.where(group == ((own + head + part) & 3), turned[part], message)
                out[head * GROUP + owner] = message.astype(jnp.bfloat16)


def project(numbers, blocks, weight, order):
    return pl.pallas_call(
        project_kernel,
        in_specs=[SMEM] + [VMEM] * 6,
        out_specs=VMEM,
        out_shape=jax.ShapeDtypeStruct((NZ * GROUP, 16, HEAD), jnp.bfloat16),
        **params(2 * ROWS * WIDTH * FEATURE, 3 << 20),
    )(numbers, *blocks, weight, order)


def pack(average, row):
    high = row.astype(jnp.bfloat16).astype(jnp.float32)
    middle = (row - high).astype(jnp.bfloat16).astype(jnp.float32)
    low = row - high - middle
    place = lax.broadcasted_iota(jnp.int32, (16, HEAD), 0)
    stats = jnp.where(place == 0, high, jnp.where(place == 1, middle, jnp.where(place == 2, low, 0.0)))
    return jnp.concatenate([average, stats], axis=0).astype(jnp.bfloat16)


def diagonal(first):
    row = lax.broadcasted_iota(jnp.int32, (ALL_Q, HEAD), 0)
    return row + first == lax.broadcasted_iota(jnp.int32, (ALL_Q, HEAD), 1)


def merge(parts, first):
    rows = []
    for part in parts:
        stats = part[first + ALL_Q : first + PACK].astype(jnp.float32)
        rows.append(stats[0:1] + stats[1:2] + stats[2:3])
    lses = jnp.concatenate(rows, axis=0)
    top = jnp.max(lses, axis=0, keepdims=True)
    weights = jnp.exp(lses - top)
    total = jnp.sum(weights, axis=0, keepdims=True)
    weights = weights / total
    on_diagonal = diagonal(first)
    summed = jnp.zeros((ALL_Q, HEAD), jnp.float32)
    for index, part in enumerate(parts):
        spread = jnp.where(on_diagonal, weights[index : index + 1], 0.0).astype(jnp.bfloat16)
        summed += jnp.dot(spread, part, preferred_element_type=jnp.float32)
    return summed, top + jnp.log(total)


def history_kernel(numbers, cache, step_kv, queries, summed, tops, totals):
    t = numbers[4]
    for conv in range(CONV):
        history, length = numbers[conv], numbers[2 + conv]
        query = queries[conv]
        keys = [cache[conv, :, :HEAD], step_kv[conv, :, :HEAD]]
        values = [cache[conv, :, HEAD:], step_kv[conv, :, HEAD:]]
        position = lax.broadcasted_iota(jnp.int32, (QROWS, LOCAL), 1) * SEQ + t
        step = lax.broadcasted_iota(jnp.int32, (QROWS, 16), 1)
        asked = lax.broadcasted_iota(jnp.int32, (QROWS, 16), 0) & 3
        visible = [
            position < history,
            (step <= asked) & (((history + length + step) & (SEQ - 1)) == t),
        ]
        scores = [score(query, rows) for rows in keys]
        top = jnp.maximum(*[largest(one, seen) for one, seen in zip(scores, visible)])
        weights = [jnp.where(seen, jnp.exp(one - top), 0.0) for one, seen in zip(scores, visible)]
        total = sum(jnp.sum(weight, axis=1, keepdims=True) for weight in weights)
        rows = slice(conv * QROWS, conv * QROWS + QROWS)
        summed[rows] = sum(blend(weight, value) for weight, value in zip(weights, values))
        tops[rows] = jnp.broadcast_to(top, (QROWS, HEAD))
        totals[rows] = jnp.broadcast_to(total, (QROWS, HEAD))


def score(query, rows):
    contract = (((1,), (1,)), ((), ()))
    return lax.dot_general(query, rows, contract, preferred_element_type=jnp.float32) * HEAD ** (-0.5)


def largest(scores, seen):
    return jnp.max(jnp.where(seen, scores, -3e38), axis=1, keepdims=True)


def blend(weights, rows):
    return jnp.dot(weights.astype(jnp.bfloat16), rows, preferred_element_type=jnp.float32)


def attend_history(numbers, cache, step_kv, queries):
    return pl.pallas_call(
        history_kernel,
        in_specs=[SMEM] + [VMEM] * 3,
        out_specs=[VMEM] * 3,
        out_shape=[jax.ShapeDtypeStruct((ALL_Q, HEAD), jnp.float32)] * 3,
        **params(2 * ALL_Q * LOCAL * FEATURE, 1 << 20),
    )(numbers, cache, step_kv, queries)


def attend_kernel(numbers, arrived, cosine, sine, queries, summed, tops, totals, out):
    y, own, z = numbers[5], numbers[6], numbers[7]
    group = lane_group(16)
    sums = []
    for c in range(GROUP):
        total = arrived[c].astype(jnp.float32)
        for plane in range(1, NZ):
            total += arrived[plane * GROUP + c].astype(jnp.float32)
        sums.append(total)
    halves = []
    for tile in range(2):
        pieces = []
        for part in range(4):
            piece = sums[4 * tile]
            for c in range(4 * tile + 1, 4 * tile + 4):
                piece = jnp.where(group == ((c + z + part) & 3), sums[c], piece)
            pieces.append(pltpu.roll(piece, HEAD - part * PIECE, 1) if part else piece)
        halves.append(jnp.concatenate(pieces, axis=0))
    key, value = halves
    key = key * cosine[...] + pltpu.roll(key, HEAD // 2, 1) * sine[...]
    for row in range(NY):
        both = jnp.concatenate([key[row * 8 : row * 8 + 8], value[row * 8 : row * 8 + 8]], axis=0)
        out[row, :16] = both.astype(jnp.bfloat16)
    key, value = key.astype(jnp.bfloat16), value.astype(jnp.bfloat16)

    asker = lax.broadcasted_iota(jnp.int32, (ALL_Q, SLICE), 0) >= QROWS
    row = lax.broadcasted_iota(jnp.int32, (ALL_Q, SLICE), 1)
    history = jnp.where(asker, numbers[1], numbers[0])
    length = jnp.where(asker, numbers[3], numbers[2])
    owner = own // NC * (NY * NC) + (row >> 3) * NC + own % NC
    offset = ((row & 3) * NY + y) * SEQ + ((owner - history) & (SEQ - 1))
    visible = (((row >> 2) & 1) == asker.astype(jnp.int32)) & (offset < length)
    scores = score(jnp.concatenate([queries[0], queries[1]], axis=0), key)
    old_top = tops[:, :1]
    top = jnp.maximum(old_top, largest(scores, visible))
    weights = jnp.where(visible, jnp.exp(scores - top), 0.0)
    kept = jnp.exp(old_top - top)
    total = totals[:, :1] * kept + jnp.sum(weights, axis=1, keepdims=True)
    average = (summed[...] * kept + blend(weights, value)) / total
    lse = jnp.sum(jnp.where(diagonal(16), top + jnp.log(total), 0.0), axis=0, keepdims=True)
    packed = pack(average, lse)
    for row in range(NY):
        out[row, 16:] = packed


def attend(numbers, arrived, cosine, sine, queries, history):
    return pl.pallas_call(
        attend_kernel,
        in_specs=[SMEM] + [VMEM] * 7,
        out_specs=VMEM,
        out_shape=jax.ShapeDtypeStruct((NY, 16 + PACK, HEAD), jnp.bfloat16),
        **params(4 * ALL_Q * SLICE * HEAD, 1 << 20),
    )(numbers, arrived, cosine, sine, queries, *history)


def merge_kernel(arrived, out):
    average, lse = merge([arrived[row] for row in range(NY)], 16)
    lse = pltpu.roll(jnp.broadcast_to(lse, (8, HEAD)), HEAD - 16, 1)[0:1]
    packed = pack(average, lse)
    for device in range(GROUP):
        out[device] = packed


def finish_kernel(arrived, out):
    rest = jnp.zeros((HEAD - PACK, HEAD), jnp.bfloat16)
    parts = [jnp.concatenate([arrived[device], rest], axis=0) for device in range(GROUP)]
    out[...] = merge(parts, 0)[0].astype(jnp.bfloat16)


def combine(kernel, shape, arrived):
    return pl.pallas_call(
        kernel,
        out_shape=jax.ShapeDtypeStruct(shape, jnp.bfloat16),
        **params(PACK * HEAD * 32, 1 << 19),
    )(arrived)


def write_kernel(numbers, arrived, cache, new_cache):
    t = numbers[4]
    rows = jnp.concatenate([arrived[row, :16].astype(jnp.float32) for row in range(NY)], axis=0)
    rows = rows.astype(jnp.bfloat16)
    for conv in range(CONV):
        history, length = numbers[conv], numbers[2 + conv]
        within = (t - history) & (SEQ - 1)
        first = lax.div(history + within, SEQ)
        row = lax.broadcasted_iota(jnp.int32, (LOCAL, HEAD), 0) - first
        column = lax.broadcasted_iota(jnp.int32, (LOCAL, HEAD), 1)
        slot = (column & 3) * NY + (column >> 4)
        live = (((column >> 2) & 1) == conv) & (slot * SEQ + within < length) & (row == slot)
        written = (row >= 0) & (row < 32) & (row * SEQ + within < length)
        for half in range(2):
            place = jnp.where(live & (((column >> 3) & 1) == half), 1.0, 0.0).astype(jnp.bfloat16)
            placed = jnp.dot(place, rows, preferred_element_type=jnp.float32)
            lanes = slice(half * HEAD, half * HEAD + HEAD)
            kept = jnp.where(written, placed, cache[conv, :, lanes].astype(jnp.float32))
            new_cache[conv, :, lanes] = kept.astype(jnp.bfloat16)


def write(numbers, arrived, cache):
    return pl.pallas_call(
        write_kernel,
        in_specs=[SMEM] + [VMEM] * 2,
        out_specs=VMEM,
        out_shape=jax.ShapeDtypeStruct((CONV, LOCAL, FEATURE), jnp.bfloat16),
        **params(4 * CONV * LOCAL * HEAD * FEATURE, 1 << 20),
    )(numbers, arrived, cache)


def on_device(new_hidden, kv_weight, kv_cache, step_kv, queries, hist_len, new_len):
    x, y, core, z = (lax.axis_index(name) for name in ALL)
    t = (x * NY + y) * NC + core
    own = x * NC + core

    weight = exchange(split_weight(kv_weight), ("x", "y", "core")).reshape(WIDTH, FEATURE)

    swap = [(0, 1), (1, 0)]
    there, back = [], []
    for chip in range(NX):
        for side, step in ((0, NX - 1), (1, 1)):
            there.append((chip * NC + side, (chip + step) % NX * NC + side))
            back.append((chip * NC + side, (chip - step) % NX * NC + side))
    hidden = new_hidden.reshape(CONV * TURN_DEV, WIDTH)
    after = lax.ppermute(hidden, ("x", "core"), there)
    hidden, after = lax.optimization_barrier((hidden, after))
    before = lax.ppermute(hidden, ("x", "core"), back)
    near = jnp.concatenate([hidden, after], axis=0)
    far = jnp.concatenate([before, lax.ppermute(after, ("x", "core"), there)], axis=0)
    near_other = lax.ppermute(near, "core", swap)
    near_other, hist_len, new_len = lax.optimization_barrier((near_other, hist_len, new_len))
    blocks = [near, near_other, far, lax.ppermute(far, "core", swap)]
    numbers = jnp.concatenate([hist_len, new_len, jnp.stack([t, y, own, z])]).astype(jnp.int32)

    def axis(size, place):
        shape = [1, 1, 1, 1]
        shape[place] = size
        return jnp.arange(size, dtype=jnp.int32).reshape(shape)

    history = hist_len.reshape(1, 1, CONV, 1)
    source_x = axis(NX, 3)

    def within_of(device):
        owner = device // NC * (NY * NC) + axis(NY, 1) * NC + device % NC
        return (owner - history) % SEQ

    within = within_of(axis(GROUP, 0))
    crossed = within // TURN_DEV ^ core
    place = jnp.where(within // TURN_DEV == 0, source_x - x, x - source_x) % NX
    place = jnp.where(place < 2, place, 7 - place) + crossed * 2
    column = place * SLICE + axis(CONV, 2) * TURN_DEV + within % TURN_DEV
    order = (column.reshape(ROWS, 1) == jnp.arange(ROWS, dtype=jnp.int32)[None, :]).astype(jnp.bfloat16)

    position = history + (source_x * NY + y) * SEQ + within_of(own)
    frequency = rope_base ** (-2.0 * jnp.arange(HEAD // 2, dtype=jnp.float32) / HEAD)
    angles = position.reshape(SLICE, 1).astype(jnp.float32) * frequency[None, :]
    cosine, sine = jnp.cos(angles), jnp.sin(angles)
    cosine = jnp.concatenate([cosine, cosine], axis=1)
    sine = jnp.concatenate([-sine, sine], axis=1)

    asked = queries.transpose(0, 2, 1, 3).reshape(CONV, QROWS, HEAD)
    steps = jnp.pad(step_kv.reshape(CONV, STEPS, FEATURE), ((0, 0), (0, 16 - STEPS), (0, 0)))
    cache = kv_cache.reshape(CONV, LOCAL, FEATURE)

    partial = exchange(project(numbers, blocks, weight, order), ("kv", "x", "core"))
    history_part = attend_history(numbers, cache, steps, asked)
    rows = exchange(attend(numbers, partial, cosine, sine, asked, history_part), ("y",))
    packed = exchange(combine(merge_kernel, (GROUP, PACK, HEAD), rows), ("x", "core"))
    new_cache = write(numbers, rows, cache)
    attended = combine(finish_kernel, (ALL_Q, HEAD), packed)
    attended = attended.reshape(CONV, QPK, STEPS, HEAD).transpose(0, 2, 1, 3)
    return attended, new_cache.reshape(kv_cache.shape)


def solution(mesh):
    split = Mesh(mesh.devices.reshape(NX, NY, NC, NZ), ALL)
    seq = ALL[:3]
    return jax.shard_map(
        on_device,
        mesh=split,
        in_specs=(
            P(None, seq, "kv"),
            P(("kv",) + seq, None),
            P(None, seq, "kv", None),
            P(None, None, "kv", None),
            P(None, None, "kv", None),
            P(),
            P(),
        ),
        out_specs=(P(None, None, "kv", None), P(None, seq, "kv", None)),
        check_vma=False,
    )
```

time: 551 us -> 99.2 us (0.18)
  blocking collectives: 384 us -> 16.3 us
  waiting for transfers between devices: 94.9 us -> 23 us
  starting transfers between devices: 5.65 us -> 43.3 us
  local copies, waits for them, and re-layouts: 35.4 us -> 3.92 us
  between operations: 14.3 us -> 0.98 us
  Pallas kernels: 0 us -> 9.77 us
  matrix products: 6.81 us -> 0 us
    psum x1 -> x0, blocking collectives: 242 us -> none  [on_device(): lax.psum((weight_sum * factor, weighted * factor[..., None]), 'seq')]
    pmax x1 -> x0, blocking collectives: 124 us -> none  [on_device(): global_max = lax.pmax(local_max, 'seq')]
    all_gather x2 -> x0, waiting for transfers between devices: 84.5 us -> none  [the longest x1 62.9 us: on_device(): arrived_rows = lax.all_gather(own_columns, 'seq', axis=0, tiled=True)]
    dot_general x2 -> x0, local copies, waits for them, and re-layouts: 26 us -> none  [on_device(): jnp.dot(columns, arrived_rows, preferred_element_type=jnp.float32)]
    all_to_all x1 -> x3, starting transfers between devices: 5.58 us -> 28.1 us  [exchange(): return lax.all_to_all(value, names, split_axis=0, concat_axis=0, tiled=True)]
    ppermute x0 -> x5, starting transfers between devices: none -> 15.3 us  [the longest x1 4.71 us: on_device(): before = lax.ppermute(hidden, ('x', 'core'), back)]
    pallas_call x0 -> x7, Pallas kernels: none -> 9.77 us  [the longest x1 2.33 us: project(): pl.pallas_call(project_kernel, in_specs=[SMEM] + [VMEM] * 6, out_specs=VM...]
    all_to_all x1 -> x3, waiting for transfers between devices: 9.68 us -> 18.1 us  [exchange(): return lax.all_to_all(value, names, split_axis=0, concat_axis=0, tiled=True)]
  transfers between devices with their start and end apart: 3 -> 8, of which waited for: 3 -> 4; matrix products, arithmetic and copies ran while one was open for 7% -> 3% of each run, Pallas kernels for 0% -> 5%
where the time goes in v1:
time: 99.2 us; the launch traced here: 98.5 us
  starting transfers between devices  43.3 us (44%)
  waiting for transfers between devices  23 us (23%)
  blocking collectives  16.3 us (16%)
  Pallas kernels  9.77 us (10%)
  local copies, waits for them, and re-layouts  3.92 us (4%)
  other arithmetic  1.14 us (1%)
    all_to_all x3, starting transfers between devices, exchange(): return lax.all_to_all(value, names, split_axis=0, concat_axis=0, tiled=True)  28.1 us
    all_to_all x3, waiting for transfers between devices, exchange(): return lax.all_to_all(value, names, split_axis=0, concat_axis=0, tiled=True)  18.1 us
    all_to_all x1, blocking collectives, exchange(): return lax.all_to_all(value, names, split_axis=0, concat_axis=0, tiled=True)  16.3 us
    ppermute x1, waiting for transfers between devices, on_device(): lax.ppermute(after, ('x', 'core'), there)  4.9 us
    ppermute x1, starting transfers between devices, on_device(): before = lax.ppermute(hidden, ('x', 'core'), back)  4.71 us
    ppermute x1, starting transfers between devices, on_device(): after = lax.ppermute(hidden, ('x', 'core'), there)  3.95 us
    ppermute x1, starting transfers between devices, on_device(): near_other = lax.ppermute(near, 'core', swap)  2.78 us
    pallas_call x1, Pallas kernels, project(): pl.pallas_call(project_kernel, in_specs=[SMEM] + [VMEM] * 6, out_specs=VM...  2.33 us
  transfers between devices with their start and end apart: 8, of which 4 were waited for; matrix products, arithmetic and copies ran while one was open for 3% of the time, Pallas kernels for 5%

profile of v1, /device:TPU:1, one launch (start us, length us, event | category | flops | bytes accessed | tf_op | source)
XLA Modules:
  0.0 98.5 jit_solution(10736374483834165003)
XLA Ops:
  0.6 4.0 %collective-permute-start = (bf16[64,1536]{1,0:T(8,128)(2,1)}, bf16[64,1536]{1,0:T(8,128)(2,1)}, u32[]{:S(2)}, u32[]{:S(2)}) collective-permute-start(bf16[64,1536]{1,0:T(8,128)(2,1)} %bitcast.23), channel_id=1, source_target_pairs={{0,384},{8,136},{128,0},{136,264},{256,128},{264,392},{384,256},{3... | collective-permute-start | bytes 589832 | tf_op jit(solution)/shard_map/ppermute | solution.py:302
  4.6 1.8 %shard_map.86 = bf16[64,24,256]{2,1,0:T(8,128)(2,1)} custom-call(bf16[24,2048]{1,0:T(8,128)(2,1)} %source.1), custom_call_target="tpu_custom_call" | custom-call | flops 1048576 | bytes 1048576 | tf_op jit(solution)/shard_map/pallas_call | solution.py:62
  6.4 10.1 %all-to-all-start = ((bf16[64,24,256]{2,1,0:T(8,128)(2,1)}), bf16[64,24,256]{2,1,0:T(8,128)(2,1)S(1)}, u32[]{:S(2)}, u32[]{:S(2)}) async-start(bf16[64,24,256]{2,1,0:T(8,128)(2,1)} %shard_map.86), calls=%async_computation | async-start | bytes 1572864 | tf_op jit(solution)/shard_map/all_to_all | solution.py:35
  17.0 0.7 copy-done.4
  17.7 4.7 %collective-permute-start.2 = (bf16[64,1536]{1,0:T(8,128)(2,1)S(1)}, bf16[64,1536]{1,0:T(8,128)(2,1)S(1)}, u32[]{:S(2)}, u32[]{:S(2)}) collective-permute-start(bf16[64,1536]{1,0:T(8,128)(2,1)S(1)} %bitcast.25), channel_id=1, source_target_pairs={{0,128},{8,392},{128,256},{136,8},{256,384},{264,136},{384,0},{392... | collective-permute-start | bytes 589832 | tf_op jit(solution)/shard_map/ppermute | solution.py:304
  22.5 1.9 %collective-permute-start.3 = (bf16[64,1536]{1,0:T(8,128)(2,1)}, bf16[64,1536]{1,0:T(8,128)(2,1)S(1)}, u32[]{:S(2)}, u32[]{:S(2)}) collective-permute-start(bf16[64,1536]{1,0:T(8,128)(2,1)} %collective-permute-done), channel_id=1, source_target_pairs={{0,384},{8,136},{128,0},{136,264},{256,128},{264,392},{384,256},{3... | collective-permute-start | bytes 589832 | tf_op jit(solution)/shard_map/ppermute | solution.py:306
  24.4 1.0 constant_dynamic-update-slice_fusion.near
  25.3 2.8 %collective-permute-start.1 = (bf16[128,1536]{1,0:T(8,128)(2,1)S(1)}, bf16[128,1536]{1,0:T(8,128)(2,1)S(1)}, u32[]{:S(2)}, u32[]{:S(2)}) collective-permute-start(bf16[128,1536]{1,0:T(8,128)(2,1)S(1)} %constant_dynamic-update-slice_fusion.near), channel_id=1, source_target_pairs={{0,8},{8,0},{1,9},{9,1},{2,10},{10,2},{3,11},{11,3},{4,12},{12,4},... | collective-permute-start | bytes 1179656 | tf_op jit(solution)/shard_map/ppermute | solution.py:307
  28.2 4.9 %collective-permute-done.3 = bf16[64,1536]{1,0:T(8,128)(2,1)S(1)} collective-permute-done((bf16[64,1536]{1,0:T(8,128)(2,1)}, bf16[64,1536]{1,0:T(8,128)(2,1)S(1)}, u32[]{:S(2)}, u32[]{:S(2)}) %collective-permute-start.3) | collective-permute-done | bytes 196640 | tf_op jit(solution)/shard_map/ppermute | solution.py:306
  33.1 1.9 %collective-permute-start.4 = (bf16[128,1536]{1,0:T(8,128)(2,1)S(1)}, bf16[128,1536]{1,0:T(8,128)(2,1)S(1)}, u32[]{:S(2)}, u32[]{:S(2)}) collective-permute-start(bf16[128,1536]{1,0:T(8,128)(2,1)S(1)} %constant_dynamic-update-slice_fusion.2.far), channel_id=1, source_target_pairs={{0,8},{8,0},{1,9},{9,1},{2,10},{10,2},{3,11},{11,3},{4,12},{12,4},... | collective-permute-start | bytes 1179656 | tf_op jit(solution)/shard_map/ppermute | solution.py:309
  36.1 0.7 copy-done.5
  37.2 2.4 %all-to-all-done = bf16[64,24,256]{2,1,0:T(8,128)(2,1)S(1)} async-done(((bf16[64,24,256]{2,1,0:T(8,128)(2,1)}), bf16[64,24,256]{2,1,0:T(8,128)(2,1)S(1)}, u32[]{:S(2)}, u32[]{:S(2)}) %all-to-all-start) | async-done | bytes 786464 | tf_op jit(solution)/shard_map/all_to_all | solution.py:35
  39.6 2.3 %shard_map.87 = bf16[64,16,128]{2,1,0:T(8,128)(2,1)} custom-call(s32[8]{0:T(128)S(1)} %concatenate.16.numbers, bf16[128,1536]{1,0:T(8,128)(2,1)S(1)} %constant_dynamic-update-slice_fusion.near, bf16[128,1536]{1,0:T(8,128)(2,1)S(1)} %collective-permute-done.1.near_other, bf16[128,1536]{1,0:T(8,128)(2,1)S(1)} %constant_dynamic-update-slice_fusion.2.far, ...), custom_call_target="tpu_custom_call" | custom-call | flops 402653184 | bytes 3145728 | tf_op jit(solution)/shard_map/pallas_call | solution.py:92
  41.9 13.6 %all-to-all-start.1 = ((bf16[64,16,128]{2,1,0:T(8,128)(2,1)}), bf16[64,16,128]{2,1,0:T(8,128)(2,1)S(1)}, u32[]{:S(2)}, u32[]{:S(2)}) async-start(bf16[64,16,128]{2,1,0:T(8,128)(2,1)} %shard_map.87), calls=%async_computation.1 | async-start | bytes 524288 | tf_op jit(solution)/shard_map/all_to_all | solution.py:35
  55.7 0.5 copy-done.1
  56.3 1.1 %shard_map.88 = (f32[96,128]{1,0:T(8,128)S(1)}, f32[96,128]{1,0:T(8,128)S(1)}, f32[96,128]{1,0:T(8,128)S(1)}) custom-call(s32[8]{0:T(128)S(1)} %concatenate.16.numbers, bf16[2,256,256]{2,1,0:T(8,128)(2,1)S(1)} %bitcast.18, bf16[2,16,256]{2,1,0:T(8,128)(2,1)S(1)} %pad.4.step_kv, bf16[2,48,128]{2,1,0:T(8,128)(2,1)S(1)} %bitcast.20), custom_call_target="tpu_custom_call" | custom-call | flops 12582912 | bytes 1048576 | tf_op jit(solution)/shard_map/pallas_call | solution.py:171
  57.7 11.0 %all-to-all-done.1.arrived = bf16[64,16,128]{2,1,0:T(8,128)(2,1)S(1)} async-done(((bf16[64,16,128]{2,1,0:T(8,128)(2,1)}), bf16[64,16,128]{2,1,0:T(8,128)(2,1)S(1)}, u32[]{:S(2)}, u32[]{:S(2)}) %all-to-all-start.1) | async-done | bytes 262176 | tf_op jit(solution)/shard_map/all_to_all | solution.py:35
  68.7 1.2 %shard_map.89 = bf16[8,128,128]{2,1,0:T(8,128)(2,1)S(1)} custom-call(s32[8]{0:T(128)S(1)} %concatenate.16.numbers, bf16[64,16,128]{2,1,0:T(8,128)(2,1)S(1)} %all-to-all-done.1.arrived, f32[64,128]{1,0:T(8,128)S(1)} %get-tuple-element.31.cosine, f32[64,128]{1,0:T(8,128)S(1)} %get-tuple-element.32.sine, bf16[2,48,128]{2,1,0:T(8,128)(2,1)S(1)} %bitcast.21, ...), custom_call_target="tpu_custom_call" | custom-call | flops 3145728 | bytes 1048576 | tf_op jit(solution)/shard_map/pallas_call | solution.py:226
  69.9 16.3 %all_to_all.20.arrived = bf16[8,128,128]{2,1,0:T(8,128)(2,1)S(1)} all-to-all(bf16[8,128,128]{2,1,0:T(8,128)(2,1)S(1)} %shard_map.89), channel_id=1, replica_groups=mesh['x'=4,'y'=8,'core'=2,'kv'=8] {'y'}, dimensions={0} | all-to-all | bytes 524288 | tf_op jit(solution)/shard_map/all_to_all | solution.py:35
  86.3 0.9 shard_map.90
  87.2 4.3 %all-to-all-start.3 = ((bf16[8,112,128]{2,1,0:T(8,128)(2,1)}), bf16[8,112,128]{2,1,0:T(8,128)(2,1)S(1)}, u32[]{:S(2)}, u32[]{:S(2)}) async-start(bf16[8,112,128]{2,1,0:T(8,128)(2,1)} %shard_map.90), calls=%async_computation.3 | async-start | bytes 458752 | tf_op jit(solution)/shard_map/all_to_all | solution.py:35
  91.5 1.5 %shard_map.92 = bf16[2,256,256]{2,1,0:T(8,128)(2,1)} custom-call(s32[8]{0:T(128)S(1)} %concatenate.16.numbers, bf16[8,128,128]{2,1,0:T(8,128)(2,1)S(1)} %all_to_all.20.arrived, bf16[2,256,256]{2,1,0:T(8,128)(2,1)S(1)} %bitcast.19), custom_call_target="tpu_custom_call" | custom-call | flops 67108864 | bytes 1048576 | tf_op jit(solution)/shard_map/pallas_call | solution.py:279
  92.9 4.7 %all-to-all-done.3.arrived = bf16[8,112,128]{2,1,0:T(8,128)(2,1)S(1)} async-done(((bf16[8,112,128]{2,1,0:T(8,128)(2,1)}), bf16[8,112,128]{2,1,0:T(8,128)(2,1)S(1)}, u32[]{:S(2)}, u32[]{:S(2)}) %all-to-all-start.3) | async-done | bytes 229408 | tf_op jit(solution)/shard_map/all_to_all | solution.py:35
  97.7 0.8 shard_map.91
  (44 shorter events, 2.3 us)
Async XLA Ops:
  0.6 17.1 %collective-permute-start = (bf16[64,1536]{1,0:T(8,128)(2,1)}, bf16[64,1536]{1,0:T(8,128)(2,1)}, u32[]{:S(2)}, u32[]{:S(2)}) collective-permute-start(bf16[64,1536]{1,0:T(8,128)(2,1)} %bitcast.23), channel_id=1, source_target_pairs={{0,384},{8,136},{128,0},{136,264},{256,128},{264,392},{384,256},{3... | collective-permute-start | bytes 589832 | tf_op jit(solution)/shard_map/ppermute | solution.py:302
  6.4 33.1 %all-to-all-start = ((bf16[64,24,256]{2,1,0:T(8,128)(2,1)}), bf16[64,24,256]{2,1,0:T(8,128)(2,1)S(1)}, u32[]{:S(2)}, u32[]{:S(2)}) async-start(bf16[64,24,256]{2,1,0:T(8,128)(2,1)} %shard_map.86), calls=%async_computation | async-start | bytes 1572864 | tf_op jit(solution)/shard_map/all_to_all | solution.py:35
  16.6 1.1 %copy-start.2 = (bf16[2,32,1536]{2,1,0:T(8,128)(2,1)S(1)}, bf16[2,32,1536]{2,1,0:T(8,128)(2,1)}, u32[]{:S(2)}) copy-start(bf16[2,32,1536]{2,1,0:T(8,128)(2,1)} %param.7) | copy-start | bytes 589828
  16.9 0.7 copy-start.4
  17.7 10.4 %collective-permute-start.2 = (bf16[64,1536]{1,0:T(8,128)(2,1)S(1)}, bf16[64,1536]{1,0:T(8,128)(2,1)S(1)}, u32[]{:S(2)}, u32[]{:S(2)}) collective-permute-start(bf16[64,1536]{1,0:T(8,128)(2,1)S(1)} %bitcast.25), channel_id=1, source_target_pairs={{0,128},{8,392},{128,256},{136,8},{256,384},{264,136},{384,0},{392... | collective-permute-start | bytes 589832 | tf_op jit(solution)/shard_map/ppermute | solution.py:304
  22.5 10.6 %collective-permute-start.3 = (bf16[64,1536]{1,0:T(8,128)(2,1)}, bf16[64,1536]{1,0:T(8,128)(2,1)S(1)}, u32[]{:S(2)}, u32[]{:S(2)}) collective-permute-start(bf16[64,1536]{1,0:T(8,128)(2,1)} %collective-permute-done), channel_id=1, source_target_pairs={{0,384},{8,136},{128,0},{136,264},{256,128},{264,392},{384,256},{3... | collective-permute-start | bytes 589832 | tf_op jit(solution)/shard_map/ppermute | solution.py:306
  25.3 9.7 %collective-permute-start.1 = (bf16[128,1536]{1,0:T(8,128)(2,1)S(1)}, bf16[128,1536]{1,0:T(8,128)(2,1)S(1)}, u32[]{:S(2)}, u32[]{:S(2)}) collective-permute-start(bf16[128,1536]{1,0:T(8,128)(2,1)S(1)} %constant_dynamic-update-slice_fusion.near), channel_id=1, source_target_pairs={{0,8},{8,0},{1,9},{9,1},{2,10},{10,2},{3,11},{11,3},{4,12},{12,4},... | collective-permute-start | bytes 1179656 | tf_op jit(solution)/shard_map/ppermute | solution.py:307
  28.2 6.9 %copy-start.3 = (s32[2]{0:T(128)S(1)}, s32[2]{0:T(128)}, u32[]{:S(2)}) copy-start(s32[2]{0:T(128)} %param.12) | copy-start | bytes 28
  33.1 4.1 %collective-permute-start.4 = (bf16[128,1536]{1,0:T(8,128)(2,1)S(1)}, bf16[128,1536]{1,0:T(8,128)(2,1)S(1)}, u32[]{:S(2)}, u32[]{:S(2)}) collective-permute-start(bf16[128,1536]{1,0:T(8,128)(2,1)S(1)} %constant_dynamic-update-slice_fusion.2.far), channel_id=1, source_target_pairs={{0,8},{8,0},{1,9},{9,1},{2,10},{10,2},{3,11},{11,3},{4,12},{12,4},... | collective-permute-start | bytes 1179656 | tf_op jit(solution)/shard_map/ppermute | solution.py:309
  36.1 0.7 copy-start.5
  41.9 13.8 %copy-start = (bf16[2,256,1,256]{3,1,2,0:T(8,128)(2,1)S(1)}, bf16[2,256,1,256]{3,1,2,0:T(8,128)(2,1)}, u32[]{:S(2)}) copy-start(bf16[2,256,1,256]{3,1,2,0:T(8,128)(2,1)} %param.9) | copy-start | bytes 786436
  41.9 26.8 %all-to-all-start.1 = ((bf16[64,16,128]{2,1,0:T(8,128)(2,1)}), bf16[64,16,128]{2,1,0:T(8,128)(2,1)S(1)}, u32[]{:S(2)}, u32[]{:S(2)}) async-start(bf16[64,16,128]{2,1,0:T(8,128)(2,1)} %shard_map.87), calls=%async_computation.1 | async-start | bytes 524288 | tf_op jit(solution)/shard_map/all_to_all | solution.py:35
  55.5 0.7 copy-start.1
  87.2 10.5 %all-to-all-start.3 = ((bf16[8,112,128]{2,1,0:T(8,128)(2,1)}), bf16[8,112,128]{2,1,0:T(8,128)(2,1)S(1)}, u32[]{:S(2)}, u32[]{:S(2)}) async-start(bf16[8,112,128]{2,1,0:T(8,128)(2,1)} %shard_map.90), calls=%async_computation.3 | async-start | bytes 458752 | tf_op jit(solution)/shard_map/all_to_all | solution.py:35

commit v2 on v1

--- a/solution.py
+++ b/solution.py
@@ -19,20 +19,22 @@
 ALL_Q = CONV * QROWS
 PACK = ALL_Q + 16
 PIECE = 32
+FIRST = 6 * GROUP + 2 * NC
 VMEM_LIMIT = 48 * 1024 * 1024
 SMEM = pl.BlockSpec(memory_space=pltpu.SMEM)
 VMEM = pl.BlockSpec(memory_space=pltpu.VMEM)
 
 
-def params(flops, nbytes, limit=VMEM_LIMIT):
+def params(flops, nbytes):
     return dict(
-        compiler_params=pltpu.CompilerParams(vmem_limit_bytes=limit),
+        compiler_params=pltpu.CompilerParams(vmem_limit_bytes=VMEM_LIMIT),
         cost_estimate=pl.CostEstimate(flops=flops, bytes_accessed=nbytes, transcendentals=0),
     )
 
 
-def exchange(value, names):
-    return lax.all_to_all(value, names, split_axis=0, concat_axis=0, tiled=True)
+def exchange(value, names, order=None):
+    groups = None if order is None else [order]
+    return lax.all_to_all(value, names, split_axis=0, concat_axis=0, tiled=True, axis_index_groups=groups)
 
 
 def lane_group(rows):
@@ -64,7 +66,7 @@
         in_specs=[pl.BlockSpec(memory_space=pltpu.HBM)],
         scratch_shapes=[pltpu.VMEM(weight.shape, weight.dtype)],
         out_shape=jax.ShapeDtypeStruct((SEQ, depth, FEATURE), jnp.bfloat16),
-        **params(1 << 20, 1 << 20, 64 * 1024 * 1024 - 128 * 1024),
+        **params(1 << 20, 1 << 20),
     )(weight)
 
 
@@ -85,7 +87,7 @@
                 message = turned[0]
                 for part in range(1, 4):
                     message = jnp.where(group == ((own + head + part) & 3), turned[part], message)
-                out[head * GROUP + owner] = message.astype(jnp.bfloat16)
+                out[(head * GROUP + owner - FIRST) % (NZ * GROUP)] = message.astype(jnp.bfloat16)
 
 
 def project(numbers, blocks, weight, order):
@@ -124,9 +126,14 @@
     weights = weights / total
     on_diagonal = diagonal(first)
     summed = jnp.zeros((ALL_Q, HEAD), jnp.float32)
-    for index, part in enumerate(parts):
-        spread = jnp.where(on_diagonal, weights[index : index + 1], 0.0).astype(jnp.bfloat16)
-        summed += jnp.dot(spread, part, preferred_element_type=jnp.float32)
+    spread = [
+        jnp.where(on_diagonal, weights[index : index + 1], 0.0).astype(jnp.bfloat16)
+        for index in range(len(parts))
+    ]
+    for index in range(0, len(parts), 2):
+        pair = jnp.concatenate(spread[index : index + 2], axis=1)
+        both = jnp.concatenate(parts[index : index + 2], axis=0)
+        summed += jnp.dot(pair, both, preferred_element_type=jnp.float32)
     return summed, top + jnp.log(total)
 
 
@@ -182,9 +189,9 @@
     group = lane_group(16)
     sums = []
     for c in range(GROUP):
-        total = arrived[c].astype(jnp.float32)
+        total = arrived[(c - FIRST) % (NZ * GROUP)].astype(jnp.float32)
         for plane in range(1, NZ):
-            total += arrived[plane * GROUP + c].astype(jnp.float32)
+            total += arrived[(plane * GROUP + c - FIRST) % (NZ * GROUP)].astype(jnp.float32)
         sums.append(total)
     halves = []
     for tile in range(2):
@@ -339,7 +346,8 @@
     steps = jnp.pad(step_kv.reshape(CONV, STEPS, FEATURE), ((0, 0), (0, 16 - STEPS), (0, 0)))
     cache = kv_cache.reshape(CONV, LOCAL, FEATURE)
 
-    partial = exchange(project(numbers, blocks, weight, order), ("kv", "x", "core"))
+    members = [(place + FIRST) % (NZ * GROUP) for place in range(NZ * GROUP)]
+    partial = exchange(project(numbers, blocks, weight, order), ("kv", "x", "core"), members)
     history_part = attend_history(numbers, cache, steps, asked)
     rows = exchange(attend(numbers, partial, cosine, sine, asked, history_part), ("y",))
     packed = exchange(combine(merge_kernel, (GROUP, PACK, HEAD), rows), ("x", "core"))

time: 99.2 us -> 97 us (0.978)
  waiting for transfers between devices: 23 us -> 19.3 us
  starting transfers between devices: 43.3 us -> 46.9 us
  blocking collectives: 16.3 us -> 15.3 us
    all_to_all x3, waiting for transfers between devices: 18.1 us -> 13.4 us  [exchange(): lax.all_to_all(value, names, split_axis=0, concat_axis=0, tiled=True, axi...]
    all_to_all x3, starting transfers between devices: 28.1 us -> 31.6 us  [exchange(): lax.all_to_all(value, names, split_axis=0, concat_axis=0, tiled=True, axi...]
    all_to_all x1, blocking collectives: 16.3 us -> 15.3 us  [exchange(): lax.all_to_all(value, names, split_axis=0, concat_axis=0, tiled=True, axi...]
    unnamed x14 -> x16, local copies, waits for them, and re-layouts: 1.91 us -> 2.8 us
  transfers between devices with their start and end apart: 8 -> 8, of which waited for: 4 -> 4; matrix products, arithmetic and copies ran while one was open for 3% -> 2% of each run, Pallas kernels for 5% -> 4%
where the time goes in v2:
time: 97 us; the launch traced here: 96.4 us
  starting transfers between devices  46.9 us (48%)
  waiting for transfers between devices  19.3 us (20%)
  blocking collectives  15.3 us (16%)
  Pallas kernels  8.95 us (9%)
  local copies, waits for them, and re-layouts  3.87 us (4%)
  other arithmetic  1.14 us (1%)
  between operations  0.99 us (1%)
    all_to_all x3, starting transfers between devices, exchange(): lax.all_to_all(value, names, split_axis=0, concat_axis=0, tiled=True, axi...  31.6 us
    all_to_all x1, blocking collectives, exchange(): lax.all_to_all(value, names, split_axis=0, concat_axis=0, tiled=True, axi...  15.3 us
    all_to_all x3, waiting for transfers between devices, exchange(): lax.all_to_all(value, names, split_axis=0, concat_axis=0, tiled=True, axi...  13.4 us
    ppermute x1, waiting for transfers between devices, on_device(): lax.ppermute(after, ('x', 'core'), there)  5.83 us
    ppermute x1, starting transfers between devices, on_device(): before = lax.ppermute(hidden, ('x', 'core'), back)  4.71 us
    ppermute x1, starting transfers between devices, on_device(): after = lax.ppermute(hidden, ('x', 'core'), there)  3.95 us
    unnamed x16, local copies, waits for them, and re-layouts  2.8 us
    ppermute x1, starting transfers between devices, on_device(): near_other = lax.ppermute(near, 'core', swap)  2.78 us
  transfers between devices with their start and end apart: 8, of which 4 were waited for; matrix products, arithmetic and copies ran while one was open for 2% of the time, Pallas kernels for 4%

profile of v2, /device:TPU:1, one launch (start us, length us, event | category | flops | bytes accessed | tf_op | source)
XLA Modules:
  0.0 96.4 jit_solution(4734436294150932936)
XLA Ops:
  0.6 4.0 %collective-permute-start = (bf16[64,1536]{1,0:T(8,128)(2,1)}, bf16[64,1536]{1,0:T(8,128)(2,1)S(1)}, u32[]{:S(2)}, u32[]{:S(2)}) collective-permute-start(bf16[64,1536]{1,0:T(8,128)(2,1)} %bitcast.23), channel_id=1, source_target_pairs={{0,384},{8,136},{128,0},{136,264},{256,128},{264,392},{384,256},{3... | collective-permute-start | bytes 589832 | tf_op jit(solution)/shard_map/ppermute | solution.py:309
  4.6 0.9 copy-done.1
  5.5 1.0 %shard_map.86 = bf16[64,24,256]{2,1,0:T(8,128)(2,1)} custom-call(bf16[24,2048]{1,0:T(8,128)(2,1)S(1)} %copy-done.1), custom_call_target="tpu_custom_call" | custom-call | flops 1048576 | bytes 1048576 | tf_op jit(solution)/shard_map/pallas_call | solution.py:64
  6.5 10.1 %all-to-all-start = ((bf16[64,24,256]{2,1,0:T(8,128)(2,1)}), bf16[64,24,256]{2,1,0:T(8,128)(2,1)S(1)}, u32[]{:S(2)}, u32[]{:S(2)}) async-start(bf16[64,24,256]{2,1,0:T(8,128)(2,1)} %shard_map.86), calls=%async_computation | async-start | bytes 1572864 | tf_op jit(solution)/shard_map/all_to_all | solution.py:37
  17.1 0.7 copy-done.5
  17.8 4.7 %collective-permute-start.2 = (bf16[64,1536]{1,0:T(8,128)(2,1)S(1)}, bf16[64,1536]{1,0:T(8,128)(2,1)S(1)}, u32[]{:S(2)}, u32[]{:S(2)}) collective-permute-start(bf16[64,1536]{1,0:T(8,128)(2,1)S(1)} %bitcast.25), channel_id=1, source_target_pairs={{0,128},{8,392},{128,256},{136,8},{256,384},{264,136},{384,0},{392... | collective-permute-start | bytes 589832 | tf_op jit(solution)/shard_map/ppermute | solution.py:311
  22.5 1.9 %collective-permute-start.3 = (bf16[64,1536]{1,0:T(8,128)(2,1)S(1)}, bf16[64,1536]{1,0:T(8,128)(2,1)S(1)}, u32[]{:S(2)}, u32[]{:S(2)}) collective-permute-start(bf16[64,1536]{1,0:T(8,128)(2,1)S(1)} %collective-permute-done), channel_id=1, source_target_pairs={{0,384},{8,136},{128,0},{136,264},{256,128},{264,392},{384,256},{3... | collective-permute-start | bytes 589832 | tf_op jit(solution)/shard_map/ppermute | solution.py:313
  24.5 2.8 %collective-permute-start.1 = (bf16[128,1536]{1,0:T(8,128)(2,1)S(1)}, bf16[128,1536]{1,0:T(8,128)(2,1)S(1)}, u32[]{:S(2)}, u32[]{:S(2)}) collective-permute-start(bf16[128,1536]{1,0:T(8,128)(2,1)S(1)} %constant_dynamic-update-slice_fusion.near), channel_id=1, source_target_pairs={{0,8},{8,0},{1,9},{9,1},{2,10},{10,2},{3,11},{11,3},{4,12},{12,4},... | collective-permute-start | bytes 1179656 | tf_op jit(solution)/shard_map/ppermute | solution.py:314
  27.3 5.8 %collective-permute-done.3 = bf16[64,1536]{1,0:T(8,128)(2,1)S(1)} collective-permute-done((bf16[64,1536]{1,0:T(8,128)(2,1)S(1)}, bf16[64,1536]{1,0:T(8,128)(2,1)S(1)}, u32[]{:S(2)}, u32[]{:S(2)}) %collective-permute-start.3) | collective-permute-done | bytes 196640 | tf_op jit(solution)/shard_map/ppermute | solution.py:313
  33.2 1.9 %collective-permute-start.4 = (bf16[128,1536]{1,0:T(8,128)(2,1)S(1)}, bf16[128,1536]{1,0:T(8,128)(2,1)S(1)}, u32[]{:S(2)}, u32[]{:S(2)}) collective-permute-start(bf16[128,1536]{1,0:T(8,128)(2,1)S(1)} %constant_dynamic-update-slice_fusion.2.far), channel_id=1, source_target_pairs={{0,8},{8,0},{1,9},{9,1},{2,10},{10,2},{3,11},{11,3},{4,12},{12,4},... | collective-permute-start | bytes 1179656 | tf_op jit(solution)/shard_map/ppermute | solution.py:316
  36.2 0.7 copy-done.6
  37.3 2.4 %all-to-all-done = bf16[64,24,256]{2,1,0:T(8,128)(2,1)S(1)} async-done(((bf16[64,24,256]{2,1,0:T(8,128)(2,1)}), bf16[64,24,256]{2,1,0:T(8,128)(2,1)S(1)}, u32[]{:S(2)}, u32[]{:S(2)}) %all-to-all-start) | async-done | bytes 786464 | tf_op jit(solution)/shard_map/all_to_all | solution.py:37
  39.7 2.3 %shard_map.87 = bf16[64,16,128]{2,1,0:T(8,128)(2,1)} custom-call(s32[8]{0:T(128)S(1)} %concatenate.16.numbers, bf16[128,1536]{1,0:T(8,128)(2,1)S(1)} %constant_dynamic-update-slice_fusion.near, bf16[128,1536]{1,0:T(8,128)(2,1)S(1)} %collective-permute-done.1.near_other, bf16[128,1536]{1,0:T(8,128)(2,1)S(1)} %constant_dynamic-update-slice_fusion.2.far, ...), custom_call_target="tpu_custom_call" | custom-call | flops 402653184 | bytes 3145728 | tf_op jit(solution)/shard_map/pallas_call | solution.py:94
  42.0 15.5 %all-to-all-start.1 = ((bf16[64,16,128]{2,1,0:T(8,128)(2,1)}), bf16[64,16,128]{2,1,0:T(8,128)(2,1)S(1)}, u32[]{:S(2)}, u32[]{:S(2)}) async-start(bf16[64,16,128]{2,1,0:T(8,128)(2,1)} %shard_map.87), calls=%async_computation.1 | async-start | bytes 524288 | tf_op jit(solution)/shard_map/all_to_all | solution.py:37
  57.6 0.5 copy-done.2
  58.2 1.1 %shard_map.88 = (f32[96,128]{1,0:T(8,128)S(1)}, f32[96,128]{1,0:T(8,128)S(1)}, f32[96,128]{1,0:T(8,128)S(1)}) custom-call(s32[8]{0:T(128)S(1)} %concatenate.16.numbers, bf16[2,256,256]{2,1,0:T(8,128)(2,1)S(1)} %bitcast.18, bf16[2,16,256]{2,1,0:T(8,128)(2,1)S(1)} %pad.4.step_kv, bf16[2,48,128]{2,1,0:T(8,128)(2,1)S(1)} %bitcast.20), custom_call_target="tpu_custom_call" | custom-call | flops 12582912 | bytes 1048576 | tf_op jit(solution)/shard_map/pallas_call | solution.py:178
  59.6 6.3 %all-to-all-done.1.arrived = bf16[64,16,128]{2,1,0:T(8,128)(2,1)S(1)} async-done(((bf16[64,16,128]{2,1,0:T(8,128)(2,1)}), bf16[64,16,128]{2,1,0:T(8,128)(2,1)S(1)}, u32[]{:S(2)}, u32[]{:S(2)}) %all-to-all-start.1) | async-done | bytes 262176 | tf_op jit(solution)/shard_map/all_to_all | solution.py:37
  66.0 1.2 %shard_map.89 = bf16[8,128,128]{2,1,0:T(8,128)(2,1)S(1)} custom-call(s32[8]{0:T(128)S(1)} %concatenate.16.numbers, bf16[64,16,128]{2,1,0:T(8,128)(2,1)S(1)} %all-to-all-done.1.arrived, f32[64,128]{1,0:T(8,128)S(1)} %get-tuple-element.31.cosine, f32[64,128]{1,0:T(8,128)S(1)} %get-tuple-element.32.sine, bf16[2,48,128]{2,1,0:T(8,128)(2,1)S(1)} %bitcast.21, ...), custom_call_target="tpu_custom_call" | custom-call | flops 3145728 | bytes 1048576 | tf_op jit(solution)/shard_map/pallas_call | solution.py:233
  67.2 15.3 %all_to_all.20.arrived = bf16[8,128,128]{2,1,0:T(8,128)(2,1)S(1)} all-to-all(bf16[8,128,128]{2,1,0:T(8,128)(2,1)S(1)} %shard_map.89), channel_id=1, replica_groups=mesh['x'=4,'y'=8,'core'=2,'kv'=8] {'y'}, dimensions={0} | all-to-all | bytes 524288 | tf_op jit(solution)/shard_map/all_to_all | solution.py:37
  82.5 0.9 shard_map.90
  83.4 6.0 %all-to-all-start.3 = ((bf16[8,112,128]{2,1,0:T(8,128)(2,1)}), bf16[8,112,128]{2,1,0:T(8,128)(2,1)S(1)}, u32[]{:S(2)}, u32[]{:S(2)}) async-start(bf16[8,112,128]{2,1,0:T(8,128)(2,1)} %shard_map.90), calls=%async_computation.3 | async-start | bytes 458752 | tf_op jit(solution)/shard_map/all_to_all | solution.py:37
  89.4 1.5 %shard_map.92 = bf16[2,256,256]{2,1,0:T(8,128)(2,1)} custom-call(s32[8]{0:T(128)S(1)} %concatenate.16.numbers, bf16[8,128,128]{2,1,0:T(8,128)(2,1)S(1)} %all_to_all.20.arrived, bf16[2,256,256]{2,1,0:T(8,128)(2,1)S(1)} %bitcast.19), custom_call_target="tpu_custom_call" | custom-call | flops 67108864 | bytes 1048576 | tf_op jit(solution)/shard_map/pallas_call | solution.py:286
  90.8 4.7 %all-to-all-done.3.arrived = bf16[8,112,128]{2,1,0:T(8,128)(2,1)S(1)} async-done(((bf16[8,112,128]{2,1,0:T(8,128)(2,1)}), bf16[8,112,128]{2,1,0:T(8,128)(2,1)S(1)}, u32[]{:S(2)}, u32[]{:S(2)}) %all-to-all-start.3) | async-done | bytes 229408 | tf_op jit(solution)/shard_map/all_to_all | solution.py:37
  95.6 0.8 shard_map.91
  (46 shorter events, 2.3 us)
Async XLA Ops:
  0.6 17.2 %collective-permute-start = (bf16[64,1536]{1,0:T(8,128)(2,1)}, bf16[64,1536]{1,0:T(8,128)(2,1)S(1)}, u32[]{:S(2)}, u32[]{:S(2)}) collective-permute-start(bf16[64,1536]{1,0:T(8,128)(2,1)} %bitcast.23), channel_id=1, source_target_pairs={{0,384},{8,136},{128,0},{136,264},{256,128},{264,392},{384,256},{3... | collective-permute-start | bytes 589832 | tf_op jit(solution)/shard_map/ppermute | solution.py:309
  4.6 0.9 copy-start.1
  6.5 33.1 %all-to-all-start = ((bf16[64,24,256]{2,1,0:T(8,128)(2,1)}), bf16[64,24,256]{2,1,0:T(8,128)(2,1)S(1)}, u32[]{:S(2)}, u32[]{:S(2)}) async-start(bf16[64,24,256]{2,1,0:T(8,128)(2,1)} %shard_map.86), calls=%async_computation | async-start | bytes 1572864 | tf_op jit(solution)/shard_map/all_to_all | solution.py:37
  16.7 1.1 %copy-start.3 = (bf16[2,32,1536]{2,1,0:T(8,128)(2,1)S(1)}, bf16[2,32,1536]{2,1,0:T(8,128)(2,1)}, u32[]{:S(2)}) copy-start(bf16[2,32,1536]{2,1,0:T(8,128)(2,1)} %param.7) | copy-start | bytes 589828
  17.0 0.7 copy-start.5
  17.8 9.5 %collective-permute-start.2 = (bf16[64,1536]{1,0:T(8,128)(2,1)S(1)}, bf16[64,1536]{1,0:T(8,128)(2,1)S(1)}, u32[]{:S(2)}, u32[]{:S(2)}) collective-permute-start(bf16[64,1536]{1,0:T(8,128)(2,1)S(1)} %bitcast.25), channel_id=1, source_target_pairs={{0,128},{8,392},{128,256},{136,8},{256,384},{264,136},{384,0},{392... | collective-permute-start | bytes 589832 | tf_op jit(solution)/shard_map/ppermute | solution.py:311
  22.5 10.6 %collective-permute-start.3 = (bf16[64,1536]{1,0:T(8,128)(2,1)S(1)}, bf16[64,1536]{1,0:T(8,128)(2,1)S(1)}, u32[]{:S(2)}, u32[]{:S(2)}) collective-permute-start(bf16[64,1536]{1,0:T(8,128)(2,1)S(1)} %collective-permute-done), channel_id=1, source_target_pairs={{0,384},{8,136},{128,0},{136,264},{256,128},{264,392},{384,256},{3... | collective-permute-start | bytes 589832 | tf_op jit(solution)/shard_map/ppermute | solution.py:313
  24.5 10.6 %collective-permute-start.1 = (bf16[128,1536]{1,0:T(8,128)(2,1)S(1)}, bf16[128,1536]{1,0:T(8,128)(2,1)S(1)}, u32[]{:S(2)}, u32[]{:S(2)}) collective-permute-start(bf16[128,1536]{1,0:T(8,128)(2,1)S(1)} %constant_dynamic-update-slice_fusion.near), channel_id=1, source_target_pairs={{0,8},{8,0},{1,9},{9,1},{2,10},{10,2},{3,11},{11,3},{4,12},{12,4},... | collective-permute-start | bytes 1179656 | tf_op jit(solution)/shard_map/ppermute | solution.py:314
  27.3 7.8 %copy-start.4 = (s32[2]{0:T(128)S(1)}, s32[2]{0:T(128)}, u32[]{:S(2)}) copy-start(s32[2]{0:T(128)} %param.12) | copy-start | bytes 28
  33.2 4.1 %collective-permute-start.4 = (bf16[128,1536]{1,0:T(8,128)(2,1)S(1)}, bf16[128,1536]{1,0:T(8,128)(2,1)S(1)}, u32[]{:S(2)}, u32[]{:S(2)}) collective-permute-start(bf16[128,1536]{1,0:T(8,128)(2,1)S(1)} %constant_dynamic-update-slice_fusion.2.far), channel_id=1, source_target_pairs={{0,8},{8,0},{1,9},{9,1},{2,10},{10,2},{3,11},{11,3},{4,12},{12,4},... | collective-permute-start | bytes 1179656 | tf_op jit(solution)/shard_map/ppermute | solution.py:316
  36.2 0.7 copy-start.6
  42.0 15.7 %copy-start = (bf16[2,256,1,256]{3,1,2,0:T(8,128)(2,1)S(1)}, bf16[2,256,1,256]{3,1,2,0:T(8,128)(2,1)}, u32[]{:S(2)}) copy-start(bf16[2,256,1,256]{3,1,2,0:T(8,128)(2,1)} %param.9) | copy-start | bytes 786436
  42.0 24.0 %all-to-all-start.1 = ((bf16[64,16,128]{2,1,0:T(8,128)(2,1)}), bf16[64,16,128]{2,1,0:T(8,128)(2,1)S(1)}, u32[]{:S(2)}, u32[]{:S(2)}) async-start(bf16[64,16,128]{2,1,0:T(8,128)(2,1)} %shard_map.87), calls=%async_computation.1 | async-start | bytes 524288 | tf_op jit(solution)/shard_map/all_to_all | solution.py:37
  57.5 0.7 copy-start.2
  83.4 12.2 %all-to-all-start.3 = ((bf16[8,112,128]{2,1,0:T(8,128)(2,1)}), bf16[8,112,128]{2,1,0:T(8,128)(2,1)S(1)}, u32[]{:S(2)}, u32[]{:S(2)}) async-start(bf16[8,112,128]{2,1,0:T(8,128)(2,1)} %shard_map.90), calls=%async_computation.3 | async-start | bytes 458752 | tf_op jit(solution)/shard_map/all_to_all | solution.py:37

commit v3 on v2

--- a/solution.py
+++ b/solution.py
@@ -19,7 +19,9 @@
 ALL_Q = CONV * QROWS
 PACK = ALL_Q + 16
 PIECE = 32
+FIRST_SEQ = (2 * NY + 6) * NC
 FIRST = 6 * GROUP + 2 * NC
+FIRST_Y = 4
 VMEM_LIMIT = 48 * 1024 * 1024
 SMEM = pl.BlockSpec(memory_space=pltpu.SMEM)
 VMEM = pl.BlockSpec(memory_space=pltpu.VMEM)
@@ -32,8 +34,9 @@
     )
 
 
-def exchange(value, names, order=None):
-    groups = None if order is None else [order]
+def exchange(value, names, first=0):
+    size = value.shape[0]
+    groups = [[(place + first) % size for place in range(size)]] if first else None
     return lax.all_to_all(value, names, split_axis=0, concat_axis=0, tiled=True, axis_index_groups=groups)
 
 
@@ -56,7 +59,7 @@
             tiles.append(tile)
         columns = jnp.concatenate(tiles, axis=1).astype(jnp.bfloat16)
         for y in range(NY):
-            out[c // NC * (NY * NC) + y * NC + c % NC] = columns
+            out[(c // NC * (NY * NC) + y * NC + c % NC - FIRST_SEQ) % SEQ] = columns
 
 
 def split_weight(weight):
@@ -72,7 +75,9 @@
 
 def project_kernel(numbers, near, near_other, far, far_other, weight, order, out):
     rows = jnp.concatenate([near[...], near_other[...], far[...], far_other[...]], axis=0)
-    partial = jnp.dot(rows, weight[...], preferred_element_type=jnp.float32).astype(jnp.bfloat16)
+    start = (SEQ - FIRST_SEQ) * (WIDTH // SEQ)
+    weights = jnp.concatenate([weight[start:], weight[:start]], axis=0)
+    partial = jnp.dot(rows, weights, preferred_element_type=jnp.float32).astype(jnp.bfloat16)
     ordered = jnp.dot(order[...], partial, preferred_element_type=jnp.float32)
     own = numbers[6]
     group = lane_group(16)
@@ -206,7 +211,7 @@
     key = key * cosine[...] + pltpu.roll(key, HEAD // 2, 1) * sine[...]
     for row in range(NY):
         both = jnp.concatenate([key[row * 8 : row * 8 + 8], value[row * 8 : row * 8 + 8]], axis=0)
-        out[row, :16] = both.astype(jnp.bfloat16)
+        out[(row - FIRST_Y) % NY, :16] = both.astype(jnp.bfloat16)
     key, value = key.astype(jnp.bfloat16), value.astype(jnp.bfloat16)
 
     asker = lax.broadcasted_iota(jnp.int32, (ALL_Q, SLICE), 0) >= QROWS
@@ -263,7 +268,7 @@
 
 def write_kernel(numbers, arrived, cache, new_cache):
     t = numbers[4]
-    rows = jnp.concatenate([arrived[row, :16].astype(jnp.float32) for row in range(NY)], axis=0)
+    rows = jnp.concatenate([arrived[(row - FIRST_Y) % NY, :16].astype(jnp.float32) for row in range(NY)], axis=0)
     rows = rows.astype(jnp.bfloat16)
     for conv in range(CONV):
         history, length = numbers[conv], numbers[2 + conv]
@@ -297,7 +302,7 @@
     t = (x * NY + y) * NC + core
     own = x * NC + core
 
-    weight = exchange(split_weight(kv_weight), ("x", "y", "core")).reshape(WIDTH, FEATURE)
+    weight = exchange(split_weight(kv_weight), ("x", "y", "core"), FIRST_SEQ).reshape(WIDTH, FEATURE)
 
     swap = [(0, 1), (1, 0)]
     there, back = [], []
@@ -346,10 +351,9 @@
     steps = jnp.pad(step_kv.reshape(CONV, STEPS, FEATURE), ((0, 0), (0, 16 - STEPS), (0, 0)))
     cache = kv_cache.reshape(CONV, LOCAL, FEATURE)
 
-    members = [(place + FIRST) % (NZ * GROUP) for place in range(NZ * GROUP)]
-    partial = exchange(project(numbers, blocks, weight, order), ("kv", "x", "core"), members)
+    partial = exchange(project(numbers, blocks, weight, order), ("kv", "x", "core"), FIRST)
     history_part = attend_history(numbers, cache, steps, asked)
-    rows = exchange(attend(numbers, partial, cosine, sine, asked, history_part), ("y",))
+    rows = exchange(attend(numbers, partial, cosine, sine, asked, history_part), ("y",), FIRST_Y)
     packed = exchange(combine(merge_kernel, (GROUP, PACK, HEAD), rows), ("x", "core"))
     new_cache = write(numbers, rows, cache)
     attended = combine(finish_kernel, (ALL_Q, HEAD), packed)

time: 97 us -> 92.9 us (0.958)
  waiting for transfers between devices: 19.3 us -> 16.7 us
  blocking collectives: 15.3 us -> 13 us
    ppermute x1, starting transfers between devices: 4.71 us -> 2.18 us  [on_device(): before = lax.ppermute(hidden, ('x', 'core'), back)]
    all_to_all x3, waiting for transfers between devices: 13.4 us -> 11.1 us  [exchange(): lax.all_to_all(value, names, split_axis=0, concat_axis=0, tiled=True, axi...]
    all_to_all x1, blocking collectives: 15.3 us -> 13 us  [exchange(): lax.all_to_all(value, names, split_axis=0, concat_axis=0, tiled=True, axi...]
    ppermute x1, starting transfers between devices: 2.78 us -> 4.04 us  [on_device(): near_other = lax.ppermute(near, 'core', swap)]
    ppermute x1, starting transfers between devices: 1.92 us -> 3.11 us  [on_device(): lax.ppermute(after, ('x', 'core'), there)]
  transfers between devices with their start and end apart: 8 -> 8, of which waited for: 4 -> 3; matrix products, arithmetic and copies ran while one was open for 2% -> 2% of each run, Pallas kernels for 4% -> 4%
where the time goes in v3:
time: 92.9 us; the launch traced here: 92.3 us
  starting transfers between devices  47.7 us (51%)
  waiting for transfers between devices  16.7 us (18%)
  blocking collectives  13 us (14%)
  Pallas kernels  8.95 us (10%)
  local copies, waits for them, and re-layouts  3.87 us (4%)
  other arithmetic  1.14 us (1%)
  between operations  1 us (1%)
    all_to_all x3, starting transfers between devices, exchange(): lax.all_to_all(value, names, split_axis=0, concat_axis=0, tiled=True, axi...  32.5 us
    all_to_all x1, blocking collectives, exchange(): lax.all_to_all(value, names, split_axis=0, concat_axis=0, tiled=True, axi...  13 us
    all_to_all x3, waiting for transfers between devices, exchange(): lax.all_to_all(value, names, split_axis=0, concat_axis=0, tiled=True, axi...  11.1 us
    ppermute x1, waiting for transfers between devices, on_device(): lax.ppermute(after, ('x', 'core'), there)  5.6 us
    ppermute x1, starting transfers between devices, on_device(): near_other = lax.ppermute(near, 'core', swap)  4.04 us
    ppermute x1, starting transfers between devices, on_device(): after = lax.ppermute(hidden, ('x', 'core'), there)  3.95 us
    ppermute x1, starting transfers between devices, on_device(): lax.ppermute(after, ('x', 'core'), there)  3.11 us
    unnamed x16, local copies, waits for them, and re-layouts  2.8 us
  transfers between devices with their start and end apart: 8, of which 3 were waited for; matrix products, arithmetic and copies ran while one was open for 2% of the time, Pallas kernels for 4%

profile of v3, /device:TPU:1, one launch (start us, length us, event | category | flops | bytes accessed | tf_op | source)
XLA Modules:
  0.0 92.3 jit_solution(15172630390748614980)
XLA Ops:
  0.6 4.0 %collective-permute-start = (bf16[64,1536]{1,0:T(8,128)(2,1)}, bf16[64,1536]{1,0:T(8,128)(2,1)S(1)}, u32[]{:S(2)}, u32[]{:S(2)}) collective-permute-start(bf16[64,1536]{1,0:T(8,128)(2,1)} %bitcast.23), channel_id=1, source_target_pairs={{0,384},{8,136},{128,0},{136,264},{256,128},{264,392},{384,256},{3... | collective-permute-start | bytes 589832 | tf_op jit(solution)/shard_map/ppermute | solution.py:314
  4.6 0.9 copy-done.1
  5.5 1.0 %shard_map.86 = bf16[64,24,256]{2,1,0:T(8,128)(2,1)} custom-call(bf16[24,2048]{1,0:T(8,128)(2,1)S(1)} %copy-done.1), custom_call_target="tpu_custom_call" | custom-call | flops 1048576 | bytes 1048576 | tf_op jit(solution)/shard_map/pallas_call | solution.py:67
  6.5 13.4 %all-to-all-start = ((bf16[64,24,256]{2,1,0:T(8,128)(2,1)}), bf16[64,24,256]{2,1,0:T(8,128)(2,1)S(1)}, u32[]{:S(2)}, u32[]{:S(2)}) async-start(bf16[64,24,256]{2,1,0:T(8,128)(2,1)} %shard_map.86), calls=%async_computation | async-start | bytes 1572864 | tf_op jit(solution)/shard_map/all_to_all | solution.py:40
  20.3 0.7 copy-done.5
  21.1 2.2 %collective-permute-start.2 = (bf16[64,1536]{1,0:T(8,128)(2,1)S(1)}, bf16[64,1536]{1,0:T(8,128)(2,1)S(1)}, u32[]{:S(2)}, u32[]{:S(2)}) collective-permute-start(bf16[64,1536]{1,0:T(8,128)(2,1)S(1)} %bitcast.25), channel_id=1, source_target_pairs={{0,128},{8,392},{128,256},{136,8},{256,384},{264,136},{384,0},{392... | collective-permute-start | bytes 589832 | tf_op jit(solution)/shard_map/ppermute | solution.py:316
  23.3 3.1 %collective-permute-start.3 = (bf16[64,1536]{1,0:T(8,128)(2,1)S(1)}, bf16[64,1536]{1,0:T(8,128)(2,1)S(1)}, u32[]{:S(2)}, u32[]{:S(2)}) collective-permute-start(bf16[64,1536]{1,0:T(8,128)(2,1)S(1)} %collective-permute-done), channel_id=1, source_target_pairs={{0,384},{8,136},{128,0},{136,264},{256,128},{264,392},{384,256},{3... | collective-permute-start | bytes 589832 | tf_op jit(solution)/shard_map/ppermute | solution.py:318
  26.4 4.0 %collective-permute-start.1 = (bf16[128,1536]{1,0:T(8,128)(2,1)S(1)}, bf16[128,1536]{1,0:T(8,128)(2,1)S(1)}, u32[]{:S(2)}, u32[]{:S(2)}) collective-permute-start(bf16[128,1536]{1,0:T(8,128)(2,1)S(1)} %constant_dynamic-update-slice_fusion.near), channel_id=1, source_target_pairs={{0,8},{8,0},{1,9},{9,1},{2,10},{10,2},{3,11},{11,3},{4,12},{12,4},... | collective-permute-start | bytes 1179656 | tf_op jit(solution)/shard_map/ppermute | solution.py:319
  30.5 5.6 %collective-permute-done.3 = bf16[64,1536]{1,0:T(8,128)(2,1)S(1)} collective-permute-done((bf16[64,1536]{1,0:T(8,128)(2,1)S(1)}, bf16[64,1536]{1,0:T(8,128)(2,1)S(1)}, u32[]{:S(2)}, u32[]{:S(2)}) %collective-permute-start.3) | collective-permute-done | bytes 196640 | tf_op jit(solution)/shard_map/ppermute | solution.py:318
  36.1 1.9 %collective-permute-start.4 = (bf16[128,1536]{1,0:T(8,128)(2,1)S(1)}, bf16[128,1536]{1,0:T(8,128)(2,1)S(1)}, u32[]{:S(2)}, u32[]{:S(2)}) collective-permute-start(bf16[128,1536]{1,0:T(8,128)(2,1)S(1)} %constant_dynamic-update-slice_fusion.2.far), channel_id=1, source_target_pairs={{0,8},{8,0},{1,9},{9,1},{2,10},{10,2},{3,11},{11,3},{4,12},{12,4},... | collective-permute-start | bytes 1179656 | tf_op jit(solution)/shard_map/ppermute | solution.py:321
  39.2 0.7 copy-done.6
  40.2 2.3 %shard_map.87 = bf16[64,16,128]{2,1,0:T(8,128)(2,1)} custom-call(s32[8]{0:T(128)S(1)} %concatenate.16.numbers, bf16[128,1536]{1,0:T(8,128)(2,1)S(1)} %constant_dynamic-update-slice_fusion.near, bf16[128,1536]{1,0:T(8,128)(2,1)S(1)} %collective-permute-done.1.near_other, bf16[128,1536]{1,0:T(8,128)(2,1)S(1)} %constant_dynamic-update-slice_fusion.2.far, ...), custom_call_target="tpu_custom_call" | custom-call | flops 402653184 | bytes 3145728 | tf_op jit(solution)/shard_map/pallas_call | solution.py:99
  42.6 14.1 %all-to-all-start.1 = ((bf16[64,16,128]{2,1,0:T(8,128)(2,1)}), bf16[64,16,128]{2,1,0:T(8,128)(2,1)S(1)}, u32[]{:S(2)}, u32[]{:S(2)}) async-start(bf16[64,16,128]{2,1,0:T(8,128)(2,1)} %shard_map.87), calls=%async_computation.1 | async-start | bytes 524288 | tf_op jit(solution)/shard_map/all_to_all | solution.py:40
  56.9 0.5 copy-done.2
  57.4 1.1 %shard_map.88 = (f32[96,128]{1,0:T(8,128)S(1)}, f32[96,128]{1,0:T(8,128)S(1)}, f32[96,128]{1,0:T(8,128)S(1)}) custom-call(s32[8]{0:T(128)S(1)} %concatenate.16.numbers, bf16[2,256,256]{2,1,0:T(8,128)(2,1)S(1)} %bitcast.18, bf16[2,16,256]{2,1,0:T(8,128)(2,1)S(1)} %pad.4.step_kv, bf16[2,48,128]{2,1,0:T(8,128)(2,1)S(1)} %bitcast.20), custom_call_target="tpu_custom_call" | custom-call | flops 12582912 | bytes 1048576 | tf_op jit(solution)/shard_map/pallas_call | solution.py:183
  58.5 0.2 fusion.4
  58.8 6.3 %all-to-all-done.1.arrived = bf16[64,16,128]{2,1,0:T(8,128)(2,1)S(1)} async-done(((bf16[64,16,128]{2,1,0:T(8,128)(2,1)}), bf16[64,16,128]{2,1,0:T(8,128)(2,1)S(1)}, u32[]{:S(2)}, u32[]{:S(2)}) %all-to-all-start.1) | async-done | bytes 262176 | tf_op jit(solution)/shard_map/all_to_all | solution.py:40
  65.2 1.2 %shard_map.89 = bf16[8,128,128]{2,1,0:T(8,128)(2,1)S(1)} custom-call(s32[8]{0:T(128)S(1)} %concatenate.16.numbers, bf16[64,16,128]{2,1,0:T(8,128)(2,1)S(1)} %all-to-all-done.1.arrived, f32[64,128]{1,0:T(8,128)S(1)} %get-tuple-element.31.cosine, f32[64,128]{1,0:T(8,128)S(1)} %get-tuple-element.32.sine, bf16[2,48,128]{2,1,0:T(8,128)(2,1)S(1)} %bitcast.21, ...), custom_call_target="tpu_custom_call" | custom-call | flops 3145728 | bytes 1048576 | tf_op jit(solution)/shard_map/pallas_call | solution.py:238
  66.4 13.0 %all_to_all.20.arrived = bf16[8,128,128]{2,1,0:T(8,128)(2,1)S(1)} all-to-all(bf16[8,128,128]{2,1,0:T(8,128)(2,1)S(1)} %shard_map.89), channel_id=1, replica_groups={{64,80,96,112,0,16,32,48},{65,81,97,113,1,17,33,49},{66,82,98,114,2,18,..., dimensions={0} | all-to-all | bytes 524288 | tf_op jit(solution)/shard_map/all_to_all | solution.py:40
  79.3 0.9 shard_map.90
  80.3 5.0 %all-to-all-start.3 = ((bf16[8,112,128]{2,1,0:T(8,128)(2,1)}), bf16[8,112,128]{2,1,0:T(8,128)(2,1)S(1)}, u32[]{:S(2)}, u32[]{:S(2)}) async-start(bf16[8,112,128]{2,1,0:T(8,128)(2,1)} %shard_map.90), calls=%async_computation.3 | async-start | bytes 458752 | tf_op jit(solution)/shard_map/all_to_all | solution.py:40
  85.3 1.5 %shard_map.92 = bf16[2,256,256]{2,1,0:T(8,128)(2,1)} custom-call(s32[8]{0:T(128)S(1)} %concatenate.16.numbers, bf16[8,128,128]{2,1,0:T(8,128)(2,1)S(1)} %all_to_all.20.arrived, bf16[2,256,256]{2,1,0:T(8,128)(2,1)S(1)} %bitcast.19), custom_call_target="tpu_custom_call" | custom-call | flops 67108864 | bytes 1048576 | tf_op jit(solution)/shard_map/pallas_call | solution.py:291
  86.7 4.7 %all-to-all-done.3.arrived = bf16[8,112,128]{2,1,0:T(8,128)(2,1)S(1)} async-done(((bf16[8,112,128]{2,1,0:T(8,128)(2,1)}), bf16[8,112,128]{2,1,0:T(8,128)(2,1)S(1)}, u32[]{:S(2)}, u32[]{:S(2)}) %all-to-all-start.3) | async-done | bytes 229408 | tf_op jit(solution)/shard_map/all_to_all | solution.py:40
  91.4 0.8 shard_map.91
  (46 shorter events, 2.1 us)
Async XLA Ops:
  0.6 20.5 %collective-permute-start = (bf16[64,1536]{1,0:T(8,128)(2,1)}, bf16[64,1536]{1,0:T(8,128)(2,1)S(1)}, u32[]{:S(2)}, u32[]{:S(2)}) collective-permute-start(bf16[64,1536]{1,0:T(8,128)(2,1)} %bitcast.23), channel_id=1, source_target_pairs={{0,384},{8,136},{128,0},{136,264},{256,128},{264,392},{384,256},{3... | collective-permute-start | bytes 589832 | tf_op jit(solution)/shard_map/ppermute | solution.py:314
  4.6 0.9 copy-start.1
  6.5 33.7 %all-to-all-start = ((bf16[64,24,256]{2,1,0:T(8,128)(2,1)}), bf16[64,24,256]{2,1,0:T(8,128)(2,1)S(1)}, u32[]{:S(2)}, u32[]{:S(2)}) async-start(bf16[64,24,256]{2,1,0:T(8,128)(2,1)} %shard_map.86), calls=%async_computation | async-start | bytes 1572864 | tf_op jit(solution)/shard_map/all_to_all | solution.py:40
  20.0 1.1 %copy-start.3 = (bf16[2,32,1536]{2,1,0:T(8,128)(2,1)S(1)}, bf16[2,32,1536]{2,1,0:T(8,128)(2,1)}, u32[]{:S(2)}) copy-start(bf16[2,32,1536]{2,1,0:T(8,128)(2,1)} %param.7) | copy-start | bytes 589828
  20.3 0.7 copy-start.5
  21.1 9.4 %collective-permute-start.2 = (bf16[64,1536]{1,0:T(8,128)(2,1)S(1)}, bf16[64,1536]{1,0:T(8,128)(2,1)S(1)}, u32[]{:S(2)}, u32[]{:S(2)}) collective-permute-start(bf16[64,1536]{1,0:T(8,128)(2,1)S(1)} %bitcast.25), channel_id=1, source_target_pairs={{0,128},{8,392},{128,256},{136,8},{256,384},{264,136},{384,0},{392... | collective-permute-start | bytes 589832 | tf_op jit(solution)/shard_map/ppermute | solution.py:316
  23.3 12.8 %collective-permute-start.3 = (bf16[64,1536]{1,0:T(8,128)(2,1)S(1)}, bf16[64,1536]{1,0:T(8,128)(2,1)S(1)}, u32[]{:S(2)}, u32[]{:S(2)}) collective-permute-start(bf16[64,1536]{1,0:T(8,128)(2,1)S(1)} %collective-permute-done), channel_id=1, source_target_pairs={{0,384},{8,136},{128,0},{136,264},{256,128},{264,392},{384,256},{3... | collective-permute-start | bytes 589832 | tf_op jit(solution)/shard_map/ppermute | solution.py:318
  26.4 11.6 %collective-permute-start.1 = (bf16[128,1536]{1,0:T(8,128)(2,1)S(1)}, bf16[128,1536]{1,0:T(8,128)(2,1)S(1)}, u32[]{:S(2)}, u32[]{:S(2)}) collective-permute-start(bf16[128,1536]{1,0:T(8,128)(2,1)S(1)} %constant_dynamic-update-slice_fusion.near), channel_id=1, source_target_pairs={{0,8},{8,0},{1,9},{9,1},{2,10},{10,2},{3,11},{11,3},{4,12},{12,4},... | collective-permute-start | bytes 1179656 | tf_op jit(solution)/shard_map/ppermute | solution.py:319
  30.5 7.6 %copy-start.4 = (s32[2]{0:T(128)S(1)}, s32[2]{0:T(128)}, u32[]{:S(2)}) copy-start(s32[2]{0:T(128)} %param.12) | copy-start | bytes 28
  36.1 4.1 %collective-permute-start.4 = (bf16[128,1536]{1,0:T(8,128)(2,1)S(1)}, bf16[128,1536]{1,0:T(8,128)(2,1)S(1)}, u32[]{:S(2)}, u32[]{:S(2)}) collective-permute-start(bf16[128,1536]{1,0:T(8,128)(2,1)S(1)} %constant_dynamic-update-slice_fusion.2.far), channel_id=1, source_target_pairs={{0,8},{8,0},{1,9},{9,1},{2,10},{10,2},{3,11},{11,3},{4,12},{12,4},... | collective-permute-start | bytes 1179656 | tf_op jit(solution)/shard_map/ppermute | solution.py:321
  39.1 0.7 copy-start.6
  42.6 14.3 %copy-start = (bf16[2,256,1,256]{3,1,2,0:T(8,128)(2,1)S(1)}, bf16[2,256,1,256]{3,1,2,0:T(8,128)(2,1)}, u32[]{:S(2)}) copy-start(bf16[2,256,1,256]{3,1,2,0:T(8,128)(2,1)} %param.9) | copy-start | bytes 786436
  42.6 22.6 %all-to-all-start.1 = ((bf16[64,16,128]{2,1,0:T(8,128)(2,1)}), bf16[64,16,128]{2,1,0:T(8,128)(2,1)S(1)}, u32[]{:S(2)}, u32[]{:S(2)}) async-start(bf16[64,16,128]{2,1,0:T(8,128)(2,1)} %shard_map.87), calls=%async_computation.1 | async-start | bytes 524288 | tf_op jit(solution)/shard_map/all_to_all | solution.py:40
  56.7 0.7 copy-start.2
  80.3 11.2 %all-to-all-start.3 = ((bf16[8,112,128]{2,1,0:T(8,128)(2,1)}), bf16[8,112,128]{2,1,0:T(8,128)(2,1)S(1)}, u32[]{:S(2)}, u32[]{:S(2)}) async-start(bf16[8,112,128]{2,1,0:T(8,128)(2,1)} %shard_map.90), calls=%async_computation.3 | async-start | bytes 458752 | tf_op jit(solution)/shard_map/all_to_all | solution.py:40

commit v4 on v3

--- a/solution.py
+++ b/solution.py
@@ -22,6 +22,7 @@
 FIRST_SEQ = (2 * NY + 6) * NC
 FIRST = 6 * GROUP + 2 * NC
 FIRST_Y = 4
+FIRST_GROUP = 2 * NC
 VMEM_LIMIT = 48 * 1024 * 1024
 SMEM = pl.BlockSpec(memory_space=pltpu.SMEM)
 VMEM = pl.BlockSpec(memory_space=pltpu.VMEM)
@@ -354,7 +355,7 @@
     partial = exchange(project(numbers, blocks, weight, order), ("kv", "x", "core"), FIRST)
     history_part = attend_history(numbers, cache, steps, asked)
     rows = exchange(attend(numbers, partial, cosine, sine, asked, history_part), ("y",), FIRST_Y)
-    packed = exchange(combine(merge_kernel, (GROUP, PACK, HEAD), rows), ("x", "core"))
+    packed = exchange(combine(merge_kernel, (GROUP, PACK, HEAD), rows), ("x", "core"), FIRST_GROUP)
     new_cache = write(numbers, rows, cache)
     attended = combine(finish_kernel, (ALL_Q, HEAD), packed)
     attended = attended.reshape(CONV, QPK, STEPS, HEAD).transpose(0, 2, 1, 3)

time: 92.9 us -> 91.6 us (0.986)
  waiting for transfers between devices: 16.7 us -> 14.2 us
  starting transfers between devices: 47.7 us -> 48.9 us
    all_to_all x3, waiting for transfers between devices: 11.1 us -> 8.58 us  [exchange(): lax.all_to_all(value, names, split_axis=0, concat_axis=0, tiled=True, axi...]
    all_to_all x3, starting transfers between devices: 32.5 us -> 33.7 us  [exchange(): lax.all_to_all(value, names, split_axis=0, concat_axis=0, tiled=True, axi...]
where the time goes in v4:
time: 91.6 us; the launch traced here: 91 us
  starting transfers between devices  48.9 us (53%)
  waiting for transfers between devices  14.2 us (16%)
  blocking collectives  13 us (14%)
  Pallas kernels  8.95 us (10%)
  local copies, waits for them, and re-layouts  3.87 us (4%)
  other arithmetic  1.14 us (1%)
  between operations  1 us (1%)
    all_to_all x3, starting transfers between devices, exchange(): lax.all_to_all(value, names, split_axis=0, concat_axis=0, tiled=True, axi...  33.7 us
    all_to_all x1, blocking collectives, exchange(): lax.all_to_all(value, names, split_axis=0, concat_axis=0, tiled=True, axi...  13 us
    all_to_all x3, waiting for transfers between devices, exchange(): lax.all_to_all(value, names, split_axis=0, concat_axis=0, tiled=True, axi...  8.58 us
    ppermute x1, waiting for transfers between devices, on_device(): lax.ppermute(after, ('x', 'core'), there)  5.6 us
    ppermute x1, starting transfers between devices, on_device(): near_other = lax.ppermute(near, 'core', swap)  4.04 us
    ppermute x1, starting transfers between devices, on_device(): after = lax.ppermute(hidden, ('x', 'core'), there)  3.95 us
    ppermute x1, starting transfers between devices, on_device(): lax.ppermute(after, ('x', 'core'), there)  3.11 us
    unnamed x16, local copies, waits for them, and re-layouts  2.8 us
  transfers between devices with their start and end apart: 8, of which 3 were waited for; matrix products, arithmetic and copies ran while one was open for 2% of the time, Pallas kernels for 4%

profile of v4, /device:TPU:1, one launch (start us, length us, event | category | flops | bytes accessed | tf_op | source)
XLA Modules:
  0.0 91.0 jit_solution(4933699192025636489)
XLA Ops:
  0.6 4.0 %collective-permute-start = (bf16[64,1536]{1,0:T(8,128)(2,1)}, bf16[64,1536]{1,0:T(8,128)(2,1)S(1)}, u32[]{:S(2)}, u32[]{:S(2)}) collective-permute-start(bf16[64,1536]{1,0:T(8,128)(2,1)} %bitcast.23), channel_id=1, source_target_pairs={{0,384},{8,136},{128,0},{136,264},{256,128},{264,392},{384,256},{3... | collective-permute-start | bytes 589832 | tf_op jit(solution)/shard_map/ppermute | solution.py:315
  4.6 0.9 copy-done.1
  5.5 1.0 %shard_map.86 = bf16[64,24,256]{2,1,0:T(8,128)(2,1)} custom-call(bf16[24,2048]{1,0:T(8,128)(2,1)S(1)} %copy-done.1), custom_call_target="tpu_custom_call" | custom-call | flops 1048576 | bytes 1048576 | tf_op jit(solution)/shard_map/pallas_call | solution.py:68
  6.5 13.4 %all-to-all-start = ((bf16[64,24,256]{2,1,0:T(8,128)(2,1)}), bf16[64,24,256]{2,1,0:T(8,128)(2,1)S(1)}, u32[]{:S(2)}, u32[]{:S(2)}) async-start(bf16[64,24,256]{2,1,0:T(8,128)(2,1)} %shard_map.86), calls=%async_computation | async-start | bytes 1572864 | tf_op jit(solution)/shard_map/all_to_all | solution.py:41
  20.3 0.7 copy-done.5
  21.1 2.2 %collective-permute-start.2 = (bf16[64,1536]{1,0:T(8,128)(2,1)S(1)}, bf16[64,1536]{1,0:T(8,128)(2,1)S(1)}, u32[]{:S(2)}, u32[]{:S(2)}) collective-permute-start(bf16[64,1536]{1,0:T(8,128)(2,1)S(1)} %bitcast.25), channel_id=1, source_target_pairs={{0,128},{8,392},{128,256},{136,8},{256,384},{264,136},{384,0},{392... | collective-permute-start | bytes 589832 | tf_op jit(solution)/shard_map/ppermute | solution.py:317
  23.3 3.1 %collective-permute-start.3 = (bf16[64,1536]{1,0:T(8,128)(2,1)S(1)}, bf16[64,1536]{1,0:T(8,128)(2,1)S(1)}, u32[]{:S(2)}, u32[]{:S(2)}) collective-permute-start(bf16[64,1536]{1,0:T(8,128)(2,1)S(1)} %collective-permute-done), channel_id=1, source_target_pairs={{0,384},{8,136},{128,0},{136,264},{256,128},{264,392},{384,256},{3... | collective-permute-start | bytes 589832 | tf_op jit(solution)/shard_map/ppermute | solution.py:319
  26.4 4.0 %collective-permute-start.1 = (bf16[128,1536]{1,0:T(8,128)(2,1)S(1)}, bf16[128,1536]{1,0:T(8,128)(2,1)S(1)}, u32[]{:S(2)}, u32[]{:S(2)}) collective-permute-start(bf16[128,1536]{1,0:T(8,128)(2,1)S(1)} %constant_dynamic-update-slice_fusion.near), channel_id=1, source_target_pairs={{0,8},{8,0},{1,9},{9,1},{2,10},{10,2},{3,11},{11,3},{4,12},{12,4},... | collective-permute-start | bytes 1179656 | tf_op jit(solution)/shard_map/ppermute | solution.py:320
  30.5 5.6 %collective-permute-done.3 = bf16[64,1536]{1,0:T(8,128)(2,1)S(1)} collective-permute-done((bf16[64,1536]{1,0:T(8,128)(2,1)S(1)}, bf16[64,1536]{1,0:T(8,128)(2,1)S(1)}, u32[]{:S(2)}, u32[]{:S(2)}) %collective-permute-start.3) | collective-permute-done | bytes 196640 | tf_op jit(solution)/shard_map/ppermute | solution.py:319
  36.1 1.9 %collective-permute-start.4 = (bf16[128,1536]{1,0:T(8,128)(2,1)S(1)}, bf16[128,1536]{1,0:T(8,128)(2,1)S(1)}, u32[]{:S(2)}, u32[]{:S(2)}) collective-permute-start(bf16[128,1536]{1,0:T(8,128)(2,1)S(1)} %constant_dynamic-update-slice_fusion.2.far), channel_id=1, source_target_pairs={{0,8},{8,0},{1,9},{9,1},{2,10},{10,2},{3,11},{11,3},{4,12},{12,4},... | collective-permute-start | bytes 1179656 | tf_op jit(solution)/shard_map/ppermute | solution.py:322
  39.2 0.7 copy-done.6
  40.2 2.3 %shard_map.87 = bf16[64,16,128]{2,1,0:T(8,128)(2,1)} custom-call(s32[8]{0:T(128)S(1)} %concatenate.16.numbers, bf16[128,1536]{1,0:T(8,128)(2,1)S(1)} %constant_dynamic-update-slice_fusion.near, bf16[128,1536]{1,0:T(8,128)(2,1)S(1)} %collective-permute-done.1.near_other, bf16[128,1536]{1,0:T(8,128)(2,1)S(1)} %constant_dynamic-update-slice_fusion.2.far, ...), custom_call_target="tpu_custom_call" | custom-call | flops 402653184 | bytes 3145728 | tf_op jit(solution)/shard_map/pallas_call | solution.py:100
  42.6 14.1 %all-to-all-start.1 = ((bf16[64,16,128]{2,1,0:T(8,128)(2,1)}), bf16[64,16,128]{2,1,0:T(8,128)(2,1)S(1)}, u32[]{:S(2)}, u32[]{:S(2)}) async-start(bf16[64,16,128]{2,1,0:T(8,128)(2,1)} %shard_map.87), calls=%async_computation.1 | async-start | bytes 524288 | tf_op jit(solution)/shard_map/all_to_all | solution.py:41
  56.9 0.5 copy-done.2
  57.4 1.1 %shard_map.88 = (f32[96,128]{1,0:T(8,128)S(1)}, f32[96,128]{1,0:T(8,128)S(1)}, f32[96,128]{1,0:T(8,128)S(1)}) custom-call(s32[8]{0:T(128)S(1)} %concatenate.16.numbers, bf16[2,256,256]{2,1,0:T(8,128)(2,1)S(1)} %bitcast.18, bf16[2,16,256]{2,1,0:T(8,128)(2,1)S(1)} %pad.4.step_kv, bf16[2,48,128]{2,1,0:T(8,128)(2,1)S(1)} %bitcast.20), custom_call_target="tpu_custom_call" | custom-call | flops 12582912 | bytes 1048576 | tf_op jit(solution)/shard_map/pallas_call | solution.py:184
  58.5 0.2 fusion.4
  58.8 6.3 %all-to-all-done.1.arrived = bf16[64,16,128]{2,1,0:T(8,128)(2,1)S(1)} async-done(((bf16[64,16,128]{2,1,0:T(8,128)(2,1)}), bf16[64,16,128]{2,1,0:T(8,128)(2,1)S(1)}, u32[]{:S(2)}, u32[]{:S(2)}) %all-to-all-start.1) | async-done | bytes 262176 | tf_op jit(solution)/shard_map/all_to_all | solution.py:41
  65.2 1.2 %shard_map.89 = bf16[8,128,128]{2,1,0:T(8,128)(2,1)S(1)} custom-call(s32[8]{0:T(128)S(1)} %concatenate.16.numbers, bf16[64,16,128]{2,1,0:T(8,128)(2,1)S(1)} %all-to-all-done.1.arrived, f32[64,128]{1,0:T(8,128)S(1)} %get-tuple-element.31.cosine, f32[64,128]{1,0:T(8,128)S(1)} %get-tuple-element.32.sine, bf16[2,48,128]{2,1,0:T(8,128)(2,1)S(1)} %bitcast.21, ...), custom_call_target="tpu_custom_call" | custom-call | flops 3145728 | bytes 1048576 | tf_op jit(solution)/shard_map/pallas_call | solution.py:239
  66.4 13.0 %all_to_all.20.arrived = bf16[8,128,128]{2,1,0:T(8,128)(2,1)S(1)} all-to-all(bf16[8,128,128]{2,1,0:T(8,128)(2,1)S(1)} %shard_map.89), channel_id=1, replica_groups={{64,80,96,112,0,16,32,48},{65,81,97,113,1,17,33,49},{66,82,98,114,2,18,..., dimensions={0} | all-to-all | bytes 524288 | tf_op jit(solution)/shard_map/all_to_all | solution.py:41
  79.3 0.9 %shard_map.90 = bf16[8,112,128]{2,1,0:T(8,128)(2,1)} custom-call(bf16[8,128,128]{2,1,0:T(8,128)(2,1)S(1)} %all_to_all.20.arrived), custom_call_target="tpu_custom_call" | custom-call | flops 458752 | bytes 524288 | tf_op jit(solution)/shard_map/pallas_call | solution.py:263
  80.3 6.2 %all-to-all-start.3 = ((bf16[8,112,128]{2,1,0:T(8,128)(2,1)}), bf16[8,112,128]{2,1,0:T(8,128)(2,1)S(1)}, u32[]{:S(2)}, u32[]{:S(2)}) async-start(bf16[8,112,128]{2,1,0:T(8,128)(2,1)} %shard_map.90), calls=%async_computation.3 | async-start | bytes 458752 | tf_op jit(solution)/shard_map/all_to_all | solution.py:41
  86.4 1.5 %shard_map.92 = bf16[2,256,256]{2,1,0:T(8,128)(2,1)} custom-call(s32[8]{0:T(128)S(1)} %concatenate.16.numbers, bf16[8,128,128]{2,1,0:T(8,128)(2,1)S(1)} %all_to_all.20.arrived, bf16[2,256,256]{2,1,0:T(8,128)(2,1)S(1)} %bitcast.19), custom_call_target="tpu_custom_call" | custom-call | flops 67108864 | bytes 1048576 | tf_op jit(solution)/shard_map/pallas_call | solution.py:292
  87.9 2.3 %all-to-all-done.3.arrived = bf16[8,112,128]{2,1,0:T(8,128)(2,1)S(1)} async-done(((bf16[8,112,128]{2,1,0:T(8,128)(2,1)}), bf16[8,112,128]{2,1,0:T(8,128)(2,1)S(1)}, u32[]{:S(2)}, u32[]{:S(2)}) %all-to-all-start.3) | async-done | bytes 229408 | tf_op jit(solution)/shard_map/all_to_all | solution.py:41
  90.1 0.8 shard_map.91
  (46 shorter events, 2.1 us)
Async XLA Ops:
  0.6 20.5 %collective-permute-start = (bf16[64,1536]{1,0:T(8,128)(2,1)}, bf16[64,1536]{1,0:T(8,128)(2,1)S(1)}, u32[]{:S(2)}, u32[]{:S(2)}) collective-permute-start(bf16[64,1536]{1,0:T(8,128)(2,1)} %bitcast.23), channel_id=1, source_target_pairs={{0,384},{8,136},{128,0},{136,264},{256,128},{264,392},{384,256},{3... | collective-permute-start | bytes 589832 | tf_op jit(solution)/shard_map/ppermute | solution.py:315
  4.6 0.9 copy-start.1
  6.5 33.7 %all-to-all-start = ((bf16[64,24,256]{2,1,0:T(8,128)(2,1)}), bf16[64,24,256]{2,1,0:T(8,128)(2,1)S(1)}, u32[]{:S(2)}, u32[]{:S(2)}) async-start(bf16[64,24,256]{2,1,0:T(8,128)(2,1)} %shard_map.86), calls=%async_computation | async-start | bytes 1572864 | tf_op jit(solution)/shard_map/all_to_all | solution.py:41
  20.0 1.1 %copy-start.3 = (bf16[2,32,1536]{2,1,0:T(8,128)(2,1)S(1)}, bf16[2,32,1536]{2,1,0:T(8,128)(2,1)}, u32[]{:S(2)}) copy-start(bf16[2,32,1536]{2,1,0:T(8,128)(2,1)} %param.7) | copy-start | bytes 589828
  20.3 0.7 copy-start.5
  21.1 9.4 %collective-permute-start.2 = (bf16[64,1536]{1,0:T(8,128)(2,1)S(1)}, bf16[64,1536]{1,0:T(8,128)(2,1)S(1)}, u32[]{:S(2)}, u32[]{:S(2)}) collective-permute-start(bf16[64,1536]{1,0:T(8,128)(2,1)S(1)} %bitcast.25), channel_id=1, source_target_pairs={{0,128},{8,392},{128,256},{136,8},{256,384},{264,136},{384,0},{392... | collective-permute-start | bytes 589832 | tf_op jit(solution)/shard_map/ppermute | solution.py:317
  23.3 12.8 %collective-permute-start.3 = (bf16[64,1536]{1,0:T(8,128)(2,1)S(1)}, bf16[64,1536]{1,0:T(8,128)(2,1)S(1)}, u32[]{:S(2)}, u32[]{:S(2)}) collective-permute-start(bf16[64,1536]{1,0:T(8,128)(2,1)S(1)} %collective-permute-done), channel_id=1, source_target_pairs={{0,384},{8,136},{128,0},{136,264},{256,128},{264,392},{384,256},{3... | collective-permute-start | bytes 589832 | tf_op jit(solution)/shard_map/ppermute | solution.py:319
  26.4 11.6 %collective-permute-start.1 = (bf16[128,1536]{1,0:T(8,128)(2,1)S(1)}, bf16[128,1536]{1,0:T(8,128)(2,1)S(1)}, u32[]{:S(2)}, u32[]{:S(2)}) collective-permute-start(bf16[128,1536]{1,0:T(8,128)(2,1)S(1)} %constant_dynamic-update-slice_fusion.near), channel_id=1, source_target_pairs={{0,8},{8,0},{1,9},{9,1},{2,10},{10,2},{3,11},{11,3},{4,12},{12,4},... | collective-permute-start | bytes 1179656 | tf_op jit(solution)/shard_map/ppermute | solution.py:320
  30.5 7.6 %copy-start.4 = (s32[2]{0:T(128)S(1)}, s32[2]{0:T(128)}, u32[]{:S(2)}) copy-start(s32[2]{0:T(128)} %param.12) | copy-start | bytes 28
  36.1 4.1 %collective-permute-start.4 = (bf16[128,1536]{1,0:T(8,128)(2,1)S(1)}, bf16[128,1536]{1,0:T(8,128)(2,1)S(1)}, u32[]{:S(2)}, u32[]{:S(2)}) collective-permute-start(bf16[128,1536]{1,0:T(8,128)(2,1)S(1)} %constant_dynamic-update-slice_fusion.2.far), channel_id=1, source_target_pairs={{0,8},{8,0},{1,9},{9,1},{2,10},{10,2},{3,11},{11,3},{4,12},{12,4},... | collective-permute-start | bytes 1179656 | tf_op jit(solution)/shard_map/ppermute | solution.py:322
  39.1 0.7 copy-start.6
  42.6 14.3 %copy-start = (bf16[2,256,1,256]{3,1,2,0:T(8,128)(2,1)S(1)}, bf16[2,256,1,256]{3,1,2,0:T(8,128)(2,1)}, u32[]{:S(2)}) copy-start(bf16[2,256,1,256]{3,1,2,0:T(8,128)(2,1)} %param.9) | copy-start | bytes 786436
  42.6 22.6 %all-to-all-start.1 = ((bf16[64,16,128]{2,1,0:T(8,128)(2,1)}), bf16[64,16,128]{2,1,0:T(8,128)(2,1)S(1)}, u32[]{:S(2)}, u32[]{:S(2)}) async-start(bf16[64,16,128]{2,1,0:T(8,128)(2,1)} %shard_map.87), calls=%async_computation.1 | async-start | bytes 524288 | tf_op jit(solution)/shard_map/all_to_all | solution.py:41
  56.7 0.7 copy-start.2
  80.3 9.9 %all-to-all-start.3 = ((bf16[8,112,128]{2,1,0:T(8,128)(2,1)}), bf16[8,112,128]{2,1,0:T(8,128)(2,1)S(1)}, u32[]{:S(2)}, u32[]{:S(2)}) async-start(bf16[8,112,128]{2,1,0:T(8,128)(2,1)} %shard_map.90), calls=%async_computation.3 | async-start | bytes 458752 | tf_op jit(solution)/shard_map/all_to_all | solution.py:41

commit v5 on v4

--- a/solution.py
+++ b/solution.py
@@ -79,15 +79,19 @@
     start = (SEQ - FIRST_SEQ) * (WIDTH // SEQ)
     weights = jnp.concatenate([weight[start:], weight[:start]], axis=0)
     partial = jnp.dot(rows, weights, preferred_element_type=jnp.float32).astype(jnp.bfloat16)
-    ordered = jnp.dot(order[...], partial, preferred_element_type=jnp.float32)
+    half_rows = ROWS // 2
+    halves = [
+        jnp.dot(order[start : start + half_rows], partial, preferred_element_type=jnp.float32)
+        for start in (0, half_rows)
+    ]
     own = numbers[6]
     group = lane_group(16)
     for owner in range(GROUP):
         for half in range(2):
             turned = []
             for part in range(4):
-                start = owner * SLICE + part * 16
-                tile = ordered[start : start + 16, half * HEAD : half * HEAD + HEAD]
+                start = owner % (GROUP // 2) * SLICE + part * 16
+                tile = halves[owner // (GROUP // 2)][start : start + 16, half * HEAD : half * HEAD + HEAD]
                 turned.append(pltpu.roll(tile, part * PIECE, 1) if part else tile)
             for head in range(4 * half, 4 * half + 4):
                 message = turned[0]
@@ -352,8 +356,11 @@
     steps = jnp.pad(step_kv.reshape(CONV, STEPS, FEATURE), ((0, 0), (0, 16 - STEPS), (0, 0)))
     cache = kv_cache.reshape(CONV, LOCAL, FEATURE)
 
+    history_part = attend_history(numbers, cache, steps, asked)
+    order, cosine, sine, asked, history_part = lax.optimization_barrier(
+        (order, cosine, sine, asked, history_part)
+    )
     partial = exchange(project(numbers, blocks, weight, order), ("kv", "x", "core"), FIRST)
-    history_part = attend_history(numbers, cache, steps, asked)
     rows = exchange(attend(numbers, partial, cosine, sine, asked, history_part), ("y",), FIRST_Y)
     packed = exchange(combine(merge_kernel, (GROUP, PACK, HEAD), rows), ("x", "core"), FIRST_GROUP)
     new_cache = write(numbers, rows, cache)

time: 91.6 us -> 92.2 us (level)
  blocking collectives: 13 us -> 35.2 us
  starting transfers between devices: 48.9 us -> 34.8 us
  waiting for transfers between devices: 14.2 us -> 7.87 us
    all_to_all x1 -> x2, blocking collectives: 13 us -> 35.2 us  [exchange(): lax.all_to_all(value, names, split_axis=0, concat_axis=0, tiled=True, axi...]
    all_to_all x3 -> x2, starting transfers between devices: 33.7 us -> 19.6 us  [exchange(): lax.all_to_all(value, names, split_axis=0, concat_axis=0, tiled=True, axi...]
    all_to_all x3 -> x2, waiting for transfers between devices: 8.58 us -> 2.26 us  [exchange(): lax.all_to_all(value, names, split_axis=0, concat_axis=0, tiled=True, axi...]
  transfers between devices with their start and end apart: 8 -> 7, of which waited for: 3 -> 2; matrix products, arithmetic and copies ran while one was open for 2% -> 2% of each run, Pallas kernels for 4% -> 4%
where the time goes in v5:
time: 92.2 us; the launch traced here: 91.6 us
  blocking collectives  35.2 us (38%)
  starting transfers between devices  34.8 us (38%)
  Pallas kernels  8.23 us (9%)
  waiting for transfers between devices  7.87 us (9%)
  local copies, waits for them, and re-layouts  3.32 us (4%)
  other arithmetic  1.14 us (1%)
  between operations  1 us (1%)
    all_to_all x2, blocking collectives, exchange(): lax.all_to_all(value, names, split_axis=0, concat_axis=0, tiled=True, axi...  35.2 us
    all_to_all x2, starting transfers between devices, exchange(): lax.all_to_all(value, names, split_axis=0, concat_axis=0, tiled=True, axi...  19.6 us
    ppermute x1, waiting for transfers between devices, on_device(): lax.ppermute(after, ('x', 'core'), there)  5.6 us
    ppermute x1, starting transfers between devices, on_device(): near_other = lax.ppermute(near, 'core', swap)  4.04 us
    ppermute x1, starting transfers between devices, on_device(): after = lax.ppermute(hidden, ('x', 'core'), there)  3.95 us
    ppermute x1, starting transfers between devices, on_device(): lax.ppermute(after, ('x', 'core'), there)  3.11 us
    all_to_all x2, waiting for transfers between devices, exchange(): lax.all_to_all(value, names, split_axis=0, concat_axis=0, tiled=True, axi...  2.26 us
    unnamed x16, local copies, waits for them, and re-layouts  2.23 us
  transfers between devices with their start and end apart: 7, of which 2 were waited for; matrix products, arithmetic and copies ran while one was open for 2% of the time, Pallas kernels for 4%

profile of v5, /device:TPU:1, one launch (start us, length us, event | category | flops | bytes accessed | tf_op | source)
XLA Modules:
  0.0 91.6 jit_solution(13177711818947905066)
XLA Ops:
  0.6 4.0 %collective-permute-start = (bf16[64,1536]{1,0:T(8,128)(2,1)}, bf16[64,1536]{1,0:T(8,128)(2,1)S(1)}, u32[]{:S(2)}, u32[]{:S(2)}) collective-permute-start(bf16[64,1536]{1,0:T(8,128)(2,1)} %bitcast.23), channel_id=1, source_target_pairs={{0,384},{8,136},{128,0},{136,264},{256,128},{264,392},{384,256},{3... | collective-permute-start | bytes 589832 | tf_op jit(solution)/shard_map/ppermute | solution.py:319
  4.6 0.9 copy-done.1
  5.5 1.0 %shard_map.86 = bf16[64,24,256]{2,1,0:T(8,128)(2,1)} custom-call(bf16[24,2048]{1,0:T(8,128)(2,1)S(1)} %copy-done.1), custom_call_target="tpu_custom_call" | custom-call | flops 1048576 | bytes 1048576 | tf_op jit(solution)/shard_map/pallas_call | solution.py:68
  6.5 13.4 %all-to-all-start = ((bf16[64,24,256]{2,1,0:T(8,128)(2,1)}), bf16[64,24,256]{2,1,0:T(8,128)(2,1)S(1)}, u32[]{:S(2)}, u32[]{:S(2)}) async-start(bf16[64,24,256]{2,1,0:T(8,128)(2,1)} %shard_map.86), calls=%async_computation | async-start | bytes 1572864 | tf_op jit(solution)/shard_map/all_to_all | solution.py:41
  20.3 0.7 copy-done.5
  21.1 2.2 %collective-permute-start.2 = (bf16[64,1536]{1,0:T(8,128)(2,1)S(1)}, bf16[64,1536]{1,0:T(8,128)(2,1)S(1)}, u32[]{:S(2)}, u32[]{:S(2)}) collective-permute-start(bf16[64,1536]{1,0:T(8,128)(2,1)S(1)} %bitcast.25), channel_id=1, source_target_pairs={{0,128},{8,392},{128,256},{136,8},{256,384},{264,136},{384,0},{392... | collective-permute-start | bytes 589832 | tf_op jit(solution)/shard_map/ppermute | solution.py:321
  23.3 3.1 %collective-permute-start.3 = (bf16[64,1536]{1,0:T(8,128)(2,1)S(1)}, bf16[64,1536]{1,0:T(8,128)(2,1)S(1)}, u32[]{:S(2)}, u32[]{:S(2)}) collective-permute-start(bf16[64,1536]{1,0:T(8,128)(2,1)S(1)} %collective-permute-done), channel_id=1, source_target_pairs={{0,384},{8,136},{128,0},{136,264},{256,128},{264,392},{384,256},{3... | collective-permute-start | bytes 589832 | tf_op jit(solution)/shard_map/ppermute | solution.py:323
  26.4 4.0 %collective-permute-start.1 = (bf16[128,1536]{1,0:T(8,128)(2,1)S(1)}, bf16[128,1536]{1,0:T(8,128)(2,1)S(1)}, u32[]{:S(2)}, u32[]{:S(2)}) collective-permute-start(bf16[128,1536]{1,0:T(8,128)(2,1)S(1)} %constant_dynamic-update-slice_fusion.near), channel_id=1, source_target_pairs={{0,8},{8,0},{1,9},{9,1},{2,10},{10,2},{3,11},{11,3},{4,12},{12,4},... | collective-permute-start | bytes 1179656 | tf_op jit(solution)/shard_map/ppermute | solution.py:324
  30.5 5.6 %collective-permute-done.3 = bf16[64,1536]{1,0:T(8,128)(2,1)S(1)} collective-permute-done((bf16[64,1536]{1,0:T(8,128)(2,1)S(1)}, bf16[64,1536]{1,0:T(8,128)(2,1)S(1)}, u32[]{:S(2)}, u32[]{:S(2)}) %collective-permute-start.3) | collective-permute-done | bytes 196640 | tf_op jit(solution)/shard_map/ppermute | solution.py:323
  36.1 1.9 %collective-permute-start.4 = (bf16[128,1536]{1,0:T(8,128)(2,1)S(1)}, bf16[128,1536]{1,0:T(8,128)(2,1)S(1)}, u32[]{:S(2)}, u32[]{:S(2)}) collective-permute-start(bf16[128,1536]{1,0:T(8,128)(2,1)S(1)} %constant_dynamic-update-slice_fusion.2.far), channel_id=1, source_target_pairs={{0,8},{8,0},{1,9},{9,1},{2,10},{10,2},{3,11},{11,3},{4,12},{12,4},... | collective-permute-start | bytes 1179656 | tf_op jit(solution)/shard_map/ppermute | solution.py:326
  39.5 0.2 fusion.4
  39.7 0.4 copy-done.6
  40.2 0.2 copy-done.2
  40.4 1.1 %shard_map.87 = (f32[96,128]{1,0:T(8,128)S(1)}, f32[96,128]{1,0:T(8,128)S(1)}, f32[96,128]{1,0:T(8,128)S(1)}) custom-call(s32[8]{0:T(128)S(1)} %concatenate.16.numbers, bf16[2,256,256]{2,1,0:T(8,128)(2,1)S(1)} %bitcast.18, bf16[2,16,256]{2,1,0:T(8,128)(2,1)S(1)} %pad.4.step_kv, bf16[2,48,128]{2,1,0:T(8,128)(2,1)S(1)} %bitcast.20), custom_call_target="tpu_custom_call" | custom-call | flops 12582912 | bytes 1048576 | tf_op jit(solution)/shard_map/pallas_call | solution.py:188
  41.7 0.2 fusion.order
  41.8 1.6 %shard_map.88 = bf16[64,16,128]{2,1,0:T(8,128)(2,1)S(1)} custom-call(s32[8]{0:T(128)S(1)} %concatenate.16.numbers, bf16[128,1536]{1,0:T(8,128)(2,1)S(1)} %constant_dynamic-update-slice_fusion.near, bf16[128,1536]{1,0:T(8,128)(2,1)S(1)} %collective-permute-done.1.near_other, bf16[128,1536]{1,0:T(8,128)(2,1)S(1)} %constant_dynamic-update-slice_fusion.2.far, ...), custom_call_target="tpu_custom_call" | custom-call | flops 402653184 | bytes 3145728 | tf_op jit(solution)/shard_map/pallas_call | solution.py:104
  43.5 22.3 %all_to_all.20.arrived = bf16[64,16,128]{2,1,0:T(8,128)(2,1)S(1)} all-to-all(bf16[64,16,128]{2,1,0:T(8,128)(2,1)S(1)} %shard_map.88), channel_id=1, replica_groups={{262,270,390,398,7,15,135,143,263,271,391,399,0,8,128,136,256,264,384,3..., dimensions={0} | all-to-all | bytes 524288 | tf_op jit(solution)/shard_map/all_to_all | solution.py:41
  65.7 1.2 %shard_map.89 = bf16[8,128,128]{2,1,0:T(8,128)(2,1)S(1)} custom-call(s32[8]{0:T(128)S(1)} %concatenate.16.numbers, bf16[64,16,128]{2,1,0:T(8,128)(2,1)S(1)} %all_to_all.20.arrived, f32[64,128]{1,0:T(8,128)S(1)} %get-tuple-element.26.cosine, f32[64,128]{1,0:T(8,128)S(1)} %get-tuple-element.27.sine, bf16[2,48,128]{2,1,0:T(8,128)(2,1)S(1)} %bitcast.21, ...), custom_call_target="tpu_custom_call" | custom-call | flops 3145728 | bytes 1048576 | tf_op jit(solution)/shard_map/pallas_call | solution.py:243
  67.0 13.0 %all_to_all.21.arrived = bf16[8,128,128]{2,1,0:T(8,128)(2,1)S(1)} all-to-all(bf16[8,128,128]{2,1,0:T(8,128)(2,1)S(1)} %shard_map.89), channel_id=1, replica_groups={{64,80,96,112,0,16,32,48},{65,81,97,113,1,17,33,49},{66,82,98,114,2,18,..., dimensions={0} | all-to-all | bytes 524288 | tf_op jit(solution)/shard_map/all_to_all | solution.py:41
  79.9 0.9 shard_map.90
  80.8 6.2 %all-to-all-start.3 = ((bf16[8,112,128]{2,1,0:T(8,128)(2,1)}), bf16[8,112,128]{2,1,0:T(8,128)(2,1)S(1)}, u32[]{:S(2)}, u32[]{:S(2)}) async-start(bf16[8,112,128]{2,1,0:T(8,128)(2,1)} %shard_map.90), calls=%async_computation.3 | async-start | bytes 458752 | tf_op jit(solution)/shard_map/all_to_all | solution.py:41
  87.0 1.5 %shard_map.92 = bf16[2,256,256]{2,1,0:T(8,128)(2,1)} custom-call(s32[8]{0:T(128)S(1)} %concatenate.16.numbers, bf16[8,128,128]{2,1,0:T(8,128)(2,1)S(1)} %all_to_all.21.arrived, bf16[2,256,256]{2,1,0:T(8,128)(2,1)S(1)} %bitcast.19), custom_call_target="tpu_custom_call" | custom-call | flops 67108864 | bytes 1048576 | tf_op jit(solution)/shard_map/pallas_call | solution.py:296
  88.5 2.3 %all-to-all-done.3.arrived = bf16[8,112,128]{2,1,0:T(8,128)(2,1)S(1)} async-done(((bf16[8,112,128]{2,1,0:T(8,128)(2,1)}), bf16[8,112,128]{2,1,0:T(8,128)(2,1)S(1)}, u32[]{:S(2)}, u32[]{:S(2)}) %all-to-all-start.3) | async-done | bytes 229408 | tf_op jit(solution)/shard_map/all_to_all | solution.py:41
  90.7 0.8 shard_map.91
  (45 shorter events, 2.0 us)
Async XLA Ops:
  0.6 20.4 %collective-permute-start = (bf16[64,1536]{1,0:T(8,128)(2,1)}, bf16[64,1536]{1,0:T(8,128)(2,1)S(1)}, u32[]{:S(2)}, u32[]{:S(2)}) collective-permute-start(bf16[64,1536]{1,0:T(8,128)(2,1)} %bitcast.23), channel_id=1, source_target_pairs={{0,384},{8,136},{128,0},{136,264},{256,128},{264,392},{384,256},{3... | collective-permute-start | bytes 589832 | tf_op jit(solution)/shard_map/ppermute | solution.py:319
  4.6 0.9 copy-start.1
  6.5 35.3 %all-to-all-start = ((bf16[64,24,256]{2,1,0:T(8,128)(2,1)}), bf16[64,24,256]{2,1,0:T(8,128)(2,1)S(1)}, u32[]{:S(2)}, u32[]{:S(2)}) async-start(bf16[64,24,256]{2,1,0:T(8,128)(2,1)} %shard_map.86), calls=%async_computation | async-start | bytes 1572864 | tf_op jit(solution)/shard_map/all_to_all | solution.py:41
  20.0 1.1 %copy-start.3 = (bf16[2,32,1536]{2,1,0:T(8,128)(2,1)S(1)}, bf16[2,32,1536]{2,1,0:T(8,128)(2,1)}, u32[]{:S(2)}) copy-start(bf16[2,32,1536]{2,1,0:T(8,128)(2,1)} %param.7) | copy-start | bytes 589828
  20.3 0.7 copy-start.5
  21.1 9.4 %collective-permute-start.2 = (bf16[64,1536]{1,0:T(8,128)(2,1)S(1)}, bf16[64,1536]{1,0:T(8,128)(2,1)S(1)}, u32[]{:S(2)}, u32[]{:S(2)}) collective-permute-start(bf16[64,1536]{1,0:T(8,128)(2,1)S(1)} %bitcast.25), channel_id=1, source_target_pairs={{0,128},{8,392},{128,256},{136,8},{256,384},{264,136},{384,0},{392... | collective-permute-start | bytes 589832 | tf_op jit(solution)/shard_map/ppermute | solution.py:321
  23.3 12.8 %collective-permute-start.3 = (bf16[64,1536]{1,0:T(8,128)(2,1)S(1)}, bf16[64,1536]{1,0:T(8,128)(2,1)S(1)}, u32[]{:S(2)}, u32[]{:S(2)}) collective-permute-start(bf16[64,1536]{1,0:T(8,128)(2,1)S(1)} %collective-permute-done), channel_id=1, source_target_pairs={{0,384},{8,136},{128,0},{136,264},{256,128},{264,392},{384,256},{3... | collective-permute-start | bytes 589832 | tf_op jit(solution)/shard_map/ppermute | solution.py:323
  26.4 11.6 %collective-permute-start.1 = (bf16[128,1536]{1,0:T(8,128)(2,1)S(1)}, bf16[128,1536]{1,0:T(8,128)(2,1)S(1)}, u32[]{:S(2)}, u32[]{:S(2)}) collective-permute-start(bf16[128,1536]{1,0:T(8,128)(2,1)S(1)} %constant_dynamic-update-slice_fusion.near), channel_id=1, source_target_pairs={{0,8},{8,0},{1,9},{9,1},{2,10},{10,2},{3,11},{11,3},{4,12},{12,4},... | collective-permute-start | bytes 1179656 | tf_op jit(solution)/shard_map/ppermute | solution.py:324
  30.5 7.6 %copy-start.4 = (s32[2]{0:T(128)S(1)}, s32[2]{0:T(128)}, u32[]{:S(2)}) copy-start(s32[2]{0:T(128)} %param.12) | copy-start | bytes 28
  36.1 5.7 %collective-permute-start.4 = (bf16[128,1536]{1,0:T(8,128)(2,1)S(1)}, bf16[128,1536]{1,0:T(8,128)(2,1)S(1)}, u32[]{:S(2)}, u32[]{:S(2)}) collective-permute-start(bf16[128,1536]{1,0:T(8,128)(2,1)S(1)} %constant_dynamic-update-slice_fusion.2.far), channel_id=1, source_target_pairs={{0,8},{8,0},{1,9},{9,1},{2,10},{10,2},{3,11},{11,3},{4,12},{12,4},... | collective-permute-start | bytes 1179656 | tf_op jit(solution)/shard_map/ppermute | solution.py:326
  38.5 1.8 %copy-start = (bf16[2,256,1,256]{3,1,2,0:T(8,128)(2,1)S(1)}, bf16[2,256,1,256]{3,1,2,0:T(8,128)(2,1)}, u32[]{:S(2)}) copy-start(bf16[2,256,1,256]{3,1,2,0:T(8,128)(2,1)} %param.9) | copy-start | bytes 786436
  39.5 0.7 copy-start.6
  39.7 0.7 copy-start.2
  80.8 9.9 %all-to-all-start.3 = ((bf16[8,112,128]{2,1,0:T(8,128)(2,1)}), bf16[8,112,128]{2,1,0:T(8,128)(2,1)S(1)}, u32[]{:S(2)}, u32[]{:S(2)}) async-start(bf16[8,112,128]{2,1,0:T(8,128)(2,1)} %shard_map.90), calls=%async_computation.3 | async-start | bytes 458752 | tf_op jit(solution)/shard_map/all_to_all | solution.py:41

commit v6 on v5

--- a/solution.py
+++ b/solution.py
@@ -323,8 +323,13 @@
     far = jnp.concatenate([before, lax.ppermute(after, ("x", "core"), there)], axis=0)
     near_other = lax.ppermute(near, "core", swap)
     near_other, hist_len, new_len = lax.optimization_barrier((near_other, hist_len, new_len))
+    numbers = jnp.concatenate([hist_len, new_len, jnp.stack([t, y, own, z])]).astype(jnp.int32)
+    asked = queries.transpose(0, 2, 1, 3).reshape(CONV, QROWS, HEAD)
+    steps = jnp.pad(step_kv.reshape(CONV, STEPS, FEATURE), ((0, 0), (0, 16 - STEPS), (0, 0)))
+    cache = kv_cache.reshape(CONV, LOCAL, FEATURE)
+    history_part = attend_history(numbers, cache, steps, asked)
+    far, history_part = lax.optimization_barrier((far, history_part))
     blocks = [near, near_other, far, lax.ppermute(far, "core", swap)]
-    numbers = jnp.concatenate([hist_len, new_len, jnp.stack([t, y, own, z])]).astype(jnp.int32)
 
     def axis(size, place):
         shape = [1, 1, 1, 1]
@@ -352,14 +357,7 @@
     cosine = jnp.concatenate([cosine, cosine], axis=1)
     sine = jnp.concatenate([-sine, sine], axis=1)
 
-    asked = queries.transpose(0, 2, 1, 3).reshape(CONV, QROWS, HEAD)
-    steps = jnp.pad(step_kv.reshape(CONV, STEPS, FEATURE), ((0, 0), (0, 16 - STEPS), (0, 0)))
-    cache = kv_cache.reshape(CONV, LOCAL, FEATURE)
-
-    history_part = attend_history(numbers, cache, steps, asked)
-    order, cosine, sine, asked, history_part = lax.optimization_barrier(
-        (order, cosine, sine, asked, history_part)
-    )
+    order, cosine, sine, asked = lax.optimization_barrier((order, cosine, sine, asked))
     partial = exchange(project(numbers, blocks, weight, order), ("kv", "x", "core"), FIRST)
     rows = exchange(attend(numbers, partial, cosine, sine, asked, history_part), ("y",), FIRST_Y)
     packed = exchange(combine(merge_kernel, (GROUP, PACK, HEAD), rows), ("x", "core"), FIRST_GROUP)

time: 92.2 us -> 91.1 us (0.988)
  waiting for transfers between devices: 7.87 us -> 6.78 us
    ppermute x1, waiting for transfers between devices: 5.6 us -> 4.52 us  [on_device(): lax.ppermute(after, ('x', 'core'), there)]
    unnamed x16 -> x15, local copies, waits for them, and re-layouts: 2.23 us -> 2.12 us
where the time goes in v6:
time: 91.1 us; the launch traced here: 90.5 us
  blocking collectives  35.2 us (39%)
  starting transfers between devices  34.9 us (38%)
  Pallas kernels  8.23 us (9%)
  waiting for transfers between devices  6.78 us (7%)
  local copies, waits for them, and re-layouts  3.19 us (4%)
  other arithmetic  1.18 us (1%)
  between operations  0.96 us (1%)
    all_to_all x2, blocking collectives, exchange(): lax.all_to_all(value, names, split_axis=0, concat_axis=0, tiled=True, axi...  35.2 us
    all_to_all x2, starting transfers between devices, exchange(): lax.all_to_all(value, names, split_axis=0, concat_axis=0, tiled=True, axi...  19.7 us
    ppermute x1, waiting for transfers between devices, on_device(): lax.ppermute(after, ('x', 'core'), there)  4.52 us
    ppermute x1, starting transfers between devices, on_device(): near_other = lax.ppermute(near, 'core', swap)  4.04 us
    ppermute x1, starting transfers between devices, on_device(): after = lax.ppermute(hidden, ('x', 'core'), there)  3.95 us
    ppermute x1, starting transfers between devices, on_device(): lax.ppermute(after, ('x', 'core'), there)  3.11 us
    all_to_all x2, waiting for transfers between devices, exchange(): lax.all_to_all(value, names, split_axis=0, concat_axis=0, tiled=True, axi...  2.26 us
    ppermute x1, starting transfers between devices, on_device(): before = lax.ppermute(hidden, ('x', 'core'), back)  2.18 us
  transfers between devices with their start and end apart: 7, of which 2 were waited for; matrix products, arithmetic and copies ran while one was open for 2% of the time, Pallas kernels for 4%

profile of v6, /device:TPU:1, one launch (start us, length us, event | category | flops | bytes accessed | tf_op | source)
XLA Modules:
  0.0 90.5 jit_solution(15636873773675933815)
XLA Ops:
  0.6 4.0 %collective-permute-start = (bf16[64,1536]{1,0:T(8,128)(2,1)}, bf16[64,1536]{1,0:T(8,128)(2,1)S(1)}, u32[]{:S(2)}, u32[]{:S(2)}) collective-permute-start(bf16[64,1536]{1,0:T(8,128)(2,1)} %bitcast.23), channel_id=1, source_target_pairs={{0,384},{8,136},{128,0},{136,264},{256,128},{264,392},{384,256},{3... | collective-permute-start | bytes 589832 | tf_op jit(solution)/shard_map/ppermute | solution.py:319
  4.6 0.9 copy-done.1
  5.5 1.0 %shard_map.87 = bf16[64,24,256]{2,1,0:T(8,128)(2,1)} custom-call(bf16[24,2048]{1,0:T(8,128)(2,1)S(1)} %copy-done.1), custom_call_target="tpu_custom_call" | custom-call | flops 1048576 | bytes 1048576 | tf_op jit(solution)/shard_map/pallas_call | solution.py:68
  6.5 13.6 %all-to-all-start = ((bf16[64,24,256]{2,1,0:T(8,128)(2,1)}), bf16[64,24,256]{2,1,0:T(8,128)(2,1)S(1)}, u32[]{:S(2)}, u32[]{:S(2)}) async-start(bf16[64,24,256]{2,1,0:T(8,128)(2,1)} %shard_map.87), calls=%async_computation | async-start | bytes 1572864 | tf_op jit(solution)/shard_map/all_to_all | solution.py:41
  20.3 2.2 %collective-permute-start.2 = (bf16[64,1536]{1,0:T(8,128)(2,1)S(1)}, bf16[64,1536]{1,0:T(8,128)(2,1)S(1)}, u32[]{:S(2)}, u32[]{:S(2)}) collective-permute-start(bf16[64,1536]{1,0:T(8,128)(2,1)S(1)} %bitcast.25), channel_id=1, source_target_pairs={{0,128},{8,392},{128,256},{136,8},{256,384},{264,136},{384,0},{392... | collective-permute-start | bytes 589832 | tf_op jit(solution)/shard_map/ppermute | solution.py:321
  22.5 3.1 %collective-permute-start.3 = (bf16[64,1536]{1,0:T(8,128)(2,1)S(1)}, bf16[64,1536]{1,0:T(8,128)(2,1)S(1)}, u32[]{:S(2)}, u32[]{:S(2)}) collective-permute-start(bf16[64,1536]{1,0:T(8,128)(2,1)S(1)} %collective-permute-done), channel_id=1, source_target_pairs={{0,384},{8,136},{128,0},{136,264},{256,128},{264,392},{384,256},{3... | collective-permute-start | bytes 589832 | tf_op jit(solution)/shard_map/ppermute | solution.py:323
  25.6 4.0 %collective-permute-start.1 = (bf16[128,1536]{1,0:T(8,128)(2,1)S(1)}, bf16[128,1536]{1,0:T(8,128)(2,1)S(1)}, u32[]{:S(2)}, u32[]{:S(2)}) collective-permute-start(bf16[128,1536]{1,0:T(8,128)(2,1)S(1)} %constant_dynamic-update-slice_fusion.near), channel_id=1, source_target_pairs={{0,8},{8,0},{1,9},{9,1},{2,10},{10,2},{3,11},{11,3},{4,12},{12,4},... | collective-permute-start | bytes 1179656 | tf_op jit(solution)/shard_map/ppermute | solution.py:324
  29.9 0.5 copy-done.5
  30.5 4.5 %collective-permute-done.3 = bf16[64,1536]{1,0:T(8,128)(2,1)S(1)} collective-permute-done((bf16[64,1536]{1,0:T(8,128)(2,1)S(1)}, bf16[64,1536]{1,0:T(8,128)(2,1)S(1)}, u32[]{:S(2)}, u32[]{:S(2)}) %collective-permute-start.3) | collective-permute-done | bytes 196640 | tf_op jit(solution)/shard_map/ppermute | solution.py:323
  35.1 0.6 copy-done.4
  35.8 1.1 %shard_map.86 = (f32[96,128]{1,0:T(8,128)S(1)}, f32[96,128]{1,0:T(8,128)S(1)}, f32[96,128]{1,0:T(8,128)S(1)}) custom-call(s32[8]{0:T(128)S(1)} %concatenate.16.numbers, bf16[2,256,256]{2,1,0:T(8,128)(2,1)S(1)} %bitcast.18, bf16[2,16,256]{2,1,0:T(8,128)(2,1)S(1)} %pad.4.step_kv, bf16[2,48,128]{2,1,0:T(8,128)(2,1)S(1)} %bitcast.20), custom_call_target="tpu_custom_call" | custom-call | flops 12582912 | bytes 1048576 | tf_op jit(solution)/shard_map/pallas_call | solution.py:188
  37.0 1.9 %collective-permute-start.4 = (bf16[128,1536]{1,0:T(8,128)(2,1)S(1)}, bf16[128,1536]{1,0:T(8,128)(2,1)S(1)}, u32[]{:S(2)}, u32[]{:S(2)}) collective-permute-start(bf16[128,1536]{1,0:T(8,128)(2,1)S(1)} %pad_maximum_fusion.far), channel_id=1, source_target_pairs={{0,8},{8,0},{1,9},{9,1},{2,10},{10,2},{3,11},{11,3},{4,12},{12,4},... | collective-permute-start | bytes 1179656 | tf_op jit(solution)/shard_map/ppermute | solution.py:332
  39.7 0.1 add.246
  40.3 0.2 fusion.4
  40.6 0.2 fusion.order
  40.8 1.6 %shard_map.88 = bf16[64,16,128]{2,1,0:T(8,128)(2,1)S(1)} custom-call(s32[8]{0:T(128)S(1)} %concatenate.16.numbers, bf16[128,1536]{1,0:T(8,128)(2,1)S(1)} %constant_dynamic-update-slice_fusion.near, bf16[128,1536]{1,0:T(8,128)(2,1)S(1)} %collective-permute-done.1.near_other, bf16[128,1536]{1,0:T(8,128)(2,1)S(1)} %pad_maximum_fusion.far, ...), custom_call_target="tpu_custom_call" | custom-call | flops 402653184 | bytes 3145728 | tf_op jit(solution)/shard_map/pallas_call | solution.py:104
  42.4 22.2 %all_to_all.20.arrived = bf16[64,16,128]{2,1,0:T(8,128)(2,1)S(1)} all-to-all(bf16[64,16,128]{2,1,0:T(8,128)(2,1)S(1)} %shard_map.88), channel_id=1, replica_groups={{262,270,390,398,7,15,135,143,263,271,391,399,0,8,128,136,256,264,384,3..., dimensions={0} | all-to-all | bytes 524288 | tf_op jit(solution)/shard_map/all_to_all | solution.py:41
  64.7 1.2 %shard_map.89 = bf16[8,128,128]{2,1,0:T(8,128)(2,1)S(1)} custom-call(s32[8]{0:T(128)S(1)} %concatenate.16.numbers, bf16[64,16,128]{2,1,0:T(8,128)(2,1)S(1)} %all_to_all.20.arrived, f32[64,128]{1,0:T(8,128)S(1)} %get-tuple-element.28.cosine, f32[64,128]{1,0:T(8,128)S(1)} %get-tuple-element.29.sine, bf16[2,48,128]{2,1,0:T(8,128)(2,1)S(1)} %bitcast.21, ...), custom_call_target="tpu_custom_call" | custom-call | flops 3145728 | bytes 1048576 | tf_op jit(solution)/shard_map/pallas_call | solution.py:243
  65.9 13.0 %all_to_all.21.arrived = bf16[8,128,128]{2,1,0:T(8,128)(2,1)S(1)} all-to-all(bf16[8,128,128]{2,1,0:T(8,128)(2,1)S(1)} %shard_map.89), channel_id=1, replica_groups={{64,80,96,112,0,16,32,48},{65,81,97,113,1,17,33,49},{66,82,98,114,2,18,..., dimensions={0} | all-to-all | bytes 524288 | tf_op jit(solution)/shard_map/all_to_all | solution.py:41
  78.8 0.9 shard_map.90
  79.7 6.2 %all-to-all-start.3 = ((bf16[8,112,128]{2,1,0:T(8,128)(2,1)}), bf16[8,112,128]{2,1,0:T(8,128)(2,1)S(1)}, u32[]{:S(2)}, u32[]{:S(2)}) async-start(bf16[8,112,128]{2,1,0:T(8,128)(2,1)} %shard_map.90), calls=%async_computation.3 | async-start | bytes 458752 | tf_op jit(solution)/shard_map/all_to_all | solution.py:41
  85.9 1.5 %shard_map.92 = bf16[2,256,256]{2,1,0:T(8,128)(2,1)} custom-call(s32[8]{0:T(128)S(1)} %concatenate.16.numbers, bf16[8,128,128]{2,1,0:T(8,128)(2,1)S(1)} %all_to_all.21.arrived, bf16[2,256,256]{2,1,0:T(8,128)(2,1)S(1)} %bitcast.19), custom_call_target="tpu_custom_call" | custom-call | flops 67108864 | bytes 1048576 | tf_op jit(solution)/shard_map/pallas_call | solution.py:296
  87.4 2.3 %all-to-all-done.3.arrived = bf16[8,112,128]{2,1,0:T(8,128)(2,1)S(1)} async-done(((bf16[8,112,128]{2,1,0:T(8,128)(2,1)}), bf16[8,112,128]{2,1,0:T(8,128)(2,1)S(1)}, u32[]{:S(2)}, u32[]{:S(2)}) %all-to-all-start.3) | async-done | bytes 229408 | tf_op jit(solution)/shard_map/all_to_all | solution.py:41
  89.6 0.8 shard_map.91
  (44 shorter events, 1.8 us)
Async XLA Ops:
  0.6 19.6 %collective-permute-start = (bf16[64,1536]{1,0:T(8,128)(2,1)}, bf16[64,1536]{1,0:T(8,128)(2,1)S(1)}, u32[]{:S(2)}, u32[]{:S(2)}) collective-permute-start(bf16[64,1536]{1,0:T(8,128)(2,1)} %bitcast.23), channel_id=1, source_target_pairs={{0,384},{8,136},{128,0},{136,264},{256,128},{264,392},{384,256},{3... | collective-permute-start | bytes 589832 | tf_op jit(solution)/shard_map/ppermute | solution.py:319
  4.6 0.9 copy-start.1
  6.5 13.8 %copy-start.3 = (bf16[2,32,1536]{2,1,0:T(8,128)(2,1)S(1)}, bf16[2,32,1536]{2,1,0:T(8,128)(2,1)}, u32[]{:S(2)}) copy-start(bf16[2,32,1536]{2,1,0:T(8,128)(2,1)} %param.7) | copy-start | bytes 589828
  6.5 34.2 %all-to-all-start = ((bf16[64,24,256]{2,1,0:T(8,128)(2,1)}), bf16[64,24,256]{2,1,0:T(8,128)(2,1)S(1)}, u32[]{:S(2)}, u32[]{:S(2)}) async-start(bf16[64,24,256]{2,1,0:T(8,128)(2,1)} %shard_map.87), calls=%async_computation | async-start | bytes 1572864 | tf_op jit(solution)/shard_map/all_to_all | solution.py:41
  20.3 14.7 %collective-permute-start.2 = (bf16[64,1536]{1,0:T(8,128)(2,1)S(1)}, bf16[64,1536]{1,0:T(8,128)(2,1)S(1)}, u32[]{:S(2)}, u32[]{:S(2)}) collective-permute-start(bf16[64,1536]{1,0:T(8,128)(2,1)S(1)} %bitcast.25), channel_id=1, source_target_pairs={{0,128},{8,392},{128,256},{136,8},{256,384},{264,136},{384,0},{392... | collective-permute-start | bytes 589832 | tf_op jit(solution)/shard_map/ppermute | solution.py:321
  22.5 12.5 %collective-permute-start.3 = (bf16[64,1536]{1,0:T(8,128)(2,1)S(1)}, bf16[64,1536]{1,0:T(8,128)(2,1)S(1)}, u32[]{:S(2)}, u32[]{:S(2)}) collective-permute-start(bf16[64,1536]{1,0:T(8,128)(2,1)S(1)} %collective-permute-done), channel_id=1, source_target_pairs={{0,384},{8,136},{128,0},{136,264},{256,128},{264,392},{384,256},{3... | collective-permute-start | bytes 589832 | tf_op jit(solution)/shard_map/ppermute | solution.py:323
  25.6 9.4 %collective-permute-start.1 = (bf16[128,1536]{1,0:T(8,128)(2,1)S(1)}, bf16[128,1536]{1,0:T(8,128)(2,1)S(1)}, u32[]{:S(2)}, u32[]{:S(2)}) collective-permute-start(bf16[128,1536]{1,0:T(8,128)(2,1)S(1)} %constant_dynamic-update-slice_fusion.near), channel_id=1, source_target_pairs={{0,8},{8,0},{1,9},{9,1},{2,10},{10,2},{3,11},{11,3},{4,12},{12,4},... | collective-permute-start | bytes 1179656 | tf_op jit(solution)/shard_map/ppermute | solution.py:324
  29.8 0.7 copy-start.5
  30.5 5.3 %copy-start = (bf16[2,256,1,256]{3,1,2,0:T(8,128)(2,1)S(1)}, bf16[2,256,1,256]{3,1,2,0:T(8,128)(2,1)}, u32[]{:S(2)}) copy-start(bf16[2,256,1,256]{3,1,2,0:T(8,128)(2,1)} %param.9) | copy-start | bytes 786436
  35.0 0.8 copy-start.2
  35.1 0.7 copy-start.4
  35.1 0.7 copy-start.6
  37.0 3.8 %collective-permute-start.4 = (bf16[128,1536]{1,0:T(8,128)(2,1)S(1)}, bf16[128,1536]{1,0:T(8,128)(2,1)S(1)}, u32[]{:S(2)}, u32[]{:S(2)}) collective-permute-start(bf16[128,1536]{1,0:T(8,128)(2,1)S(1)} %pad_maximum_fusion.far), channel_id=1, source_target_pairs={{0,8},{8,0},{1,9},{9,1},{2,10},{10,2},{3,11},{11,3},{4,12},{12,4},... | collective-permute-start | bytes 1179656 | tf_op jit(solution)/shard_map/ppermute | solution.py:332
  79.7 9.9 %all-to-all-start.3 = ((bf16[8,112,128]{2,1,0:T(8,128)(2,1)}), bf16[8,112,128]{2,1,0:T(8,128)(2,1)S(1)}, u32[]{:S(2)}, u32[]{:S(2)}) async-start(bf16[8,112,128]{2,1,0:T(8,128)(2,1)} %shard_map.90), calls=%async_computation.3 | async-start | bytes 458752 | tf_op jit(solution)/shard_map/all_to_all | solution.py:41

commit v7 on v6

--- a/solution.py
+++ b/solution.py
@@ -19,10 +19,10 @@
 ALL_Q = CONV * QROWS
 PACK = ALL_Q + 16
 PIECE = 32
-FIRST_SEQ = (2 * NY + 6) * NC
-FIRST = 6 * GROUP + 2 * NC
-FIRST_Y = 4
-FIRST_GROUP = 2 * NC
+SEQ_ORDER = [(2 * NY + 6 + 11 * place) % (NX * NY) * NC + core for place in range(NX * NY) for core in range(NC)]
+SUM_ORDER = [(6 * GROUP + 2 * NC + 11 * place) % (NZ * GROUP) for place in range(NZ * GROUP)]
+Y_ORDER = [(4 + 3 * place) % NY for place in range(NY)]
+GROUP_ORDER = [(2 * NC + place) % GROUP for place in range(GROUP)]
 VMEM_LIMIT = 48 * 1024 * 1024
 SMEM = pl.BlockSpec(memory_space=pltpu.SMEM)
 VMEM = pl.BlockSpec(memory_space=pltpu.VMEM)
@@ -35,10 +35,8 @@
     )
 
 
-def exchange(value, names, first=0):
-    size = value.shape[0]
-    groups = [[(place + first) % size for place in range(size)]] if first else None
-    return lax.all_to_all(value, names, split_axis=0, concat_axis=0, tiled=True, axis_index_groups=groups)
+def exchange(value, names, order):
+    return lax.all_to_all(value, names, split_axis=0, concat_axis=0, tiled=True, axis_index_groups=[order])
 
 
 def lane_group(rows):
@@ -60,7 +58,7 @@
             tiles.append(tile)
         columns = jnp.concatenate(tiles, axis=1).astype(jnp.bfloat16)
         for y in range(NY):
-            out[(c // NC * (NY * NC) + y * NC + c % NC - FIRST_SEQ) % SEQ] = columns
+            out[SEQ_ORDER.index(c // NC * (NY * NC) + y * NC + c % NC)] = columns
 
 
 def split_weight(weight):
@@ -76,8 +74,9 @@
 
 def project_kernel(numbers, near, near_other, far, far_other, weight, order, out):
     rows = jnp.concatenate([near[...], near_other[...], far[...], far_other[...]], axis=0)
-    start = (SEQ - FIRST_SEQ) * (WIDTH // SEQ)
-    weights = jnp.concatenate([weight[start:], weight[:start]], axis=0)
+    run = WIDTH // (NX * NY)
+    starts = [SEQ_ORDER.index(chip * NC) // NC * run for chip in range(NX * NY)]
+    weights = jnp.concatenate([weight[start : start + run] for start in starts], axis=0)
     partial = jnp.dot(rows, weights, preferred_element_type=jnp.float32).astype(jnp.bfloat16)
     half_rows = ROWS // 2
     halves = [
@@ -97,7 +96,7 @@
                 message = turned[0]
                 for part in range(1, 4):
                     message = jnp.where(group == ((own + head + part) & 3), turned[part], message)
-                out[(head * GROUP + owner - FIRST) % (NZ * GROUP)] = message.astype(jnp.bfloat16)
+                out[SUM_ORDER.index(head * GROUP + owner)] = message.astype(jnp.bfloat16)
 
 
 def project(numbers, blocks, weight, order):
@@ -199,9 +198,9 @@
     group = lane_group(16)
     sums = []
     for c in range(GROUP):
-        total = arrived[(c - FIRST) % (NZ * GROUP)].astype(jnp.float32)
+        total = arrived[SUM_ORDER.index(c)].astype(jnp.float32)
         for plane in range(1, NZ):
-            total += arrived[(plane * GROUP + c - FIRST) % (NZ * GROUP)].astype(jnp.float32)
+            total += arrived[SUM_ORDER.index(plane * GROUP + c)].astype(jnp.float32)
         sums.append(total)
     halves = []
     for tile in range(2):
@@ -216,7 +215,7 @@
     key = key * cosine[...] + pltpu.roll(key, HEAD // 2, 1) * sine[...]
     for row in range(NY):
         both = jnp.concatenate([key[row * 8 : row * 8 + 8], value[row * 8 : row * 8 + 8]], axis=0)
-        out[(row - FIRST_Y) % NY, :16] = both.astype(jnp.bfloat16)
+        out[Y_ORDER.index(row), :16] = both.astype(jnp.bfloat16)
     key, value = key.astype(jnp.bfloat16), value.astype(jnp.bfloat16)
 
     asker = lax.broadcasted_iota(jnp.int32, (ALL_Q, SLICE), 0) >= QROWS
@@ -273,7 +272,7 @@
 
 def write_kernel(numbers, arrived, cache, new_cache):
     t = numbers[4]
-    rows = jnp.concatenate([arrived[(row - FIRST_Y) % NY, :16].astype(jnp.float32) for row in range(NY)], axis=0)
+    rows = jnp.concatenate([arrived[Y_ORDER.index(row), :16].astype(jnp.float32) for row in range(NY)], axis=0)
     rows = rows.astype(jnp.bfloat16)
     for conv in range(CONV):
         history, length = numbers[conv], numbers[2 + conv]
@@ -307,7 +306,7 @@
     t = (x * NY + y) * NC + core
     own = x * NC + core
 
-    weight = exchange(split_weight(kv_weight), ("x", "y", "core"), FIRST_SEQ).reshape(WIDTH, FEATURE)
+    weight = exchange(split_weight(kv_weight), ("x", "y", "core"), SEQ_ORDER).reshape(WIDTH, FEATURE)
 
     swap = [(0, 1), (1, 0)]
     there, back = [], []
@@ -358,9 +357,9 @@
     sine = jnp.concatenate([-sine, sine], axis=1)
 
     order, cosine, sine, asked = lax.optimization_barrier((order, cosine, sine, asked))
-    partial = exchange(project(numbers, blocks, weight, order), ("kv", "x", "core"), FIRST)
-    rows = exchange(attend(numbers, partial, cosine, sine, asked, history_part), ("y",), FIRST_Y)
-    packed = exchange(combine(merge_kernel, (GROUP, PACK, HEAD), rows), ("x", "core"), FIRST_GROUP)
+    partial = exchange(project(numbers, blocks, weight, order), ("kv", "x", "core"), SUM_ORDER)
+    rows = exchange(attend(numbers, partial, cosine, sine, asked, history_part), ("y",), Y_ORDER)
+    packed = exchange(combine(merge_kernel, (GROUP, PACK, HEAD), rows), ("x", "core"), GROUP_ORDER)
     new_cache = write(numbers, rows, cache)
     attended = combine(finish_kernel, (ALL_Q, HEAD), packed)
     attended = attended.reshape(CONV, QPK, STEPS, HEAD).transpose(0, 2, 1, 3)

time: 91.1 us -> 91.6 us (level)
  starting transfers between devices: 34.9 us -> 38 us
  blocking collectives: 35.2 us -> 33.4 us
    all_to_all x2, starting transfers between devices: 19.7 us -> 22.8 us  [exchange(): lax.all_to_all(value, names, split_axis=0, concat_axis=0, tiled=True, axi...]
    all_to_all x2, blocking collectives: 35.2 us -> 33.4 us  [exchange(): lax.all_to_all(value, names, split_axis=0, concat_axis=0, tiled=True, axi...]
where the time goes in v7:
time: 91.6 us; the launch traced here: 91 us
  starting transfers between devices  38 us (41%)
  blocking collectives  33.4 us (36%)
  Pallas kernels  8.23 us (9%)
  waiting for transfers between devices  5.97 us (7%)
  local copies, waits for them, and re-layouts  3.19 us (3%)
  other arithmetic  1.18 us (1%)
  between operations  0.96 us (1%)
    all_to_all x2, blocking collectives, exchange(): lax.all_to_all(value, names, split_axis=0, concat_axis=0, tiled=True, axi...  33.4 us
    all_to_all x2, starting transfers between devices, exchange(): lax.all_to_all(value, names, split_axis=0, concat_axis=0, tiled=True, axi...  22.8 us
    ppermute x1, starting transfers between devices, on_device(): near_other = lax.ppermute(near, 'core', swap)  4.04 us
    ppermute x1, starting transfers between devices, on_device(): after = lax.ppermute(hidden, ('x', 'core'), there)  3.95 us
    ppermute x1, waiting for transfers between devices, on_device(): lax.ppermute(after, ('x', 'core'), there)  3.66 us
    ppermute x1, starting transfers between devices, on_device(): lax.ppermute(after, ('x', 'core'), there)  3.36 us
    all_to_all x2, waiting for transfers between devices, exchange(): lax.all_to_all(value, names, split_axis=0, concat_axis=0, tiled=True, axi...  2.3 us
    unnamed x15, local copies, waits for them, and re-layouts  2.12 us
  transfers between devices with their start and end apart: 7, of which 2 were waited for; matrix products, arithmetic and copies ran while one was open for 2% of the time, Pallas kernels for 4%

profile of v7, /device:TPU:1, one launch (start us, length us, event | category | flops | bytes accessed | tf_op | source)
XLA Modules:
  0.0 91.0 jit_solution(3435927945077712973)
XLA Ops:
  0.6 4.0 %collective-permute-start = (bf16[64,1536]{1,0:T(8,128)(2,1)}, bf16[64,1536]{1,0:T(8,128)(2,1)S(1)}, u32[]{:S(2)}, u32[]{:S(2)}) collective-permute-start(bf16[64,1536]{1,0:T(8,128)(2,1)} %bitcast.23), channel_id=1, source_target_pairs={{0,384},{8,136},{128,0},{136,264},{256,128},{264,392},{384,256},{3... | collective-permute-start | bytes 589832 | tf_op jit(solution)/shard_map/ppermute | solution.py:318
  4.6 0.9 copy-done.1
  5.5 1.0 %shard_map.87 = bf16[64,24,256]{2,1,0:T(8,128)(2,1)} custom-call(bf16[24,2048]{1,0:T(8,128)(2,1)S(1)} %copy-done.1), custom_call_target="tpu_custom_call" | custom-call | flops 1048576 | bytes 1048576 | tf_op jit(solution)/shard_map/pallas_call | solution.py:66
  6.5 13.8 %all-to-all-start = ((bf16[64,24,256]{2,1,0:T(8,128)(2,1)}), bf16[64,24,256]{2,1,0:T(8,128)(2,1)S(1)}, u32[]{:S(2)}, u32[]{:S(2)}) async-start(bf16[64,24,256]{2,1,0:T(8,128)(2,1)} %shard_map.87), calls=%async_computation | async-start | bytes 1572864 | tf_op jit(solution)/shard_map/all_to_all | solution.py:39
  20.6 1.9 %collective-permute-start.2 = (bf16[64,1536]{1,0:T(8,128)(2,1)S(1)}, bf16[64,1536]{1,0:T(8,128)(2,1)S(1)}, u32[]{:S(2)}, u32[]{:S(2)}) collective-permute-start(bf16[64,1536]{1,0:T(8,128)(2,1)S(1)} %bitcast.25), channel_id=1, source_target_pairs={{0,128},{8,392},{128,256},{136,8},{256,384},{264,136},{384,0},{392... | collective-permute-start | bytes 589832 | tf_op jit(solution)/shard_map/ppermute | solution.py:320
  22.5 3.4 %collective-permute-start.3 = (bf16[64,1536]{1,0:T(8,128)(2,1)S(1)}, bf16[64,1536]{1,0:T(8,128)(2,1)S(1)}, u32[]{:S(2)}, u32[]{:S(2)}) collective-permute-start(bf16[64,1536]{1,0:T(8,128)(2,1)S(1)} %collective-permute-done), channel_id=1, source_target_pairs={{0,384},{8,136},{128,0},{136,264},{256,128},{264,392},{384,256},{3... | collective-permute-start | bytes 589832 | tf_op jit(solution)/shard_map/ppermute | solution.py:322
  25.9 4.0 %collective-permute-start.1 = (bf16[128,1536]{1,0:T(8,128)(2,1)S(1)}, bf16[128,1536]{1,0:T(8,128)(2,1)S(1)}, u32[]{:S(2)}, u32[]{:S(2)}) collective-permute-start(bf16[128,1536]{1,0:T(8,128)(2,1)S(1)} %constant_dynamic-update-slice_fusion.near), channel_id=1, source_target_pairs={{0,8},{8,0},{1,9},{9,1},{2,10},{10,2},{3,11},{11,3},{4,12},{12,4},... | collective-permute-start | bytes 1179656 | tf_op jit(solution)/shard_map/ppermute | solution.py:323
  30.2 0.5 copy-done.5
  30.8 3.7 %collective-permute-done.3 = bf16[64,1536]{1,0:T(8,128)(2,1)S(1)} collective-permute-done((bf16[64,1536]{1,0:T(8,128)(2,1)S(1)}, bf16[64,1536]{1,0:T(8,128)(2,1)S(1)}, u32[]{:S(2)}, u32[]{:S(2)}) %collective-permute-start.3) | collective-permute-done | bytes 196640 | tf_op jit(solution)/shard_map/ppermute | solution.py:322
  34.5 0.6 copy-done.4
  35.2 1.1 %shard_map.86 = (f32[96,128]{1,0:T(8,128)S(1)}, f32[96,128]{1,0:T(8,128)S(1)}, f32[96,128]{1,0:T(8,128)S(1)}) custom-call(s32[8]{0:T(128)S(1)} %concatenate.16.numbers, bf16[2,256,256]{2,1,0:T(8,128)(2,1)S(1)} %bitcast.18, bf16[2,16,256]{2,1,0:T(8,128)(2,1)S(1)} %pad.4.step_kv, bf16[2,48,128]{2,1,0:T(8,128)(2,1)S(1)} %bitcast.20), custom_call_target="tpu_custom_call" | custom-call | flops 12582912 | bytes 1048576 | tf_op jit(solution)/shard_map/pallas_call | solution.py:187
  36.4 1.9 %collective-permute-start.4 = (bf16[128,1536]{1,0:T(8,128)(2,1)S(1)}, bf16[128,1536]{1,0:T(8,128)(2,1)S(1)}, u32[]{:S(2)}, u32[]{:S(2)}) collective-permute-start(bf16[128,1536]{1,0:T(8,128)(2,1)S(1)} %pad_maximum_fusion.far), channel_id=1, source_target_pairs={{0,8},{8,0},{1,9},{9,1},{2,10},{10,2},{3,11},{11,3},{4,12},{12,4},... | collective-permute-start | bytes 1179656 | tf_op jit(solution)/shard_map/ppermute | solution.py:331
  38.8 0.1 add.253
  39.7 0.2 fusion.4
  40.0 0.2 fusion.order
  40.2 1.6 %shard_map.88 = bf16[64,16,128]{2,1,0:T(8,128)(2,1)S(1)} custom-call(s32[8]{0:T(128)S(1)} %concatenate.16.numbers, bf16[128,1536]{1,0:T(8,128)(2,1)S(1)} %constant_dynamic-update-slice_fusion.near, bf16[128,1536]{1,0:T(8,128)(2,1)S(1)} %collective-permute-done.1.near_other, bf16[128,1536]{1,0:T(8,128)(2,1)S(1)} %pad_maximum_fusion.far, ...), custom_call_target="tpu_custom_call" | custom-call | flops 402653184 | bytes 3145728 | tf_op jit(solution)/shard_map/pallas_call | solution.py:103
  41.8 21.3 %all_to_all.20.arrived = bf16[64,16,128]{2,1,0:T(8,128)(2,1)S(1)} all-to-all(bf16[64,16,128]{2,1,0:T(8,128)(2,1)S(1)} %shard_map.88), channel_id=1, replica_groups={{262,399,129,266,4,141,390,8,257,394,132,269,7,136,385,11,260,397,135,2..., dimensions={0} | all-to-all | bytes 524288 | tf_op jit(solution)/shard_map/all_to_all | solution.py:39
  63.2 1.2 %shard_map.89 = bf16[8,128,128]{2,1,0:T(8,128)(2,1)S(1)} custom-call(s32[8]{0:T(128)S(1)} %concatenate.16.numbers, bf16[64,16,128]{2,1,0:T(8,128)(2,1)S(1)} %all_to_all.20.arrived, f32[64,128]{1,0:T(8,128)S(1)} %get-tuple-element.28.cosine, f32[64,128]{1,0:T(8,128)S(1)} %get-tuple-element.29.sine, bf16[2,48,128]{2,1,0:T(8,128)(2,1)S(1)} %bitcast.21, ...), custom_call_target="tpu_custom_call" | custom-call | flops 3145728 | bytes 1048576 | tf_op jit(solution)/shard_map/pallas_call | solution.py:242
  64.4 12.1 %all_to_all.21.arrived = bf16[8,128,128]{2,1,0:T(8,128)(2,1)S(1)} all-to-all(bf16[8,128,128]{2,1,0:T(8,128)(2,1)S(1)} %shard_map.89), channel_id=1, replica_groups={{64,112,32,80,0,48,96,16},{65,113,33,81,1,49,97,17},{66,114,34,82,2,50,..., dimensions={0} | all-to-all | bytes 524288 | tf_op jit(solution)/shard_map/all_to_all | solution.py:39
  76.4 0.9 shard_map.90
  77.4 9.0 %all-to-all-start.3 = ((bf16[8,112,128]{2,1,0:T(8,128)(2,1)}), bf16[8,112,128]{2,1,0:T(8,128)(2,1)S(1)}, u32[]{:S(2)}, u32[]{:S(2)}) async-start(bf16[8,112,128]{2,1,0:T(8,128)(2,1)} %shard_map.90), calls=%async_computation.3 | async-start | bytes 458752 | tf_op jit(solution)/shard_map/all_to_all | solution.py:39
  86.3 1.5 %shard_map.92 = bf16[2,256,256]{2,1,0:T(8,128)(2,1)} custom-call(s32[8]{0:T(128)S(1)} %concatenate.16.numbers, bf16[8,128,128]{2,1,0:T(8,128)(2,1)S(1)} %all_to_all.21.arrived, bf16[2,256,256]{2,1,0:T(8,128)(2,1)S(1)} %bitcast.19), custom_call_target="tpu_custom_call" | custom-call | flops 67108864 | bytes 1048576 | tf_op jit(solution)/shard_map/pallas_call | solution.py:295
  87.8 2.3 %all-to-all-done.3.arrived = bf16[8,112,128]{2,1,0:T(8,128)(2,1)S(1)} async-done(((bf16[8,112,128]{2,1,0:T(8,128)(2,1)}), bf16[8,112,128]{2,1,0:T(8,128)(2,1)S(1)}, u32[]{:S(2)}, u32[]{:S(2)}) %all-to-all-start.3) | async-done | bytes 229408 | tf_op jit(solution)/shard_map/all_to_all | solution.py:39
  90.1 0.8 shard_map.91
  (44 shorter events, 1.8 us)
Async XLA Ops:
  0.6 19.9 %collective-permute-start = (bf16[64,1536]{1,0:T(8,128)(2,1)}, bf16[64,1536]{1,0:T(8,128)(2,1)S(1)}, u32[]{:S(2)}, u32[]{:S(2)}) collective-permute-start(bf16[64,1536]{1,0:T(8,128)(2,1)} %bitcast.23), channel_id=1, source_target_pairs={{0,384},{8,136},{128,0},{136,264},{256,128},{264,392},{384,256},{3... | collective-permute-start | bytes 589832 | tf_op jit(solution)/shard_map/ppermute | solution.py:318
  4.6 0.9 copy-start.1
  6.5 14.0 %copy-start.3 = (bf16[2,32,1536]{2,1,0:T(8,128)(2,1)S(1)}, bf16[2,32,1536]{2,1,0:T(8,128)(2,1)}, u32[]{:S(2)}) copy-start(bf16[2,32,1536]{2,1,0:T(8,128)(2,1)} %param.7) | copy-start | bytes 589828
  6.5 33.7 %all-to-all-start = ((bf16[64,24,256]{2,1,0:T(8,128)(2,1)}), bf16[64,24,256]{2,1,0:T(8,128)(2,1)S(1)}, u32[]{:S(2)}, u32[]{:S(2)}) async-start(bf16[64,24,256]{2,1,0:T(8,128)(2,1)} %shard_map.87), calls=%async_computation | async-start | bytes 1572864 | tf_op jit(solution)/shard_map/all_to_all | solution.py:39
  20.6 13.9 %collective-permute-start.2 = (bf16[64,1536]{1,0:T(8,128)(2,1)S(1)}, bf16[64,1536]{1,0:T(8,128)(2,1)S(1)}, u32[]{:S(2)}, u32[]{:S(2)}) collective-permute-start(bf16[64,1536]{1,0:T(8,128)(2,1)S(1)} %bitcast.25), channel_id=1, source_target_pairs={{0,128},{8,392},{128,256},{136,8},{256,384},{264,136},{384,0},{392... | collective-permute-start | bytes 589832 | tf_op jit(solution)/shard_map/ppermute | solution.py:320
  22.5 11.9 %collective-permute-start.3 = (bf16[64,1536]{1,0:T(8,128)(2,1)S(1)}, bf16[64,1536]{1,0:T(8,128)(2,1)S(1)}, u32[]{:S(2)}, u32[]{:S(2)}) collective-permute-start(bf16[64,1536]{1,0:T(8,128)(2,1)S(1)} %collective-permute-done), channel_id=1, source_target_pairs={{0,384},{8,136},{128,0},{136,264},{256,128},{264,392},{384,256},{3... | collective-permute-start | bytes 589832 | tf_op jit(solution)/shard_map/ppermute | solution.py:322
  25.9 8.6 %collective-permute-start.1 = (bf16[128,1536]{1,0:T(8,128)(2,1)S(1)}, bf16[128,1536]{1,0:T(8,128)(2,1)S(1)}, u32[]{:S(2)}, u32[]{:S(2)}) collective-permute-start(bf16[128,1536]{1,0:T(8,128)(2,1)S(1)} %constant_dynamic-update-slice_fusion.near), channel_id=1, source_target_pairs={{0,8},{8,0},{1,9},{9,1},{2,10},{10,2},{3,11},{11,3},{4,12},{12,4},... | collective-permute-start | bytes 1179656 | tf_op jit(solution)/shard_map/ppermute | solution.py:323
  30.0 0.7 copy-start.5
  30.8 4.5 %copy-start = (bf16[2,256,1,256]{3,1,2,0:T(8,128)(2,1)S(1)}, bf16[2,256,1,256]{3,1,2,0:T(8,128)(2,1)}, u32[]{:S(2)}) copy-start(bf16[2,256,1,256]{3,1,2,0:T(8,128)(2,1)} %param.9) | copy-start | bytes 786436
  34.4 0.8 copy-start.2
  34.5 0.7 copy-start.4
  34.5 0.7 copy-start.6
  36.4 3.8 %collective-permute-start.4 = (bf16[128,1536]{1,0:T(8,128)(2,1)S(1)}, bf16[128,1536]{1,0:T(8,128)(2,1)S(1)}, u32[]{:S(2)}, u32[]{:S(2)}) collective-permute-start(bf16[128,1536]{1,0:T(8,128)(2,1)S(1)} %pad_maximum_fusion.far), channel_id=1, source_target_pairs={{0,8},{8,0},{1,9},{9,1},{2,10},{10,2},{3,11},{11,3},{4,12},{12,4},... | collective-permute-start | bytes 1179656 | tf_op jit(solution)/shard_map/ppermute | solution.py:331
  77.4 12.8 %all-to-all-start.3 = ((bf16[8,112,128]{2,1,0:T(8,128)(2,1)}), bf16[8,112,128]{2,1,0:T(8,128)(2,1)S(1)}, u32[]{:S(2)}, u32[]{:S(2)}) async-start(bf16[8,112,128]{2,1,0:T(8,128)(2,1)} %shard_map.90), calls=%async_computation.3 | async-start | bytes 458752 | tf_op jit(solution)/shard_map/all_to_all | solution.py:39

commit v8 on v7

--- a/solution.py
+++ b/solution.py
@@ -21,7 +21,7 @@
 PIECE = 32
 SEQ_ORDER = [(2 * NY + 6 + 11 * place) % (NX * NY) * NC + core for place in range(NX * NY) for core in range(NC)]
 SUM_ORDER = [(6 * GROUP + 2 * NC + 11 * place) % (NZ * GROUP) for place in range(NZ * GROUP)]
-Y_ORDER = [(4 + 3 * place) % NY for place in range(NY)]
+Y_ORDER = [(4 + place) % NY for place in range(NY)]
 GROUP_ORDER = [(2 * NC + place) % GROUP for place in range(GROUP)]
 VMEM_LIMIT = 48 * 1024 * 1024
 SMEM = pl.BlockSpec(memory_space=pltpu.SMEM)

time: 91.6 us -> 92 us (level)
  no operation moved by 1% of the time
where the time goes in v8:
time: 92 us; the launch traced here: 91.3 us
  starting transfers between devices  37.5 us (41%)
  blocking collectives  34.3 us (37%)
  Pallas kernels  8.23 us (9%)
  waiting for transfers between devices  5.99 us (7%)
  local copies, waits for them, and re-layouts  3.19 us (3%)
  other arithmetic  1.18 us (1%)
  between operations  0.96 us (1%)
    all_to_all x2, blocking collectives, exchange(): lax.all_to_all(value, names, split_axis=0, concat_axis=0, tiled=True, axi...  34.3 us
    all_to_all x2, starting transfers between devices, exchange(): lax.all_to_all(value, names, split_axis=0, concat_axis=0, tiled=True, axi...  22.3 us
    ppermute x1, starting transfers between devices, on_device(): near_other = lax.ppermute(near, 'core', swap)  4.04 us
    ppermute x1, starting transfers between devices, on_device(): after = lax.ppermute(hidden, ('x', 'core'), there)  3.95 us
    ppermute x1, waiting for transfers between devices, on_device(): lax.ppermute(after, ('x', 'core'), there)  3.66 us
    ppermute x1, starting transfers between devices, on_device(): lax.ppermute(after, ('x', 'core'), there)  3.36 us
    all_to_all x2, waiting for transfers between devices, exchange(): lax.all_to_all(value, names, split_axis=0, concat_axis=0, tiled=True, axi...  2.32 us
    unnamed x15, local copies, waits for them, and re-layouts  2.12 us
  transfers between devices with their start and end apart: 7, of which 2 were waited for; matrix products, arithmetic and copies ran while one was open for 2% of the time, Pallas kernels for 4%

profile of v8, /device:TPU:1, one launch (start us, length us, event | category | flops | bytes accessed | tf_op | source)
XLA Modules:
  0.0 91.3 jit_solution(13131356817363548721)
XLA Ops:
  0.6 4.0 %collective-permute-start = (bf16[64,1536]{1,0:T(8,128)(2,1)}, bf16[64,1536]{1,0:T(8,128)(2,1)S(1)}, u32[]{:S(2)}, u32[]{:S(2)}) collective-permute-start(bf16[64,1536]{1,0:T(8,128)(2,1)} %bitcast.23), channel_id=1, source_target_pairs={{0,384},{8,136},{128,0},{136,264},{256,128},{264,392},{384,256},{3... | collective-permute-start | bytes 589832 | tf_op jit(solution)/shard_map/ppermute | solution.py:318
  4.6 0.9 copy-done.1
  5.5 1.0 %shard_map.87 = bf16[64,24,256]{2,1,0:T(8,128)(2,1)} custom-call(bf16[24,2048]{1,0:T(8,128)(2,1)S(1)} %copy-done.1), custom_call_target="tpu_custom_call" | custom-call | flops 1048576 | bytes 1048576 | tf_op jit(solution)/shard_map/pallas_call | solution.py:66
  6.5 13.8 %all-to-all-start = ((bf16[64,24,256]{2,1,0:T(8,128)(2,1)}), bf16[64,24,256]{2,1,0:T(8,128)(2,1)S(1)}, u32[]{:S(2)}, u32[]{:S(2)}) async-start(bf16[64,24,256]{2,1,0:T(8,128)(2,1)} %shard_map.87), calls=%async_computation | async-start | bytes 1572864 | tf_op jit(solution)/shard_map/all_to_all | solution.py:39
  20.6 1.9 %collective-permute-start.2 = (bf16[64,1536]{1,0:T(8,128)(2,1)S(1)}, bf16[64,1536]{1,0:T(8,128)(2,1)S(1)}, u32[]{:S(2)}, u32[]{:S(2)}) collective-permute-start(bf16[64,1536]{1,0:T(8,128)(2,1)S(1)} %bitcast.25), channel_id=1, source_target_pairs={{0,128},{8,392},{128,256},{136,8},{256,384},{264,136},{384,0},{392... | collective-permute-start | bytes 589832 | tf_op jit(solution)/shard_map/ppermute | solution.py:320
  22.5 3.4 %collective-permute-start.3 = (bf16[64,1536]{1,0:T(8,128)(2,1)S(1)}, bf16[64,1536]{1,0:T(8,128)(2,1)S(1)}, u32[]{:S(2)}, u32[]{:S(2)}) collective-permute-start(bf16[64,1536]{1,0:T(8,128)(2,1)S(1)} %collective-permute-done), channel_id=1, source_target_pairs={{0,384},{8,136},{128,0},{136,264},{256,128},{264,392},{384,256},{3... | collective-permute-start | bytes 589832 | tf_op jit(solution)/shard_map/ppermute | solution.py:322
  25.9 4.0 %collective-permute-start.1 = (bf16[128,1536]{1,0:T(8,128)(2,1)S(1)}, bf16[128,1536]{1,0:T(8,128)(2,1)S(1)}, u32[]{:S(2)}, u32[]{:S(2)}) collective-permute-start(bf16[128,1536]{1,0:T(8,128)(2,1)S(1)} %constant_dynamic-update-slice_fusion.near), channel_id=1, source_target_pairs={{0,8},{8,0},{1,9},{9,1},{2,10},{10,2},{3,11},{11,3},{4,12},{12,4},... | collective-permute-start | bytes 1179656 | tf_op jit(solution)/shard_map/ppermute | solution.py:323
  30.2 0.5 copy-done.5
  30.8 3.7 %collective-permute-done.3 = bf16[64,1536]{1,0:T(8,128)(2,1)S(1)} collective-permute-done((bf16[64,1536]{1,0:T(8,128)(2,1)S(1)}, bf16[64,1536]{1,0:T(8,128)(2,1)S(1)}, u32[]{:S(2)}, u32[]{:S(2)}) %collective-permute-start.3) | collective-permute-done | bytes 196640 | tf_op jit(solution)/shard_map/ppermute | solution.py:322
  34.5 0.6 copy-done.4
  35.2 1.1 %shard_map.86 = (f32[96,128]{1,0:T(8,128)S(1)}, f32[96,128]{1,0:T(8,128)S(1)}, f32[96,128]{1,0:T(8,128)S(1)}) custom-call(s32[8]{0:T(128)S(1)} %concatenate.16.numbers, bf16[2,256,256]{2,1,0:T(8,128)(2,1)S(1)} %bitcast.18, bf16[2,16,256]{2,1,0:T(8,128)(2,1)S(1)} %pad.4.step_kv, bf16[2,48,128]{2,1,0:T(8,128)(2,1)S(1)} %bitcast.20), custom_call_target="tpu_custom_call" | custom-call | flops 12582912 | bytes 1048576 | tf_op jit(solution)/shard_map/pallas_call | solution.py:187
  36.4 1.9 %collective-permute-start.4 = (bf16[128,1536]{1,0:T(8,128)(2,1)S(1)}, bf16[128,1536]{1,0:T(8,128)(2,1)S(1)}, u32[]{:S(2)}, u32[]{:S(2)}) collective-permute-start(bf16[128,1536]{1,0:T(8,128)(2,1)S(1)} %pad_maximum_fusion.far), channel_id=1, source_target_pairs={{0,8},{8,0},{1,9},{9,1},{2,10},{10,2},{3,11},{11,3},{4,12},{12,4},... | collective-permute-start | bytes 1179656 | tf_op jit(solution)/shard_map/ppermute | solution.py:331
  38.8 0.1 add.253
  39.7 0.2 fusion.4
  40.0 0.2 fusion.order
  40.2 1.6 %shard_map.88 = bf16[64,16,128]{2,1,0:T(8,128)(2,1)S(1)} custom-call(s32[8]{0:T(128)S(1)} %concatenate.16.numbers, bf16[128,1536]{1,0:T(8,128)(2,1)S(1)} %constant_dynamic-update-slice_fusion.near, bf16[128,1536]{1,0:T(8,128)(2,1)S(1)} %collective-permute-done.1.near_other, bf16[128,1536]{1,0:T(8,128)(2,1)S(1)} %pad_maximum_fusion.far, ...), custom_call_target="tpu_custom_call" | custom-call | flops 402653184 | bytes 3145728 | tf_op jit(solution)/shard_map/pallas_call | solution.py:103
  41.8 21.3 %all_to_all.20.arrived = bf16[64,16,128]{2,1,0:T(8,128)(2,1)S(1)} all-to-all(bf16[64,16,128]{2,1,0:T(8,128)(2,1)S(1)} %shard_map.88), channel_id=1, replica_groups={{262,399,129,266,4,141,390,8,257,394,132,269,7,136,385,11,260,397,135,2..., dimensions={0} | all-to-all | bytes 524288 | tf_op jit(solution)/shard_map/all_to_all | solution.py:39
  63.2 1.2 %shard_map.89 = bf16[8,128,128]{2,1,0:T(8,128)(2,1)S(1)} custom-call(s32[8]{0:T(128)S(1)} %concatenate.16.numbers, bf16[64,16,128]{2,1,0:T(8,128)(2,1)S(1)} %all_to_all.20.arrived, f32[64,128]{1,0:T(8,128)S(1)} %get-tuple-element.28.cosine, f32[64,128]{1,0:T(8,128)S(1)} %get-tuple-element.29.sine, bf16[2,48,128]{2,1,0:T(8,128)(2,1)S(1)} %bitcast.21, ...), custom_call_target="tpu_custom_call" | custom-call | flops 3145728 | bytes 1048576 | tf_op jit(solution)/shard_map/pallas_call | solution.py:242
  64.4 13.0 %all_to_all.21.arrived = bf16[8,128,128]{2,1,0:T(8,128)(2,1)S(1)} all-to-all(bf16[8,128,128]{2,1,0:T(8,128)(2,1)S(1)} %shard_map.89), channel_id=1, replica_groups={{64,80,96,112,0,16,32,48},{65,81,97,113,1,17,33,49},{66,82,98,114,2,18,..., dimensions={0} | all-to-all | bytes 524288 | tf_op jit(solution)/shard_map/all_to_all | solution.py:39
  77.3 0.9 shard_map.90
  78.2 8.5 %all-to-all-start.3 = ((bf16[8,112,128]{2,1,0:T(8,128)(2,1)}), bf16[8,112,128]{2,1,0:T(8,128)(2,1)S(1)}, u32[]{:S(2)}, u32[]{:S(2)}) async-start(bf16[8,112,128]{2,1,0:T(8,128)(2,1)} %shard_map.90), calls=%async_computation.3 | async-start | bytes 458752 | tf_op jit(solution)/shard_map/all_to_all | solution.py:39
  86.7 1.5 %shard_map.92 = bf16[2,256,256]{2,1,0:T(8,128)(2,1)} custom-call(s32[8]{0:T(128)S(1)} %concatenate.16.numbers, bf16[8,128,128]{2,1,0:T(8,128)(2,1)S(1)} %all_to_all.21.arrived, bf16[2,256,256]{2,1,0:T(8,128)(2,1)S(1)} %bitcast.19), custom_call_target="tpu_custom_call" | custom-call | flops 67108864 | bytes 1048576 | tf_op jit(solution)/shard_map/pallas_call | solution.py:295
  88.2 2.3 %all-to-all-done.3.arrived = bf16[8,112,128]{2,1,0:T(8,128)(2,1)S(1)} async-done(((bf16[8,112,128]{2,1,0:T(8,128)(2,1)}), bf16[8,112,128]{2,1,0:T(8,128)(2,1)S(1)}, u32[]{:S(2)}, u32[]{:S(2)}) %all-to-all-start.3) | async-done | bytes 229408 | tf_op jit(solution)/shard_map/all_to_all | solution.py:39
  90.5 0.8 shard_map.91
  (44 shorter events, 1.8 us)
Async XLA Ops:
  0.6 19.9 %collective-permute-start = (bf16[64,1536]{1,0:T(8,128)(2,1)}, bf16[64,1536]{1,0:T(8,128)(2,1)S(1)}, u32[]{:S(2)}, u32[]{:S(2)}) collective-permute-start(bf16[64,1536]{1,0:T(8,128)(2,1)} %bitcast.23), channel_id=1, source_target_pairs={{0,384},{8,136},{128,0},{136,264},{256,128},{264,392},{384,256},{3... | collective-permute-start | bytes 589832 | tf_op jit(solution)/shard_map/ppermute | solution.py:318
  4.6 0.9 copy-start.1
  6.5 14.0 %copy-start.3 = (bf16[2,32,1536]{2,1,0:T(8,128)(2,1)S(1)}, bf16[2,32,1536]{2,1,0:T(8,128)(2,1)}, u32[]{:S(2)}) copy-start(bf16[2,32,1536]{2,1,0:T(8,128)(2,1)} %param.7) | copy-start | bytes 589828
  6.5 33.7 %all-to-all-start = ((bf16[64,24,256]{2,1,0:T(8,128)(2,1)}), bf16[64,24,256]{2,1,0:T(8,128)(2,1)S(1)}, u32[]{:S(2)}, u32[]{:S(2)}) async-start(bf16[64,24,256]{2,1,0:T(8,128)(2,1)} %shard_map.87), calls=%async_computation | async-start | bytes 1572864 | tf_op jit(solution)/shard_map/all_to_all | solution.py:39
  20.6 13.9 %collective-permute-start.2 = (bf16[64,1536]{1,0:T(8,128)(2,1)S(1)}, bf16[64,1536]{1,0:T(8,128)(2,1)S(1)}, u32[]{:S(2)}, u32[]{:S(2)}) collective-permute-start(bf16[64,1536]{1,0:T(8,128)(2,1)S(1)} %bitcast.25), channel_id=1, source_target_pairs={{0,128},{8,392},{128,256},{136,8},{256,384},{264,136},{384,0},{392... | collective-permute-start | bytes 589832 | tf_op jit(solution)/shard_map/ppermute | solution.py:320
  22.5 11.9 %collective-permute-start.3 = (bf16[64,1536]{1,0:T(8,128)(2,1)S(1)}, bf16[64,1536]{1,0:T(8,128)(2,1)S(1)}, u32[]{:S(2)}, u32[]{:S(2)}) collective-permute-start(bf16[64,1536]{1,0:T(8,128)(2,1)S(1)} %collective-permute-done), channel_id=1, source_target_pairs={{0,384},{8,136},{128,0},{136,264},{256,128},{264,392},{384,256},{3... | collective-permute-start | bytes 589832 | tf_op jit(solution)/shard_map/ppermute | solution.py:322
  25.9 8.6 %collective-permute-start.1 = (bf16[128,1536]{1,0:T(8,128)(2,1)S(1)}, bf16[128,1536]{1,0:T(8,128)(2,1)S(1)}, u32[]{:S(2)}, u32[]{:S(2)}) collective-permute-start(bf16[128,1536]{1,0:T(8,128)(2,1)S(1)} %constant_dynamic-update-slice_fusion.near), channel_id=1, source_target_pairs={{0,8},{8,0},{1,9},{9,1},{2,10},{10,2},{3,11},{11,3},{4,12},{12,4},... | collective-permute-start | bytes 1179656 | tf_op jit(solution)/shard_map/ppermute | solution.py:323
  30.0 0.7 copy-start.5
  30.8 4.5 %copy-start = (bf16[2,256,1,256]{3,1,2,0:T(8,128)(2,1)S(1)}, bf16[2,256,1,256]{3,1,2,0:T(8,128)(2,1)}, u32[]{:S(2)}) copy-start(bf16[2,256,1,256]{3,1,2,0:T(8,128)(2,1)} %param.9) | copy-start | bytes 786436
  34.4 0.8 copy-start.2
  34.5 0.7 copy-start.4
  34.5 0.7 copy-start.6
  36.4 3.8 %collective-permute-start.4 = (bf16[128,1536]{1,0:T(8,128)(2,1)S(1)}, bf16[128,1536]{1,0:T(8,128)(2,1)S(1)}, u32[]{:S(2)}, u32[]{:S(2)}) collective-permute-start(bf16[128,1536]{1,0:T(8,128)(2,1)S(1)} %pad_maximum_fusion.far), channel_id=1, source_target_pairs={{0,8},{8,0},{1,9},{9,1},{2,10},{10,2},{3,11},{11,3},{4,12},{12,4},... | collective-permute-start | bytes 1179656 | tf_op jit(solution)/shard_map/ppermute | solution.py:331
  78.2 12.3 %all-to-all-start.3 = ((bf16[8,112,128]{2,1,0:T(8,128)(2,1)}), bf16[8,112,128]{2,1,0:T(8,128)(2,1)S(1)}, u32[]{:S(2)}, u32[]{:S(2)}) async-start(bf16[8,112,128]{2,1,0:T(8,128)(2,1)} %shard_map.90), calls=%async_computation.3 | async-start | bytes 458752 | tf_op jit(solution)/shard_map/all_to_all | solution.py:39

commit v9 on v8

--- a/solution.py
+++ b/solution.py
@@ -19,7 +19,7 @@
 ALL_Q = CONV * QROWS
 PACK = ALL_Q + 16
 PIECE = 32
-SEQ_ORDER = [(2 * NY + 6 + 11 * place) % (NX * NY) * NC + core for place in range(NX * NY) for core in range(NC)]
+SEQ_ORDER = [((2 * NY + 6) * NC + place) % SEQ for place in range(SEQ)]
 SUM_ORDER = [(6 * GROUP + 2 * NC + 11 * place) % (NZ * GROUP) for place in range(NZ * GROUP)]
 Y_ORDER = [(4 + place) % NY for place in range(NY)]
 GROUP_ORDER = [(2 * NC + place) % GROUP for place in range(GROUP)]

time: 92 us -> 91.1 us (level)
  blocking collectives: 34.3 us -> 32.8 us
    all_to_all x2, blocking collectives: 34.3 us -> 32.8 us  [exchange(): lax.all_to_all(value, names, split_axis=0, concat_axis=0, tiled=True, axi...]
where the time goes in v9:
time: 91.1 us; the launch traced here: 90.5 us
  starting transfers between devices  37.2 us (41%)
  blocking collectives  32.8 us (36%)
  Pallas kernels  8.23 us (9%)
  waiting for transfers between devices  6.85 us (8%)
  local copies, waits for them, and re-layouts  3.19 us (4%)
  other arithmetic  1.18 us (1%)
  between operations  0.96 us (1%)
    all_to_all x2, blocking collectives, exchange(): lax.all_to_all(value, names, split_axis=0, concat_axis=0, tiled=True, axi...  32.8 us
    all_to_all x2, starting transfers between devices, exchange(): lax.all_to_all(value, names, split_axis=0, concat_axis=0, tiled=True, axi...  22 us
    ppermute x1, waiting for transfers between devices, on_device(): lax.ppermute(after, ('x', 'core'), there)  4.52 us
    ppermute x1, starting transfers between devices, on_device(): near_other = lax.ppermute(near, 'core', swap)  4.04 us
    ppermute x1, starting transfers between devices, on_device(): after = lax.ppermute(hidden, ('x', 'core'), there)  3.95 us
    ppermute x1, starting transfers between devices, on_device(): lax.ppermute(after, ('x', 'core'), there)  3.11 us
    all_to_all x2, waiting for transfers between devices, exchange(): lax.all_to_all(value, names, split_axis=0, concat_axis=0, tiled=True, axi...  2.32 us
    ppermute x1, starting transfers between devices, on_device(): before = lax.ppermute(hidden, ('x', 'core'), back)  2.18 us
  transfers between devices with their start and end apart: 7, of which 2 were waited for; matrix products, arithmetic and copies ran while one was open for 2% of the time, Pallas kernels for 4%

profile of v9, /device:TPU:1, one launch (start us, length us, event | category | flops | bytes accessed | tf_op | source)
XLA Modules:
  0.0 90.5 jit_solution(10609174889945140208)
XLA Ops:
  0.6 4.0 %collective-permute-start = (bf16[64,1536]{1,0:T(8,128)(2,1)}, bf16[64,1536]{1,0:T(8,128)(2,1)S(1)}, u32[]{:S(2)}, u32[]{:S(2)}) collective-permute-start(bf16[64,1536]{1,0:T(8,128)(2,1)} %bitcast.23), channel_id=1, source_target_pairs={{0,384},{8,136},{128,0},{136,264},{256,128},{264,392},{384,256},{3... | collective-permute-start | bytes 589832 | tf_op jit(solution)/shard_map/ppermute | solution.py:318
  4.6 0.9 copy-done.1
  5.5 1.0 %shard_map.87 = bf16[64,24,256]{2,1,0:T(8,128)(2,1)} custom-call(bf16[24,2048]{1,0:T(8,128)(2,1)S(1)} %copy-done.1), custom_call_target="tpu_custom_call" | custom-call | flops 1048576 | bytes 1048576 | tf_op jit(solution)/shard_map/pallas_call | solution.py:66
  6.5 13.6 %all-to-all-start = ((bf16[64,24,256]{2,1,0:T(8,128)(2,1)}), bf16[64,24,256]{2,1,0:T(8,128)(2,1)S(1)}, u32[]{:S(2)}, u32[]{:S(2)}) async-start(bf16[64,24,256]{2,1,0:T(8,128)(2,1)} %shard_map.87), calls=%async_computation | async-start | bytes 1572864 | tf_op jit(solution)/shard_map/all_to_all | solution.py:39
  20.3 2.2 %collective-permute-start.2 = (bf16[64,1536]{1,0:T(8,128)(2,1)S(1)}, bf16[64,1536]{1,0:T(8,128)(2,1)S(1)}, u32[]{:S(2)}, u32[]{:S(2)}) collective-permute-start(bf16[64,1536]{1,0:T(8,128)(2,1)S(1)} %bitcast.25), channel_id=1, source_target_pairs={{0,128},{8,392},{128,256},{136,8},{256,384},{264,136},{384,0},{392... | collective-permute-start | bytes 589832 | tf_op jit(solution)/shard_map/ppermute | solution.py:320
  22.5 3.1 %collective-permute-start.3 = (bf16[64,1536]{1,0:T(8,128)(2,1)S(1)}, bf16[64,1536]{1,0:T(8,128)(2,1)S(1)}, u32[]{:S(2)}, u32[]{:S(2)}) collective-permute-start(bf16[64,1536]{1,0:T(8,128)(2,1)S(1)} %collective-permute-done), channel_id=1, source_target_pairs={{0,384},{8,136},{128,0},{136,264},{256,128},{264,392},{384,256},{3... | collective-permute-start | bytes 589832 | tf_op jit(solution)/shard_map/ppermute | solution.py:322
  25.6 4.0 %collective-permute-start.1 = (bf16[128,1536]{1,0:T(8,128)(2,1)S(1)}, bf16[128,1536]{1,0:T(8,128)(2,1)S(1)}, u32[]{:S(2)}, u32[]{:S(2)}) collective-permute-start(bf16[128,1536]{1,0:T(8,128)(2,1)S(1)} %constant_dynamic-update-slice_fusion.near), channel_id=1, source_target_pairs={{0,8},{8,0},{1,9},{9,1},{2,10},{10,2},{3,11},{11,3},{4,12},{12,4},... | collective-permute-start | bytes 1179656 | tf_op jit(solution)/shard_map/ppermute | solution.py:323
  29.9 0.5 copy-done.5
  30.5 4.5 %collective-permute-done.3 = bf16[64,1536]{1,0:T(8,128)(2,1)S(1)} collective-permute-done((bf16[64,1536]{1,0:T(8,128)(2,1)S(1)}, bf16[64,1536]{1,0:T(8,128)(2,1)S(1)}, u32[]{:S(2)}, u32[]{:S(2)}) %collective-permute-start.3) | collective-permute-done | bytes 196640 | tf_op jit(solution)/shard_map/ppermute | solution.py:322
  35.1 0.6 copy-done.4
  35.8 1.1 %shard_map.86 = (f32[96,128]{1,0:T(8,128)S(1)}, f32[96,128]{1,0:T(8,128)S(1)}, f32[96,128]{1,0:T(8,128)S(1)}) custom-call(s32[8]{0:T(128)S(1)} %concatenate.16.numbers, bf16[2,256,256]{2,1,0:T(8,128)(2,1)S(1)} %bitcast.18, bf16[2,16,256]{2,1,0:T(8,128)(2,1)S(1)} %pad.4.step_kv, bf16[2,48,128]{2,1,0:T(8,128)(2,1)S(1)} %bitcast.20), custom_call_target="tpu_custom_call" | custom-call | flops 12582912 | bytes 1048576 | tf_op jit(solution)/shard_map/pallas_call | solution.py:187
  37.0 1.9 %collective-permute-start.4 = (bf16[128,1536]{1,0:T(8,128)(2,1)S(1)}, bf16[128,1536]{1,0:T(8,128)(2,1)S(1)}, u32[]{:S(2)}, u32[]{:S(2)}) collective-permute-start(bf16[128,1536]{1,0:T(8,128)(2,1)S(1)} %pad_maximum_fusion.far), channel_id=1, source_target_pairs={{0,8},{8,0},{1,9},{9,1},{2,10},{10,2},{3,11},{11,3},{4,12},{12,4},... | collective-permute-start | bytes 1179656 | tf_op jit(solution)/shard_map/ppermute | solution.py:331
  39.7 0.1 add.246
  40.3 0.2 fusion.4
  40.6 0.2 fusion.order
  40.8 1.6 %shard_map.88 = bf16[64,16,128]{2,1,0:T(8,128)(2,1)S(1)} custom-call(s32[8]{0:T(128)S(1)} %concatenate.16.numbers, bf16[128,1536]{1,0:T(8,128)(2,1)S(1)} %constant_dynamic-update-slice_fusion.near, bf16[128,1536]{1,0:T(8,128)(2,1)S(1)} %collective-permute-done.1.near_other, bf16[128,1536]{1,0:T(8,128)(2,1)S(1)} %pad_maximum_fusion.far, ...), custom_call_target="tpu_custom_call" | custom-call | flops 402653184 | bytes 3145728 | tf_op jit(solution)/shard_map/pallas_call | solution.py:103
  42.4 21.3 %all_to_all.20.arrived = bf16[64,16,128]{2,1,0:T(8,128)(2,1)S(1)} all-to-all(bf16[64,16,128]{2,1,0:T(8,128)(2,1)S(1)} %shard_map.88), channel_id=1, replica_groups={{262,399,129,266,4,141,390,8,257,394,132,269,7,136,385,11,260,397,135,2..., dimensions={0} | all-to-all | bytes 524288 | tf_op jit(solution)/shard_map/all_to_all | solution.py:39
  63.7 1.2 %shard_map.89 = bf16[8,128,128]{2,1,0:T(8,128)(2,1)S(1)} custom-call(s32[8]{0:T(128)S(1)} %concatenate.16.numbers, bf16[64,16,128]{2,1,0:T(8,128)(2,1)S(1)} %all_to_all.20.arrived, f32[64,128]{1,0:T(8,128)S(1)} %get-tuple-element.28.cosine, f32[64,128]{1,0:T(8,128)S(1)} %get-tuple-element.29.sine, bf16[2,48,128]{2,1,0:T(8,128)(2,1)S(1)} %bitcast.21, ...), custom_call_target="tpu_custom_call" | custom-call | flops 3145728 | bytes 1048576 | tf_op jit(solution)/shard_map/pallas_call | solution.py:242
  65.0 11.5 %all_to_all.21.arrived = bf16[8,128,128]{2,1,0:T(8,128)(2,1)S(1)} all-to-all(bf16[8,128,128]{2,1,0:T(8,128)(2,1)S(1)} %shard_map.89), channel_id=1, replica_groups={{64,80,96,112,0,16,32,48},{65,81,97,113,1,17,33,49},{66,82,98,114,2,18,..., dimensions={0} | all-to-all | bytes 524288 | tf_op jit(solution)/shard_map/all_to_all | solution.py:39
  76.5 0.9 shard_map.90
  77.4 8.5 %all-to-all-start.3 = ((bf16[8,112,128]{2,1,0:T(8,128)(2,1)}), bf16[8,112,128]{2,1,0:T(8,128)(2,1)S(1)}, u32[]{:S(2)}, u32[]{:S(2)}) async-start(bf16[8,112,128]{2,1,0:T(8,128)(2,1)} %shard_map.90), calls=%async_computation.3 | async-start | bytes 458752 | tf_op jit(solution)/shard_map/all_to_all | solution.py:39
  85.9 1.5 %shard_map.92 = bf16[2,256,256]{2,1,0:T(8,128)(2,1)} custom-call(s32[8]{0:T(128)S(1)} %concatenate.16.numbers, bf16[8,128,128]{2,1,0:T(8,128)(2,1)S(1)} %all_to_all.21.arrived, bf16[2,256,256]{2,1,0:T(8,128)(2,1)S(1)} %bitcast.19), custom_call_target="tpu_custom_call" | custom-call | flops 67108864 | bytes 1048576 | tf_op jit(solution)/shard_map/pallas_call | solution.py:295
  87.3 2.3 %all-to-all-done.3.arrived = bf16[8,112,128]{2,1,0:T(8,128)(2,1)S(1)} async-done(((bf16[8,112,128]{2,1,0:T(8,128)(2,1)}), bf16[8,112,128]{2,1,0:T(8,128)(2,1)S(1)}, u32[]{:S(2)}, u32[]{:S(2)}) %all-to-all-start.3) | async-done | bytes 229408 | tf_op jit(solution)/shard_map/all_to_all | solution.py:39
  89.6 0.8 shard_map.91
  (44 shorter events, 1.8 us)
Async XLA Ops:
  0.6 19.6 %collective-permute-start = (bf16[64,1536]{1,0:T(8,128)(2,1)}, bf16[64,1536]{1,0:T(8,128)(2,1)S(1)}, u32[]{:S(2)}, u32[]{:S(2)}) collective-permute-start(bf16[64,1536]{1,0:T(8,128)(2,1)} %bitcast.23), channel_id=1, source_target_pairs={{0,384},{8,136},{128,0},{136,264},{256,128},{264,392},{384,256},{3... | collective-permute-start | bytes 589832 | tf_op jit(solution)/shard_map/ppermute | solution.py:318
  4.6 0.9 copy-start.1
  6.5 13.8 %copy-start.3 = (bf16[2,32,1536]{2,1,0:T(8,128)(2,1)S(1)}, bf16[2,32,1536]{2,1,0:T(8,128)(2,1)}, u32[]{:S(2)}) copy-start(bf16[2,32,1536]{2,1,0:T(8,128)(2,1)} %param.7) | copy-start | bytes 589828
  6.5 34.2 %all-to-all-start = ((bf16[64,24,256]{2,1,0:T(8,128)(2,1)}), bf16[64,24,256]{2,1,0:T(8,128)(2,1)S(1)}, u32[]{:S(2)}, u32[]{:S(2)}) async-start(bf16[64,24,256]{2,1,0:T(8,128)(2,1)} %shard_map.87), calls=%async_computation | async-start | bytes 1572864 | tf_op jit(solution)/shard_map/all_to_all | solution.py:39
  20.3 14.7 %collective-permute-start.2 = (bf16[64,1536]{1,0:T(8,128)(2,1)S(1)}, bf16[64,1536]{1,0:T(8,128)(2,1)S(1)}, u32[]{:S(2)}, u32[]{:S(2)}) collective-permute-start(bf16[64,1536]{1,0:T(8,128)(2,1)S(1)} %bitcast.25), channel_id=1, source_target_pairs={{0,128},{8,392},{128,256},{136,8},{256,384},{264,136},{384,0},{392... | collective-permute-start | bytes 589832 | tf_op jit(solution)/shard_map/ppermute | solution.py:320
  22.5 12.5 %collective-permute-start.3 = (bf16[64,1536]{1,0:T(8,128)(2,1)S(1)}, bf16[64,1536]{1,0:T(8,128)(2,1)S(1)}, u32[]{:S(2)}, u32[]{:S(2)}) collective-permute-start(bf16[64,1536]{1,0:T(8,128)(2,1)S(1)} %collective-permute-done), channel_id=1, source_target_pairs={{0,384},{8,136},{128,0},{136,264},{256,128},{264,392},{384,256},{3... | collective-permute-start | bytes 589832 | tf_op jit(solution)/shard_map/ppermute | solution.py:322
  25.6 9.4 %collective-permute-start.1 = (bf16[128,1536]{1,0:T(8,128)(2,1)S(1)}, bf16[128,1536]{1,0:T(8,128)(2,1)S(1)}, u32[]{:S(2)}, u32[]{:S(2)}) collective-permute-start(bf16[128,1536]{1,0:T(8,128)(2,1)S(1)} %constant_dynamic-update-slice_fusion.near), channel_id=1, source_target_pairs={{0,8},{8,0},{1,9},{9,1},{2,10},{10,2},{3,11},{11,3},{4,12},{12,4},... | collective-permute-start | bytes 1179656 | tf_op jit(solution)/shard_map/ppermute | solution.py:323
  29.8 0.7 copy-start.5
  30.5 5.3 %copy-start = (bf16[2,256,1,256]{3,1,2,0:T(8,128)(2,1)S(1)}, bf16[2,256,1,256]{3,1,2,0:T(8,128)(2,1)}, u32[]{:S(2)}) copy-start(bf16[2,256,1,256]{3,1,2,0:T(8,128)(2,1)} %param.9) | copy-start | bytes 786436
  35.0 0.8 copy-start.2
  35.1 0.7 copy-start.4
  35.1 0.7 copy-start.6
  37.0 3.8 %collective-permute-start.4 = (bf16[128,1536]{1,0:T(8,128)(2,1)S(1)}, bf16[128,1536]{1,0:T(8,128)(2,1)S(1)}, u32[]{:S(2)}, u32[]{:S(2)}) collective-permute-start(bf16[128,1536]{1,0:T(8,128)(2,1)S(1)} %pad_maximum_fusion.far), channel_id=1, source_target_pairs={{0,8},{8,0},{1,9},{9,1},{2,10},{10,2},{3,11},{11,3},{4,12},{12,4},... | collective-permute-start | bytes 1179656 | tf_op jit(solution)/shard_map/ppermute | solution.py:331
  77.4 12.3 %all-to-all-start.3 = ((bf16[8,112,128]{2,1,0:T(8,128)(2,1)}), bf16[8,112,128]{2,1,0:T(8,128)(2,1)S(1)}, u32[]{:S(2)}, u32[]{:S(2)}) async-start(bf16[8,112,128]{2,1,0:T(8,128)(2,1)} %shard_map.90), calls=%async_computation.3 | async-start | bytes 458752 | tf_op jit(solution)/shard_map/all_to_all | solution.py:39

commit v10 on v6

--- a/solution.py
+++ b/solution.py
@@ -20,7 +20,7 @@
 PACK = ALL_Q + 16
 PIECE = 32
 FIRST_SEQ = (2 * NY + 6) * NC
-FIRST = 6 * GROUP + 2 * NC
+FIRST = 5 * GROUP + 2 * NC
 FIRST_Y = 4
 FIRST_GROUP = 2 * NC
 VMEM_LIMIT = 48 * 1024 * 1024

time: 91.1 us -> 91.3 us (level)
  no operation moved by 1% of the time
where the time goes in v10:
time: 91.3 us; the launch traced here: 90.7 us
  starting transfers between devices  35.2 us (39%)
  blocking collectives  35.2 us (39%)
  Pallas kernels  8.23 us (9%)
  waiting for transfers between devices  6.78 us (7%)
  local copies, waits for them, and re-layouts  3.19 us (3%)
  other arithmetic  1.18 us (1%)
  between operations  0.96 us (1%)
    all_to_all x2, blocking collectives, exchange(): lax.all_to_all(value, names, split_axis=0, concat_axis=0, tiled=True, axi...  35.2 us
    all_to_all x2, starting transfers between devices, exchange(): lax.all_to_all(value, names, split_axis=0, concat_axis=0, tiled=True, axi...  20 us
    ppermute x1, waiting for transfers between devices, on_device(): lax.ppermute(after, ('x', 'core'), there)  4.52 us
    ppermute x1, starting transfers between devices, on_device(): near_other = lax.ppermute(near, 'core', swap)  4.04 us
    ppermute x1, starting transfers between devices, on_device(): after = lax.ppermute(hidden, ('x', 'core'), there)  3.95 us
    ppermute x1, starting transfers between devices, on_device(): lax.ppermute(after, ('x', 'core'), there)  3.11 us
    all_to_all x2, waiting for transfers between devices, exchange(): lax.all_to_all(value, names, split_axis=0, concat_axis=0, tiled=True, axi...  2.26 us
    ppermute x1, starting transfers between devices, on_device(): before = lax.ppermute(hidden, ('x', 'core'), back)  2.18 us
  transfers between devices with their start and end apart: 7, of which 2 were waited for; matrix products, arithmetic and copies ran while one was open for 2% of the time, Pallas kernels for 4%

profile of v10, /device:TPU:1, one launch (start us, length us, event | category | flops | bytes accessed | tf_op | source)
XLA Modules:
  0.0 90.7 jit_solution(2808758011467482913)
XLA Ops:
  0.6 4.0 %collective-permute-start = (bf16[64,1536]{1,0:T(8,128)(2,1)}, bf16[64,1536]{1,0:T(8,128)(2,1)S(1)}, u32[]{:S(2)}, u32[]{:S(2)}) collective-permute-start(bf16[64,1536]{1,0:T(8,128)(2,1)} %bitcast.23), channel_id=1, source_target_pairs={{0,384},{8,136},{128,0},{136,264},{256,128},{264,392},{384,256},{3... | collective-permute-start | bytes 589832 | tf_op jit(solution)/shard_map/ppermute | solution.py:319
  4.6 0.9 copy-done.1
  5.5 1.0 %shard_map.87 = bf16[64,24,256]{2,1,0:T(8,128)(2,1)} custom-call(bf16[24,2048]{1,0:T(8,128)(2,1)S(1)} %copy-done.1), custom_call_target="tpu_custom_call" | custom-call | flops 1048576 | bytes 1048576 | tf_op jit(solution)/shard_map/pallas_call | solution.py:68
  6.5 13.6 %all-to-all-start = ((bf16[64,24,256]{2,1,0:T(8,128)(2,1)}), bf16[64,24,256]{2,1,0:T(8,128)(2,1)S(1)}, u32[]{:S(2)}, u32[]{:S(2)}) async-start(bf16[64,24,256]{2,1,0:T(8,128)(2,1)} %shard_map.87), calls=%async_computation | async-start | bytes 1572864 | tf_op jit(solution)/shard_map/all_to_all | solution.py:41
  20.3 2.2 %collective-permute-start.2 = (bf16[64,1536]{1,0:T(8,128)(2,1)S(1)}, bf16[64,1536]{1,0:T(8,128)(2,1)S(1)}, u32[]{:S(2)}, u32[]{:S(2)}) collective-permute-start(bf16[64,1536]{1,0:T(8,128)(2,1)S(1)} %bitcast.25), channel_id=1, source_target_pairs={{0,128},{8,392},{128,256},{136,8},{256,384},{264,136},{384,0},{392... | collective-permute-start | bytes 589832 | tf_op jit(solution)/shard_map/ppermute | solution.py:321
  22.5 3.1 %collective-permute-start.3 = (bf16[64,1536]{1,0:T(8,128)(2,1)S(1)}, bf16[64,1536]{1,0:T(8,128)(2,1)S(1)}, u32[]{:S(2)}, u32[]{:S(2)}) collective-permute-start(bf16[64,1536]{1,0:T(8,128)(2,1)S(1)} %collective-permute-done), channel_id=1, source_target_pairs={{0,384},{8,136},{128,0},{136,264},{256,128},{264,392},{384,256},{3... | collective-permute-start | bytes 589832 | tf_op jit(solution)/shard_map/ppermute | solution.py:323
  25.6 4.0 %collective-permute-start.1 = (bf16[128,1536]{1,0:T(8,128)(2,1)S(1)}, bf16[128,1536]{1,0:T(8,128)(2,1)S(1)}, u32[]{:S(2)}, u32[]{:S(2)}) collective-permute-start(bf16[128,1536]{1,0:T(8,128)(2,1)S(1)} %constant_dynamic-update-slice_fusion.near), channel_id=1, source_target_pairs={{0,8},{8,0},{1,9},{9,1},{2,10},{10,2},{3,11},{11,3},{4,12},{12,4},... | collective-permute-start | bytes 1179656 | tf_op jit(solution)/shard_map/ppermute | solution.py:324
  29.9 0.5 copy-done.5
  30.5 4.5 %collective-permute-done.3 = bf16[64,1536]{1,0:T(8,128)(2,1)S(1)} collective-permute-done((bf16[64,1536]{1,0:T(8,128)(2,1)S(1)}, bf16[64,1536]{1,0:T(8,128)(2,1)S(1)}, u32[]{:S(2)}, u32[]{:S(2)}) %collective-permute-start.3) | collective-permute-done | bytes 196640 | tf_op jit(solution)/shard_map/ppermute | solution.py:323
  35.1 0.6 copy-done.4
  35.8 1.1 %shard_map.86 = (f32[96,128]{1,0:T(8,128)S(1)}, f32[96,128]{1,0:T(8,128)S(1)}, f32[96,128]{1,0:T(8,128)S(1)}) custom-call(s32[8]{0:T(128)S(1)} %concatenate.16.numbers, bf16[2,256,256]{2,1,0:T(8,128)(2,1)S(1)} %bitcast.18, bf16[2,16,256]{2,1,0:T(8,128)(2,1)S(1)} %pad.4.step_kv, bf16[2,48,128]{2,1,0:T(8,128)(2,1)S(1)} %bitcast.20), custom_call_target="tpu_custom_call" | custom-call | flops 12582912 | bytes 1048576 | tf_op jit(solution)/shard_map/pallas_call | solution.py:188
  37.0 1.9 %collective-permute-start.4 = (bf16[128,1536]{1,0:T(8,128)(2,1)S(1)}, bf16[128,1536]{1,0:T(8,128)(2,1)S(1)}, u32[]{:S(2)}, u32[]{:S(2)}) collective-permute-start(bf16[128,1536]{1,0:T(8,128)(2,1)S(1)} %pad_maximum_fusion.far), channel_id=1, source_target_pairs={{0,8},{8,0},{1,9},{9,1},{2,10},{10,2},{3,11},{11,3},{4,12},{12,4},... | collective-permute-start | bytes 1179656 | tf_op jit(solution)/shard_map/ppermute | solution.py:332
  39.4 0.1 add.253
  40.3 0.2 fusion.4
  40.6 0.2 fusion.order
  40.8 1.6 %shard_map.88 = bf16[64,16,128]{2,1,0:T(8,128)(2,1)S(1)} custom-call(s32[8]{0:T(128)S(1)} %concatenate.16.numbers, bf16[128,1536]{1,0:T(8,128)(2,1)S(1)} %constant_dynamic-update-slice_fusion.near, bf16[128,1536]{1,0:T(8,128)(2,1)S(1)} %collective-permute-done.1.near_other, bf16[128,1536]{1,0:T(8,128)(2,1)S(1)} %pad_maximum_fusion.far, ...), custom_call_target="tpu_custom_call" | custom-call | flops 402653184 | bytes 3145728 | tf_op jit(solution)/shard_map/pallas_call | solution.py:104
  42.4 22.5 %all_to_all.20.arrived = bf16[64,16,128]{2,1,0:T(8,128)(2,1)S(1)} all-to-all(bf16[64,16,128]{2,1,0:T(8,128)(2,1)S(1)} %shard_map.88), channel_id=1, replica_groups={{261,269,389,397,6,14,134,142,262,270,390,398,7,15,135,143,263,271,391,..., dimensions={0} | all-to-all | bytes 524288 | tf_op jit(solution)/shard_map/all_to_all | solution.py:41
  64.9 1.2 %shard_map.89 = bf16[8,128,128]{2,1,0:T(8,128)(2,1)S(1)} custom-call(s32[8]{0:T(128)S(1)} %concatenate.16.numbers, bf16[64,16,128]{2,1,0:T(8,128)(2,1)S(1)} %all_to_all.20.arrived, f32[64,128]{1,0:T(8,128)S(1)} %get-tuple-element.28.cosine, f32[64,128]{1,0:T(8,128)S(1)} %get-tuple-element.29.sine, bf16[2,48,128]{2,1,0:T(8,128)(2,1)S(1)} %bitcast.21, ...), custom_call_target="tpu_custom_call" | custom-call | flops 3145728 | bytes 1048576 | tf_op jit(solution)/shard_map/pallas_call | solution.py:243
  66.1 12.8 %all_to_all.21.arrived = bf16[8,128,128]{2,1,0:T(8,128)(2,1)S(1)} all-to-all(bf16[8,128,128]{2,1,0:T(8,128)(2,1)S(1)} %shard_map.89), channel_id=1, replica_groups={{64,80,96,112,0,16,32,48},{65,81,97,113,1,17,33,49},{66,82,98,114,2,18,..., dimensions={0} | all-to-all | bytes 524288 | tf_op jit(solution)/shard_map/all_to_all | solution.py:41
  78.9 0.9 shard_map.90
  79.8 6.4 %all-to-all-start.3 = ((bf16[8,112,128]{2,1,0:T(8,128)(2,1)}), bf16[8,112,128]{2,1,0:T(8,128)(2,1)S(1)}, u32[]{:S(2)}, u32[]{:S(2)}) async-start(bf16[8,112,128]{2,1,0:T(8,128)(2,1)} %shard_map.90), calls=%async_computation.3 | async-start | bytes 458752 | tf_op jit(solution)/shard_map/all_to_all | solution.py:41
  86.2 1.5 %shard_map.92 = bf16[2,256,256]{2,1,0:T(8,128)(2,1)} custom-call(s32[8]{0:T(128)S(1)} %concatenate.16.numbers, bf16[8,128,128]{2,1,0:T(8,128)(2,1)S(1)} %all_to_all.21.arrived, bf16[2,256,256]{2,1,0:T(8,128)(2,1)S(1)} %bitcast.19), custom_call_target="tpu_custom_call" | custom-call | flops 67108864 | bytes 1048576 | tf_op jit(solution)/shard_map/pallas_call | solution.py:296
  87.6 2.3 %all-to-all-done.3.arrived = bf16[8,112,128]{2,1,0:T(8,128)(2,1)S(1)} async-done(((bf16[8,112,128]{2,1,0:T(8,128)(2,1)}), bf16[8,112,128]{2,1,0:T(8,128)(2,1)S(1)}, u32[]{:S(2)}, u32[]{:S(2)}) %all-to-all-start.3) | async-done | bytes 229408 | tf_op jit(solution)/shard_map/all_to_all | solution.py:41
  89.9 0.8 shard_map.91
  (44 shorter events, 1.8 us)
Async XLA Ops:
  0.6 19.6 %collective-permute-start = (bf16[64,1536]{1,0:T(8,128)(2,1)}, bf16[64,1536]{1,0:T(8,128)(2,1)S(1)}, u32[]{:S(2)}, u32[]{:S(2)}) collective-permute-start(bf16[64,1536]{1,0:T(8,128)(2,1)} %bitcast.23), channel_id=1, source_target_pairs={{0,384},{8,136},{128,0},{136,264},{256,128},{264,392},{384,256},{3... | collective-permute-start | bytes 589832 | tf_op jit(solution)/shard_map/ppermute | solution.py:319
  4.6 0.9 copy-start.1
  6.5 13.8 %copy-start.3 = (bf16[2,32,1536]{2,1,0:T(8,128)(2,1)S(1)}, bf16[2,32,1536]{2,1,0:T(8,128)(2,1)}, u32[]{:S(2)}) copy-start(bf16[2,32,1536]{2,1,0:T(8,128)(2,1)} %param.7) | copy-start | bytes 589828
  6.5 34.2 %all-to-all-start = ((bf16[64,24,256]{2,1,0:T(8,128)(2,1)}), bf16[64,24,256]{2,1,0:T(8,128)(2,1)S(1)}, u32[]{:S(2)}, u32[]{:S(2)}) async-start(bf16[64,24,256]{2,1,0:T(8,128)(2,1)} %shard_map.87), calls=%async_computation | async-start | bytes 1572864 | tf_op jit(solution)/shard_map/all_to_all | solution.py:41
  20.3 14.7 %collective-permute-start.2 = (bf16[64,1536]{1,0:T(8,128)(2,1)S(1)}, bf16[64,1536]{1,0:T(8,128)(2,1)S(1)}, u32[]{:S(2)}, u32[]{:S(2)}) collective-permute-start(bf16[64,1536]{1,0:T(8,128)(2,1)S(1)} %bitcast.25), channel_id=1, source_target_pairs={{0,128},{8,392},{128,256},{136,8},{256,384},{264,136},{384,0},{392... | collective-permute-start | bytes 589832 | tf_op jit(solution)/shard_map/ppermute | solution.py:321
  22.5 12.5 %collective-permute-start.3 = (bf16[64,1536]{1,0:T(8,128)(2,1)S(1)}, bf16[64,1536]{1,0:T(8,128)(2,1)S(1)}, u32[]{:S(2)}, u32[]{:S(2)}) collective-permute-start(bf16[64,1536]{1,0:T(8,128)(2,1)S(1)} %collective-permute-done), channel_id=1, source_target_pairs={{0,384},{8,136},{128,0},{136,264},{256,128},{264,392},{384,256},{3... | collective-permute-start | bytes 589832 | tf_op jit(solution)/shard_map/ppermute | solution.py:323
  25.6 9.4 %collective-permute-start.1 = (bf16[128,1536]{1,0:T(8,128)(2,1)S(1)}, bf16[128,1536]{1,0:T(8,128)(2,1)S(1)}, u32[]{:S(2)}, u32[]{:S(2)}) collective-permute-start(bf16[128,1536]{1,0:T(8,128)(2,1)S(1)} %constant_dynamic-update-slice_fusion.near), channel_id=1, source_target_pairs={{0,8},{8,0},{1,9},{9,1},{2,10},{10,2},{3,11},{11,3},{4,12},{12,4},... | collective-permute-start | bytes 1179656 | tf_op jit(solution)/shard_map/ppermute | solution.py:324
  29.8 0.7 copy-start.5
  30.5 5.3 %copy-start = (bf16[2,256,1,256]{3,1,2,0:T(8,128)(2,1)S(1)}, bf16[2,256,1,256]{3,1,2,0:T(8,128)(2,1)}, u32[]{:S(2)}) copy-start(bf16[2,256,1,256]{3,1,2,0:T(8,128)(2,1)} %param.9) | copy-start | bytes 786436
  35.0 0.8 copy-start.2
  35.1 0.7 copy-start.4
  35.1 0.7 copy-start.6
  37.0 3.8 %collective-permute-start.4 = (bf16[128,1536]{1,0:T(8,128)(2,1)S(1)}, bf16[128,1536]{1,0:T(8,128)(2,1)S(1)}, u32[]{:S(2)}, u32[]{:S(2)}) collective-permute-start(bf16[128,1536]{1,0:T(8,128)(2,1)S(1)} %pad_maximum_fusion.far), channel_id=1, source_target_pairs={{0,8},{8,0},{1,9},{9,1},{2,10},{10,2},{3,11},{11,3},{4,12},{12,4},... | collective-permute-start | bytes 1179656 | tf_op jit(solution)/shard_map/ppermute | solution.py:332
  79.8 10.1 %all-to-all-start.3 = ((bf16[8,112,128]{2,1,0:T(8,128)(2,1)}), bf16[8,112,128]{2,1,0:T(8,128)(2,1)S(1)}, u32[]{:S(2)}, u32[]{:S(2)}) async-start(bf16[8,112,128]{2,1,0:T(8,128)(2,1)} %shard_map.90), calls=%async_computation.3 | async-start | bytes 458752 | tf_op jit(solution)/shard_map/all_to_all | solution.py:41
